TPU v7x, 32 devices: a whole 2x2x4 slice. The times are simulated.
32 devices in a mesh: dp: 8 (over z, core), fsdp: 4 (over y, x).
Axes of the slice: x: 2, y: 2, z: 4, core: 2. Of those that a mesh axis runs over, the one named last changes fastest.
Arguments:
- tokens: bfloat16 [32768, 1024], P(('dp', 'fsdp')), may hold values from -6 to 6
- seq_lengths: int32 [32, 4], P(('dp', 'fsdp')), may hold values from 0 to 1024, as said below
- expert_ids: int32 [32768, 1], P(('dp', 'fsdp')), may hold values from 0 to 1; in each aligned block of 1024 rows (0 to 1023, 1024 to 2047, ...) at most 768 rows name the same one
- grad_out: bfloat16 [32768, 1024], P(('dp', 'fsdp')), may hold values from -6 to 6
- ln1_gain: bfloat16 [1024], P(('dp', 'fsdp')), may hold values from 0.5 to 1.5
- ln1_bias: bfloat16 [1024], P(('dp', 'fsdp')), may hold values from -1.5 to 1.5
- w_qkv: bfloat16 [1024, 3072], P(('dp', 'fsdp')), may hold values from -0.1875 to 0.1875
- w_attn_out: bfloat16 [1024, 1024], P(('dp', 'fsdp')), may hold values from -0.75 to 0.75
- ln2_gain: bfloat16 [1024], P(('dp', 'fsdp')), may hold values from 0.5 to 1.5
- ln2_bias: bfloat16 [1024], P(('dp', 'fsdp')), may hold values from -1.5 to 1.5
- w_expert_in: bfloat16 [2, 1024, 4096], P(None, ('dp', 'fsdp')), may hold values from -0.1875 to 0.1875
- w_expert_out: bfloat16 [2, 4096, 1024], P(None, ('dp', 'fsdp')), may hold values from -0.09375 to 0.09375
Outputs:
- block_out: bfloat16 [32768, 1024], P(('dp', 'fsdp'))
- grad_tokens: float32 [32768, 1024], P(('dp', 'fsdp'))
- grad_ln1_gain: float32 [1024], P(('dp', 'fsdp'))
- grad_ln1_bias: float32 [1024], P(('dp', 'fsdp'))
- grad_w_qkv: float32 [1024, 3072], P(('dp', 'fsdp'))
- grad_w_attn_out: float32 [1024, 1024], P(('dp', 'fsdp'))
- grad_ln2_gain: float32 [1024], P(('dp', 'fsdp'))
- grad_ln2_bias: float32 [1024], P(('dp', 'fsdp'))
- grad_w_expert_in: float32 [2, 1024, 4096], P(None, ('dp', 'fsdp'))
- grad_w_expert_out: float32 [2, 4096, 1024], P(None, ('dp', 'fsdp'))
Inputs may be any that keep to these rules, and one draw needn't show every extreme that they name: `seq_lengths`: each row is either one sequence of 1024 tokens followed by zeros, or 4 lengths of at least 128 that sum to 1024; some row is a single sequence in every draw. `expert_ids`: at most 768 of one device's 1024 tokens name the same expert, and that many do on some device.
All inputs are finite; a program needn't handle non-finite values.
Results may differ from a plain program's by a relative error of at most 0.012.
Values may be sent and summed in bfloat16 or wider, within the bound.
A program may use at most 320 MiB of HBM per device.

v0:
```python
import jax
import jax.numpy as jnp
from jax import lax
from jax.sharding import PartitionSpec as P

HEADS = 16
HEAD_DIM = 64
EXPERTS = 2
CAPACITY = 768


EPSILON = 1e-05
MASKED = -1000000000.0


def norm_parts(values, gain, shift):
    average = jnp.mean(values, axis=-1, keepdims=True)
    centred = values - average
    variance = jnp.mean(centred * centred, axis=-1, keepdims=True)
    inverse = lax.rsqrt(variance + EPSILON)
    scaled = centred * inverse
    return (scaled * gain + shift, scaled, inverse)


def norm_back(grad_normed, scaled, inverse, gain):
    grad_scaled = grad_normed * gain
    middle = jnp.mean(grad_scaled, axis=-1, keepdims=True)
    along = jnp.mean(grad_scaled * scaled, axis=-1, keepdims=True)
    return inverse * (grad_scaled - middle - scaled * along)


def segment_ids(lengths_row, row_count):
    bounds = jnp.cumsum(lengths_row)
    positions = jnp.arange(row_count, dtype=jnp.int32)
    return jnp.sum((positions[:, None] >= bounds[None, :]).astype(jnp.int32), axis=1)


def block_scores(first_row, block_rows, queries, keys_all, segment, score_scale):
    query_blk = lax.dynamic_slice_in_dim(queries, first_row, block_rows, 0)
    raw_scores = (
        jnp.einsum("qhd,khd->hqk", query_blk, keys_all, preferred_element_type=jnp.float32)
        * score_scale
    )
    positions = jnp.arange(keys_all.shape[0], dtype=jnp.int32)
    query_pos = first_row + jnp.arange(block_rows, dtype=jnp.int32)
    query_seg = lax.dynamic_slice_in_dim(segment, first_row, block_rows, 0)
    allowed = (query_seg[:, None] == segment[None, :]) & (positions[None, :] <= query_pos[:, None])
    return (query_blk, jnp.where(allowed[None], raw_scores, MASKED))


def local(
    tokens,
    seq_lengths,
    expert_ids,
    grad_out,
    ln1_gain,
    ln1_bias,
    w_qkv,
    w_attn_out,
    ln2_gain,
    ln2_bias,
    w_expert_in,
    w_expert_out,
):
    block_params = (
        lax.all_gather(ln1_gain, ("dp", "fsdp"), axis=0, tiled=True),
        lax.all_gather(ln1_bias, ("dp", "fsdp"), axis=0, tiled=True),
        lax.all_gather(w_qkv, ("dp", "fsdp"), axis=0, tiled=True),
        lax.all_gather(w_attn_out, ("dp", "fsdp"), axis=0, tiled=True),
        lax.all_gather(ln2_gain, ("dp", "fsdp"), axis=0, tiled=True),
        lax.all_gather(ln2_bias, ("dp", "fsdp"), axis=0, tiled=True),
    )
    expert_params = (
        lax.all_gather(w_expert_in, ("dp", "fsdp"), axis=1, tiled=True),
        lax.all_gather(w_expert_out, ("dp", "fsdp"), axis=1, tiled=True),
    )
    row_count = tokens.shape[0]
    model_width = tokens.shape[1]
    score_scale = HEAD_DIM ** (-0.5)
    block_rows = min(512, row_count)
    starts = jnp.arange(row_count // block_rows, dtype=jnp.int32) * block_rows
    segment = segment_ids(seq_lengths[0], row_count)
    tokens_wide = tokens.astype(jnp.float32)
    normed_one, scaled_one, inverse_one = norm_parts(
        tokens_wide, block_params[0].astype(jnp.float32), block_params[1].astype(jnp.float32)
    )
    normed_one_low = normed_one.astype(jnp.bfloat16)
    projected = jnp.dot(normed_one_low, block_params[2], preferred_element_type=jnp.float32).astype(
        jnp.bfloat16
    )
    queries = projected[:, :model_width].reshape(row_count, HEADS, HEAD_DIM)
    keys_all = projected[:, model_width : 2 * model_width].reshape(row_count, HEADS, HEAD_DIM)
    values_all = projected[:, 2 * model_width :].reshape(row_count, HEADS, HEAD_DIM)

    def forward_block(first_row):
        query_blk, scores = block_scores(
            first_row, block_rows, queries, keys_all, segment, score_scale
        )
        highest = jnp.max(scores, axis=-1, keepdims=True)
        exp_terms = jnp.exp(scores - highest)
        totals = jnp.sum(exp_terms, axis=-1, keepdims=True)
        attend_low = (exp_terms / totals).astype(jnp.bfloat16)
        mixed_blk = jnp.einsum(
            "hqk,khd->qhd", attend_low, values_all, preferred_element_type=jnp.float32
        ).astype(jnp.bfloat16)
        return (mixed_blk, (highest + jnp.log(totals))[..., 0])

    mixed_blocks, log_totals = lax.map(forward_block, starts)
    mixed_low = mixed_blocks.reshape(row_count, model_width)
    hidden_one = tokens_wide + jnp.dot(
        mixed_low, block_params[3], preferred_element_type=jnp.float32
    )
    normed_two, scaled_two, inverse_two = norm_parts(
        hidden_one, block_params[4].astype(jnp.float32), block_params[5].astype(jnp.float32)
    )
    normed_two_low = normed_two.astype(jnp.bfloat16)
    routed = expert_ids[:, 0]
    member = routed[:, None] == jnp.arange(EXPERTS, dtype=jnp.int32)[None, :]
    running = jnp.cumsum(member.astype(jnp.int32), axis=0) - 1
    within = jnp.sum(jnp.where(member, running, 0), axis=1)
    slot_of = routed * CAPACITY + within
    slot_token = (
        jnp.zeros((EXPERTS * CAPACITY,), jnp.int32)
        .at[slot_of]
        .set(jnp.arange(row_count, dtype=jnp.int32))
    )
    filled = jnp.zeros((EXPERTS * CAPACITY,), jnp.bool_).at[slot_of].set(True)
    zero_low = jnp.zeros((), jnp.bfloat16)
    expert_rows = jnp.where(filled[:, None], normed_two_low[slot_token], zero_low).reshape(
        EXPERTS, CAPACITY, model_width
    )
    inner_sums = jnp.einsum(
        "ecd,edf->ecf", expert_rows, expert_params[0], preferred_element_type=jnp.float32
    )
    active_low = jax.nn.gelu(inner_sums).astype(jnp.bfloat16)
    branch = jnp.einsum(
        "ecf,efd->ecd", active_low, expert_params[1], preferred_element_type=jnp.float32
    ).reshape(EXPERTS * CAPACITY, model_width)
    block_out = (hidden_one + branch[slot_of]).astype(jnp.bfloat16)
    back_params = (
        lax.all_gather(ln1_gain, ("dp", "fsdp"), axis=0, tiled=True),
        lax.all_gather(ln1_bias, ("dp", "fsdp"), axis=0, tiled=True),
        lax.all_gather(w_qkv, ("dp", "fsdp"), axis=0, tiled=True),
        lax.all_gather(w_attn_out, ("dp", "fsdp"), axis=0, tiled=True),
        lax.all_gather(ln2_gain, ("dp", "fsdp"), axis=0, tiled=True),
        lax.all_gather(ln2_bias, ("dp", "fsdp"), axis=0, tiled=True),
    )
    back_experts = (
        lax.all_gather(w_expert_in, ("dp", "fsdp"), axis=1, tiled=True),
        lax.all_gather(w_expert_out, ("dp", "fsdp"), axis=1, tiled=True),
    )
    grad_wide = grad_out.astype(jnp.float32)
    grad_slots = jnp.where(filled[:, None], grad_out[slot_token], zero_low).reshape(
        EXPERTS, CAPACITY, model_width
    )
    grad_out_weight = jnp.einsum(
        "ecf,ecd->efd", active_low, grad_slots, preferred_element_type=jnp.float32
    )
    grad_active = jnp.einsum(
        "ecd,efd->ecf", grad_slots, back_experts[1], preferred_element_type=jnp.float32
    )
    gelu_value, gelu_back = jax.vjp(jax.nn.gelu, inner_sums)
    grad_inner_low = gelu_back(grad_active)[0].astype(jnp.bfloat16)
    grad_in_weight = jnp.einsum(
        "ecd,ecf->edf", expert_rows, grad_inner_low, preferred_element_type=jnp.float32
    )
    grad_rows = jnp.einsum(
        "ecf,edf->ecd", grad_inner_low, back_experts[0], preferred_element_type=jnp.float32
    ).reshape(EXPERTS * CAPACITY, model_width)
    grad_normed_two = grad_rows[slot_of]
    grad_gain_two = jnp.sum(grad_normed_two * scaled_two, axis=0)
    grad_bias_two = jnp.sum(grad_normed_two, axis=0)
    grad_hidden = grad_wide + norm_back(
        grad_normed_two, scaled_two, inverse_two, back_params[4].astype(jnp.float32)
    )
    grad_branch_low = grad_hidden.astype(jnp.bfloat16)
    grad_attn_weight = jnp.einsum(
        "td,te->de", mixed_low, grad_branch_low, preferred_element_type=jnp.float32
    )
    grad_mixed_low = jnp.einsum(
        "te,de->td", grad_branch_low, back_params[3], preferred_element_type=jnp.float32
    ).astype(jnp.bfloat16)
    grad_mixed_heads = grad_mixed_low.reshape(row_count, HEADS, HEAD_DIM)

    def backward_block(carry, inputs):
        grad_keys, grad_values = carry
        first_row, log_total = inputs
        query_blk, scores = block_scores(
            first_row, block_rows, queries, keys_all, segment, score_scale
        )
        attend = jnp.exp(scores - log_total[..., None])
        attend_low = attend.astype(jnp.bfloat16)
        grad_blk = lax.dynamic_slice_in_dim(grad_mixed_heads, first_row, block_rows, 0)
        grad_attend = jnp.einsum(
            "qhd,khd->hqk", grad_blk, values_all, preferred_element_type=jnp.float32
        )
        row_inner = jnp.sum(attend * grad_attend, axis=-1, keepdims=True)
        grad_scores = (attend * (grad_attend - row_inner)).astype(jnp.bfloat16)
        grad_query = (
            jnp.einsum("hqk,khd->qhd", grad_scores, keys_all, preferred_element_type=jnp.float32)
            * score_scale
        )
        grad_keys = (
            grad_keys
            + jnp.einsum("hqk,qhd->khd", grad_scores, query_blk, preferred_element_type=jnp.float32)
            * score_scale
        )
        grad_values = grad_values + jnp.einsum(
            "hqk,qhd->khd", attend_low, grad_blk, preferred_element_type=jnp.float32
        )
        return ((grad_keys, grad_values), grad_query)

    zero_heads = jnp.zeros((row_count, HEADS, HEAD_DIM), jnp.float32)
    (grad_keys_all, grad_values_all), grad_query_blocks = lax.scan(
        backward_block, (zero_heads, zero_heads), (starts, log_totals)
    )
    grad_projected_low = jnp.concatenate(
        [
            grad_query_blocks.reshape(row_count, model_width),
            grad_keys_all.reshape(row_count, model_width),
            grad_values_all.reshape(row_count, model_width),
        ],
        axis=1,
    ).astype(jnp.bfloat16)
    grad_qkv_weight = jnp.einsum(
        "td,te->de", normed_one_low, grad_projected_low, preferred_element_type=jnp.float32
    )
    grad_normed_one = jnp.einsum(
        "te,de->td", grad_projected_low, back_params[2], preferred_element_type=jnp.float32
    )
    grad_gain_one = jnp.sum(grad_normed_one * scaled_one, axis=0)
    grad_bias_one = jnp.sum(grad_normed_one, axis=0)
    grad_input = grad_hidden + norm_back(
        grad_normed_one, scaled_one, inverse_one, back_params[0].astype(jnp.float32)
    )
    block_shares = (
        lax.psum_scatter(grad_gain_one, ("dp", "fsdp"), scatter_dimension=0, tiled=True),
        lax.psum_scatter(grad_bias_one, ("dp", "fsdp"), scatter_dimension=0, tiled=True),
        lax.psum_scatter(grad_qkv_weight, ("dp", "fsdp"), scatter_dimension=0, tiled=True),
        lax.psum_scatter(grad_attn_weight, ("dp", "fsdp"), scatter_dimension=0, tiled=True),
        lax.psum_scatter(grad_gain_two, ("dp", "fsdp"), scatter_dimension=0, tiled=True),
        lax.psum_scatter(grad_bias_two, ("dp", "fsdp"), scatter_dimension=0, tiled=True),
    )
    expert_shares = (
        lax.psum_scatter(grad_in_weight, ("dp", "fsdp"), scatter_dimension=1, tiled=True),
        lax.psum_scatter(grad_out_weight, ("dp", "fsdp"), scatter_dimension=1, tiled=True),
    )
    return (
        block_out,
        grad_input,
        block_shares[0],
        block_shares[1],
        block_shares[2],
        block_shares[3],
        block_shares[4],
        block_shares[5],
        expert_shares[0],
        expert_shares[1],
    )


def solution(mesh):
    return jax.shard_map(
        local,
        mesh=mesh,
        in_specs=(
            P(("dp", "fsdp"), None),
            P(("dp", "fsdp"), None),
            P(("dp", "fsdp"), None),
            P(("dp", "fsdp"), None),
            P(("dp", "fsdp")),
            P(("dp", "fsdp")),
            P(("dp", "fsdp"), None),
            P(("dp", "fsdp"), None),
            P(("dp", "fsdp")),
            P(("dp", "fsdp")),
            P(None, ("dp", "fsdp"), None),
            P(None, ("dp", "fsdp"), None),
        ),
        out_specs=(
            P(("dp", "fsdp"), None),
            P(("dp", "fsdp"), None),
            P(("dp", "fsdp")),
            P(("dp", "fsdp")),
            P(("dp", "fsdp"), None),
            P(("dp", "fsdp"), None),
            P(("dp", "fsdp")),
            P(("dp", "fsdp")),
            P(None, ("dp", "fsdp"), None),
            P(None, ("dp", "fsdp"), None),
        ),
        check_vma=False,
    )
```

profile of v0, /device:TPU:0, one launch (start us, length us, event | category | flops | bytes accessed | tf_op | source)
XLA Modules:
  0.0 2335.8 jit_solution(396611236911212222)
XLA Ops:
  14.3 42.2 %all-reduce.9 = (bf16[1024]{0:T(1024)(128)(2,1)S(1)}, bf16[1024]{0:T(1024)(128)(2,1)S(1)}, bf16[1024]{0:T(1024)(128)(2,1)S(1)}, bf16[1024]{0:T(1024)(128)(2,1)S(1)}) all-reduce(bf16[1024]{0:T(1024)(128)(2,1)S(1)} %dynamic-update-slice.1, bf16[1024]{0:T(1024)(128)(2,1)S(1)} %dynamic-update-slice, ...), channel_id=1, replica_groups=mesh['dp'=8,'fsdp'=4] {'dp','fsdp'}, use_global_device_ids=true, to_apply=%add.1 | all-reduce | flops 4096 | bytes 16384
  77.2 5.9 gather_fusion.2
  88.1 10.3 convolution_convert_fusion
  111.8 106.5 %while.27 = (s32[]{:T(128)}, bf16[2,512,16,64]{1,3,2,0:T(8,128)(2,1)}, f32[2,16,512]{2,1,0:T(8,128)S(1)}, s32[2]{0:T(128)S(1)}, s32[1024]{0:T(1024)S(1)}, /*inde...) while((s32[]{:T(128)}, ...), condition=%wide.region_7.8_spmd, body=%wide.region_4.7_spmd.sunk | while | flops 2250236416 | bytes 126105840 | solution.py:108
  115.9 16.7 fusion.123
  132.5 15.1 fusion.124
  147.7 15.5 fusion.125
  168.4 16.5 fusion.123
  184.9 15.2 fusion.124
  200.0 16.8 fusion.125
  236.4 5.8 gather_fusion
  242.2 15.5 all-gather.9.cloned.1.call-done
  257.8 22.9 fusion.53
  280.6 92.9 %all-gather.11.cloned.1.call-done = bf16[2,4096,1024]{2,1,0:T(8,128)(2,1)} async-done(((bf16[2,128,1024]{2,1,0:T(8,128)(2,1)}), bf16[2,4096,1024]{2,1,0:T(8,128)(2,1)}) %all-gather.11.cloned.1.call-update) | async-done | bytes 16777232 | tf_op jit(solution)/shard_map/all_gather | solution.py:75
  373.6 32.5 %fusion.37 = bf16[2,768,4096]{2,1,0:T(8,128)(2,1)} fusion(f32[2,768,4096]{2,1,0:T(8,128)} %fusion.53, bf16[2,4096,1024]{2,1,0:T(8,128)(2,1)} %all-gather.11.cloned.1.call-done, bf16[2,768,1024]{2,1,0:T(8,128)(2,1)S(1)} %bitcast.113, pred[2,768]{1,0:T(4,128)(4,1)S(1)} %copy-done.42), kind=kOutput, calls=%fused_computation.57 | convolution fusion | flops 13012303872 | bytes 57673216 | tf_op jit(solution)/shard_map/ecd,efd->ecf/dot_general | solution.py:159
  406.1 20.6 fusion.83
  426.6 9.1 gather_fusion.3
  435.7 23.8 %fusion.79 = f32[2,768,1024]{2,1,0:T(8,128)} fusion(bf16[2,4096,1024]{2,1,0:T(8,128)(2,1)} %all-gather.11.cloned.1.call-done, f32[2,768,4096]{2,1,0:T(8,128)} %fusion.53), kind=kOutput, calls=%fused_computation.135 | convolution fusion | flops 12941524992 | bytes 48234496 | tf_op jit(solution)/shard_map/ecf,efd->ecd/dot_general | solution.py:136
  459.5 9.6 gather_fusion.1
  469.1 5.4 copy.80
  474.5 5.5 copy.82
  480.1 5.4 multiply_reduce_fusion.1
  486.0 5.2 multiply_add_fusion
  499.2 5.8 convolution_convert_fusion.1
  505.0 226.6 %while.28 = (s32[]{:T(128)}, f32[1024,16,64]{0,2,1:T(8,128)}, f32[1024,16,64]{0,2,1:T(8,128)}, bf16[2,512,16,64]{1,3,2,0:T(8,128)(2,1)}, s32[2]{0:T(128)S(1)}, /...) while((s32[]{:T(128)}, f32[1024,16,64]{0,2,1:T(8,128)}, ...), condition=%wide.region_19.20_spmd.clone, body=%wide.region_17.19_spmd.clone.sunk | while | flops 5501870592 | bytes 350468352 | solution.py:214
  509.1 17.9 fusion.135
  527.0 18.0 bitcast_add_fusion.5
  545.0 26.0 %multiply_reduce_fusion.7 = (f32[16,512]{1,0:T(8,128)S(1)}, f32[16,512,1024]{2,1,0:T(8,128)}) fusion(f32[16,512,1024]{2,1,0:T(8,128)} %fusion.135, f32[16,512]{1,0:T(8,128)S(1)} %dynamic-slice_bitcast_fusion.2, pred[512,1024]{1,0:T(8,128)(4,1)S(1)} %fusion.136, bf16[1024,16,64]{0,2,1:T(8,128)(2,1)} %get-tuple-element.474, ...), kind=kOutput, calls=%fused_computation.25.clone.1 | convolution fusion | flops 1115676672 | bytes 70844416 | tf_op jit(solution)/shard_map/while/body/eval_jaxpr/qhd,khd->hqk/dot_general | solution.py:194
  571.0 28.1 %multiply_convert_fusion.5 = bf16[16,512,1024]{2,1,0:T(8,128)(2,1)} fusion(f32[16,512,1024]{2,1,0:T(8,128)} %get-tuple-element.401, f32[16,512,1024]{2,1,0:T(8,128)} %fusion.135, f32[16,512]{1,0:T(8,128)S(1)} %get-tuple-element.402, f32[16,512]{1,0:T(8,128)S(1)} %dynamic-slice_bitcast_fusion.2, pred[512,1024]{1,0:T(8,128)(4,1)S(1)} %fusion.136), kind=kLoop, calls=%fused_computation.24.clone.1 | loop fusion | flops 50331648 | bytes 84475904 | tf_op jit(solution)/shard_map/while/body/eval_jaxpr/convert_element_type | solution.py:198
  599.1 10.3 bitcast_dynamic-update-slice_fusion.5
  610.7 6.7 bitcast_add_fusion.4
  621.3 17.8 fusion.135
  639.1 19.0 bitcast_add_fusion.5
  658.1 26.0 %multiply_reduce_fusion.7 = (f32[16,512]{1,0:T(8,128)S(1)}, f32[16,512,1024]{2,1,0:T(8,128)}) fusion(f32[16,512,1024]{2,1,0:T(8,128)} %fusion.135, f32[16,512]{1,0:T(8,128)S(1)} %dynamic-slice_bitcast_fusion.2, pred[512,1024]{1,0:T(8,128)(4,1)S(1)} %fusion.136, bf16[1024,16,64]{0,2,1:T(8,128)(2,1)} %get-tuple-element.474, ...), kind=kOutput, calls=%fused_computation.25.clone.1 | convolution fusion | flops 1115676672 | bytes 70844416 | tf_op jit(solution)/shard_map/while/body/eval_jaxpr/qhd,khd->hqk/dot_general | solution.py:194
  684.0 27.8 %multiply_convert_fusion.5 = bf16[16,512,1024]{2,1,0:T(8,128)(2,1)} fusion(f32[16,512,1024]{2,1,0:T(8,128)} %get-tuple-element.401, f32[16,512,1024]{2,1,0:T(8,128)} %fusion.135, f32[16,512]{1,0:T(8,128)S(1)} %get-tuple-element.402, f32[16,512]{1,0:T(8,128)S(1)} %dynamic-slice_bitcast_fusion.2, pred[512,1024]{1,0:T(8,128)(4,1)S(1)} %fusion.136), kind=kLoop, calls=%fused_computation.24.clone.1 | loop fusion | flops 50331648 | bytes 84475904 | tf_op jit(solution)/shard_map/while/body/eval_jaxpr/convert_element_type | solution.py:198
  711.8 10.3 bitcast_dynamic-update-slice_fusion.5
  723.3 7.9 bitcast_add_fusion.4
  741.4 11.4 fusion.56
  753.5 29.5 %fusion.54 = f32[2,4096,1024]{2,1,0:T(8,128)} fusion(bf16[2,768,1024]{2,1,0:T(8,128)(2,1)} %bitcast.112, pred[2,768]{1,0:T(4,128)(4,1)S(1)} %copy-done.43, f32[2,768,4096]{2,1,0:T(8,128)} %fusion.53), kind=kOutput, calls=%fused_computation.91 | convolution fusion | flops 12943097856 | bytes 61867520 | tf_op jit(solution)/shard_map/ecf,ecd->efd/dot_general | solution.py:156
  783.0 26.4 %fusion.52 = f32[2,1024,4096]{2,1,0:T(8,128)} fusion(bf16[2,768,4096]{2,1,0:T(8,128)(2,1)} %fusion.37, bf16[2,768,1024]{2,1,0:T(8,128)(2,1)} %bitcast.115, pred[2,768]{1,0:T(4,128)(4,1)S(1)} %copy-done.43), kind=kOutput, calls=%fused_computation.89 | convolution fusion | flops 12886474752 | bytes 49284608 | tf_op jit(solution)/shard_map/ecd,ecf->edf/dot_general | solution.py:164
  815.9 12.1 fusion.82
  828.0 5.5 copy.84
  837.0 39.3 %all-reduce.8 = (f32[1024]{0:T(1024)S(1)}, f32[1024]{0:T(1024)S(1)}, f32[1024]{0:T(1024)S(1)}, f32[1024]{0:T(1024)S(1)}) all-reduce(f32[1024]{0:T(1024)S(1)} %get-tuple-element.214, f32[1024]{0:T(1024)S(1)} %get-tuple-element.275, f32[1024]{0:T(1024)S(1)} %copy-done.38, ...), channel_id=2, replica_groups=mesh['dp'=8,'fsdp'=4] {'dp','fsdp'}, use_global_device_ids=true, to_apply=%region_23.24.clone | all-reduce | flops 4096 | bytes 32768
  878.7 7.0 fusion.49
  885.7 5.4 copy.90
  891.1 16.8 reduce-scatter.5.cloned.1.call-done
  907.8 709.8 %reduce-scatter.11.cloned.1.call-done = f32[2,128,1024]{2,1,0:T(8,128)} async-done(((f32[2,4096,1024]{2,1,0:T(8,128)}), f32[2,128,1024]{2,1,0:T(8,128)}) %reduce-scatter.11.cloned.1.call-update) | async-done | bytes 1048592 | tf_op jit(solution)/shard_map/reduce_scatter | solution.py:246
  1617.7 711.0 %reduce-scatter.9.cloned.1.call-done = f32[2,32,4096]{2,1,0:T(8,128)} async-done(((f32[2,1024,4096]{2,1,0:T(8,128)}), f32[2,32,4096]{2,1,0:T(8,128)}) %reduce-scatter.9.cloned.1.call-update) | async-done | bytes 1048592 | tf_op jit(solution)/shard_map/reduce_scatter | solution.py:245
  (207 shorter events, 108.0 us)
Async XLA Ops:
  7.2 67.4 %copy-start.1 = (bf16[1024,1024]{1,0:T(8,128)(2,1)S(1)}, bf16[1024,1024]{1,0:T(8,128)(2,1)}, u32[]{:S(2)}) copy-start(bf16[1024,1024]{1,0:T(8,128)(2,1)} %param.19) | copy-start | bytes 6291460
  7.2 80.9 %all-gather.5.cloned.1.call-start = ((), (), s32[]{:S(2)}) async-start(), calls=%async_computation.4 | async-start | bytes 6488064 | tf_op jit(solution)/shard_map/all_gather | solution.py:68
  7.9 216.3 %all-gather.7.cloned.1.call-start = ((), (), s32[]{:S(2)}) async-start(), calls=%async_computation.5 | async-start | bytes 2162688 | tf_op jit(solution)/shard_map/all_gather | solution.py:69
  8.7 249.1 %all-gather.9.cloned.1.call-start = ((), (), s32[]{:S(2)}) async-start(), calls=%async_computation.6 | async-start | bytes 17301504 | tf_op jit(solution)/shard_map/all_gather | solution.py:74
  9.4 364.1 %all-gather.11.cloned.1.call-start = ((), (), s32[]{:S(2)}) async-start(), calls=%async_computation.7 | async-start | bytes 17301504 | tf_op jit(solution)/shard_map/all_gather | solution.py:75
  10.0 881.1 %reduce-scatter.7.cloned.1.call-start = ((), (), s32[]{:S(2)}) async-start(), calls=%async_computation.9 | async-start | bytes 4325376 | tf_op jit(solution)/shard_map/reduce_scatter | solution.py:240
  56.5 31.6 %copy-start.40 = (f32[1024]{0:T(1024)}, f32[1024]{0:T(1024)S(1)}, u32[]{:S(2)}) copy-start(f32[1024]{0:T(1024)S(1)} %convert_element_type.71) | copy-start | bytes 12292
  56.5 31.6 %copy-start.33 = (f32[1024]{0:T(1024)}, f32[1024]{0:T(1024)S(1)}, u32[]{:S(2)}) copy-start(f32[1024]{0:T(1024)S(1)} %convert_element_type.70) | copy-start | bytes 12292
  77.1 5.9 copy-start.25
  83.0 5.0 copy-start.5
  85.8 12.6 copy-start.31
  88.0 10.4 copy-start.35
  132.5 15.2 copy-start.15
  184.9 15.2 copy-start.15
  218.3 5.8 copy-start.19
  218.3 5.8 copy-start.21
  218.4 5.8 copy-start.45
  218.4 5.8 copy-start.6
  228.9 2.7 copy-start.27
  231.6 4.8 copy-start.26
  236.4 21.3 copy-start.42
  257.8 115.8 %copy-start.12 = (bf16[1536,1024]{1,0:T(8,128)(2,1)S(1)}, bf16[1536,1024]{1,0:T(8,128)(2,1)}, u32[]{:S(2)}) copy-start(bf16[1536,1024]{1,0:T(8,128)(2,1)} %gather_fusion.2) | copy-start | bytes 9437188
  406.1 20.6 copy-start.37
  474.5 5.5 copy-start.24
  474.5 5.5 copy-start.28
  474.5 5.5 copy-start.30
  474.5 10.9 copy-start.10
  480.0 5.4 copy-start.4
  480.0 5.9 copy-start.8
  486.0 7.2 copy-start.17
  497.6 7.4 copy-start.20
  497.6 7.4 copy-start.22
  497.6 7.4 copy-start.46
  497.6 410.2 %reduce-scatter.5.cloned.1.call-start = ((), (), s32[]{:S(2)}) async-start(), calls=%async_computation.8 | async-start | bytes 12976128 | tf_op jit(solution)/shard_map/reduce_scatter | solution.py:239
  599.1 11.6 copy-start
  711.8 11.5 copy-start
  731.6 4.5 copy-start.2
  736.1 4.1 copy-start.18
  736.1 3.7 copy-start.11
  736.4 3.7 copy-start.13
  736.4 5.0 copy-start.7
  736.4 5.0 copy-start.32
  736.5 5.0 copy-start.34
  736.5 4.9 copy-start.36
  736.5 4.9 copy-start.41
  752.8 864.8 %reduce-scatter.11.cloned.1.call-start = ((), (), s32[]{:S(2)}) async-start(), calls=%async_computation.11 | async-start | bytes 34603008 | tf_op jit(solution)/shard_map/reduce_scatter | solution.py:246
  783.0 1545.7 %reduce-scatter.9.cloned.1.call-start = ((), (), s32[]{:S(2)}) async-start(), calls=%async_computation.10 | async-start | bytes 34603008 | tf_op jit(solution)/shard_map/reduce_scatter | solution.py:245
  833.4 3.6 copy-start.38
  (10 other events, 15.6 us)
Sparse Core Ops, SparseCore 0:
  10.9 72.3 all-gather.4
  86.2 54.9 all-gather.6
  144.1 113.6 all-gather.8
  260.6 112.9 all-gather.10
  497.7 139.6 reduce-scatter.6
  753.0 154.8 reduce-scatter.4
  910.8 706.8 reduce-scatter.10
  1620.7 707.9 reduce-scatter.8
where the time goes:
time: 2340 us
  waiting for transfers between devices  1550 us (66%)
  matrix products  430 us (18%)
  other arithmetic  128 us (5%)
  local copies, waits for them, and re-layouts  124 us (5%)
  blocking collectives  81.5 us (3%)
    reduce_scatter x1, waiting for transfers between devices, local(): lax.psum_scatter(grad_in_weight, ('dp', 'fsdp'), scatter_dimension=1, til...  711 us
    reduce_scatter x1, waiting for transfers between devices, local(): lax.psum_scatter(grad_out_weight, ('dp', 'fsdp'), scatter_dimension=1, ti...  710 us
    all_gather x1, waiting for transfers between devices, local(): lax.all_gather(w_expert_out, ('dp', 'fsdp'), axis=1, tiled=True)  92.9 us
    unnamed x2, blocking collectives  81.5 us
    dot_general x4, matrix products, block_scores(): jnp.einsum('qhd,khd->hqk', query_blk, keys_all, preferred_element_type=jn...  68.9 us
    convert_element_type x2, other arithmetic, backward_block(): grad_scores = (attend * (grad_attend - row_inner)).astype(jnp.bfloat16)  55.9 us
    dot_general x2, matrix products, backward_block(): jnp.einsum('qhd,khd->hqk', grad_blk, values_all, preferred_element_type=j...  52 us
  transfers between devices with their start and end apart: 8, of which 5 were waited for; matrix products, arithmetic and copies ran while one was open for 23% of the time, Pallas kernels for 0%

commit v1 on v0

v1 whole, which is shorter than its diff:
```python
import functools

import jax
import jax.numpy as jnp
from jax import lax
from jax.experimental import pallas as pl
from jax.experimental.pallas import tpu as pltpu
from jax.sharding import PartitionSpec as P

HEADS = 16
HEAD_DIM = 64
EXPERTS = 2
EPSILON = 1e-05
MASKED = -1000000000.0
AXES = ("dp", "fsdp")
BLOCK = 128
TILE = 256
MIB = 1024 * 1024
F32 = jnp.float32
BF16 = jnp.bfloat16
NT = (((1,), (1,)), ((), ()))
TN = (((0,), (0,)), ((), ()))
ROOT_2_PI = 0.7978845608028654
CUBIC = 0.044715


def dot(a, b):
    return jnp.dot(a, b, preferred_element_type=F32)


def dot_nt(a, b):
    return lax.dot_general(a, b, NT, preferred_element_type=F32)


def dot_tn(a, b):
    return lax.dot_general(a, b, TN, preferred_element_type=F32)


def norm_parts(values):
    average = jnp.mean(values, axis=-1, keepdims=True)
    centred = values - average
    variance = jnp.mean(centred * centred, axis=-1, keepdims=True)
    inverse = lax.rsqrt(variance + EPSILON)
    return (centred * inverse, inverse)


def norm_back(grad_normed, scaled, inverse, gain):
    grad_scaled = grad_normed * gain
    middle = jnp.mean(grad_scaled, axis=-1, keepdims=True)
    along = jnp.mean(grad_scaled * scaled, axis=-1, keepdims=True)
    return inverse * (grad_scaled - middle - scaled * along)


class Moves:
    def __init__(self, nd, nf):
        self.nz, self.nf = nd // 2, nf
        bits = []
        bit = 1
        while bit < nf:
            bits.append(bit)
            bit *= 2
        self.orders = (tuple(bits), tuple(reversed(bits)))

    def send(self, value, where):
        pairs = []
        for zed in range(self.nz):
            for core in range(2):
                for flat in range(self.nf):
                    z_to, core_to, f_to = where(zed, core, flat)
                    pairs.append(
                        (
                            (zed * 2 + core) * self.nf + flat,
                            (z_to * 2 + core_to) * self.nf + f_to,
                        )
                    )
        return lax.ppermute(value, AXES, pairs)

    def core(self, value):
        return self.send(value, lambda z, c, f: (z, 1 - c, f))

    def flat(self, value, bit):
        return self.send(value, lambda z, c, f: (z, c, f ^ bit))

    def along(self, value, steps):
        return self.send(value, lambda z, c, f: ((z + steps) % self.nz, c, f))

    def near(self, value, bit):
        return self.send(value, lambda z, c, f: (z ^ bit, c, f))

    def relative(self, stream):
        offsets = [0]
        for bit in reversed(self.orders[stream]):
            offsets = offsets + [one ^ bit for one in offsets]
        return tuple(offsets)

    def gather_z(self, value):
        return [value] + [self.along(value, k) for k in range(1, self.nz)]

    def gather_z_pair(self, value):
        held, bit = value[:, None], 1
        while 2 * bit < self.nz:
            held = jnp.concatenate([held, self.near(held, bit)], axis=1)
            bit *= 2
        got = self.near(held, bit)
        return [jnp.concatenate([held[n], got[n]], axis=0) for n in range(2)], got

    def gather_first(self, value, stream):
        held = value[None]
        for bit in tuple(reversed(self.orders[stream]))[:-1]:
            held = jnp.concatenate([held, self.flat(held, bit)], axis=0)
        return held

    def gather_last(self, held, stream):
        return self.flat(held, self.orders[stream][0])

    def reduce_flat(self, keep, sent, stream):
        order = self.orders[stream]
        now = add_low(keep, self.flat(sent, order[0]))
        for bit in order[1:]:
            half = now.shape[0] // 2
            now = add_low(now[:half], self.flat(now[half:], bit))
        return now[0]

    def reduce_z(self, value):
        total = value[0].astype(F32)
        for k in range(1, self.nz):
            total = total + self.along(value[k], k).astype(F32)
        return total

    def reduce_z_pair(self, value):
        bit = self.nz // 2
        while bit > 1:
            value = add_low(value[:bit], self.near(value[bit:], bit))
            bit //= 2
        return value[0].astype(F32) + self.near(value[1], 1).astype(F32)


def after(value, *others):
    return lax.optimization_barrier((value,) + others)[0]


def add_low(a, b):
    return (a.astype(F32) + b.astype(F32)).astype(BF16)


def attention_forward_kernel(seg_row, seg_col, q, k, v, out, stats, bias):
    rows = q.shape[0]
    pair = pl.program_id(0)
    lane = lax.broadcasted_iota(jnp.int32, (1, BLOCK), 1)

    @pl.when(pair == 0)
    def _():
        stats[...] = jnp.zeros_like(stats)
        for i in range(rows // TILE):
            span = (i + 1) * TILE
            place = slice(i * TILE, span)
            query = lax.broadcasted_iota(jnp.int32, (TILE, span), 0) + i * TILE
            key = lax.broadcasted_iota(jnp.int32, (TILE, span), 1)
            same = seg_col[place, 0:1] == seg_row[0:1, :span]
            bias[place, :span] = jnp.where(same & (key <= query), 0.0, MASKED)

    for i in range(rows // TILE):
        span = (i + 1) * TILE
        place = slice(i * TILE, span)
        query = q[place, :] * jnp.asarray(HEAD_DIM**-0.5, BF16)
        mixed = jnp.zeros((TILE, BLOCK), F32)
        held = stats[place, :]
        for side in range(2):
            mine = (lane // HEAD_DIM) == side
            part = jnp.where(mine, query, jnp.zeros_like(query))
            scores = dot_nt(part, k[:span, :]) + bias[place, :span]
            highest = jnp.max(scores, axis=1, keepdims=True)
            terms = jnp.exp(scores - highest)
            total = jnp.sum(terms, axis=1, keepdims=True)
            attend = (terms * (1.0 / total)).astype(BF16)
            mixed = jnp.where(mine, dot(attend, v[:span, :]), mixed)
            held = jnp.where(lane == 2 * pair + side, highest + jnp.log(total), held)
        stats[place, :] = held
        out[place, :] = mixed.astype(BF16)


def attention_forward(projected, seg_row, seg_col, first, count):
    rows, width = projected.shape[0], projected.shape[1] // 3
    pairs = width // BLOCK
    column = lambda start: pl.BlockSpec((rows, BLOCK), lambda h: (0, start + h))
    whole = lambda shape: pl.BlockSpec(shape, lambda h: (0, 0))
    return pl.pallas_call(
        attention_forward_kernel,
        grid=(count,),
        in_specs=[
            whole((8, rows)),
            whole((rows, BLOCK)),
            column(first),
            column(first + pairs),
            column(first + 2 * pairs),
        ],
        out_specs=[column(0), whole((rows, BLOCK))],
        out_shape=[
            jax.ShapeDtypeStruct((rows, count * BLOCK), BF16),
            jax.ShapeDtypeStruct((rows, BLOCK), F32),
        ],
        scratch_shapes=[pltpu.VMEM((rows, rows), F32)],
        compiler_params=pltpu.CompilerParams(vmem_limit_bytes=40 * MIB),
        cost_estimate=pl.CostEstimate(
            flops=4 * rows * rows * count * BLOCK,
            bytes_accessed=8 * rows * count * BLOCK,
            transcendentals=2 * count * rows * rows,
        ),
        name="attention_forward",
    )(seg_row, seg_col, projected, projected, projected)


def attention_backward_kernel(first, seg_row, seg_col, stats, q, k, v, g, dq, dk, dv, bias, dks, dvs):
    rows = q.shape[0]
    pair = pl.program_id(0)
    lane = lax.broadcasted_iota(jnp.int32, (1, BLOCK), 1)
    row = lax.broadcasted_iota(jnp.int32, (BLOCK, 1), 0)

    @pl.when(pair == 0)
    def _():
        for i in range(rows // TILE):
            span = (i + 1) * TILE
            place = slice(i * TILE, span)
            query = lax.broadcasted_iota(jnp.int32, (span, TILE), 1) + i * TILE
            key = lax.broadcasted_iota(jnp.int32, (span, TILE), 0)
            same = seg_col[:span, 0:1] == seg_row[0:1, place]
            bias[:span, place] = jnp.where(same & (key <= query), 0.0, MASKED)

    dks[...] = jnp.zeros_like(dks)
    dvs[...] = jnp.zeros_like(dvs)
    k_turned = k[...].T
    for i in range(rows // TILE):
        span = (i + 1) * TILE
        place = slice(i * TILE, span)
        query = q[place, :] * jnp.asarray(HEAD_DIM**-0.5, BF16)
        grad = g[place, :]
        turned = jnp.zeros((BLOCK, TILE), F32)
        for side in range(2):
            mine = (lane // HEAD_DIM) == side
            part = jnp.where(mine, query, jnp.zeros_like(query))
            grad_part = jnp.where(mine, grad, jnp.zeros_like(grad))
            level = stats[pl.ds(2 * (first + pair) + side, 1), place]
            scores = dot_nt(k[:span, :], part) + bias[:span, place]
            attend = jnp.exp(scores - level)
            grad_attend = dot_nt(v[:span, :], grad_part)
            inner = jnp.sum(attend * grad_attend, axis=0, keepdims=True)
            grad_scores = (attend * (grad_attend - inner)).astype(BF16)
            dks[:span, :] += dot(grad_scores, part)
            dvs[:span, :] += dot(attend.astype(BF16), grad_part)
            turned = jnp.where(
                (row // HEAD_DIM) == side, dot(k_turned[:, :span], grad_scores), turned
            )
        dq[place, :] = (turned.T * HEAD_DIM**-0.5).astype(BF16)
    dk[...] = dks[...].astype(BF16)
    dv[...] = dvs[...].astype(BF16)


def attention_backward(projected, grad_mixed, stats, seg_row, seg_col, first, count):
    rows, width = projected.shape[0], projected.shape[1] // 3
    pairs = width // BLOCK
    column = lambda start: pl.BlockSpec((rows, BLOCK), lambda h: (0, start + h))
    whole = lambda shape: pl.BlockSpec(shape, lambda h: (0, 0))
    share = jax.ShapeDtypeStruct((rows, count * BLOCK), BF16)
    return pl.pallas_call(
        functools.partial(attention_backward_kernel, first),
        grid=(count,),
        in_specs=[
            whole((8, rows)),
            whole((rows, BLOCK)),
            whole((BLOCK, rows)),
            column(first),
            column(first + pairs),
            column(first + 2 * pairs),
            column(first),
        ],
        out_specs=[column(0), column(0), column(0)],
        out_shape=[share, share, share],
        scratch_shapes=[
            pltpu.VMEM((rows, rows), F32),
            pltpu.VMEM((rows, BLOCK), F32),
            pltpu.VMEM((rows, BLOCK), F32),
        ],
        compiler_params=pltpu.CompilerParams(vmem_limit_bytes=40 * MIB),
        cost_estimate=pl.CostEstimate(
            flops=10 * rows * rows * count * BLOCK,
            bytes_accessed=14 * rows * count * BLOCK,
            transcendentals=2 * count * rows * rows,
        ),
        name="attention_backward",
    )(seg_row, seg_col, stats, projected, projected, projected, grad_mixed)


class Copies:
    def __init__(self, send_sems, recv_sems):
        self.send_sems, self.recv_sems, self.made = send_sems, recv_sems, []

    def start(self, source, target, device):
        n = len(self.made)
        one = pltpu.make_async_remote_copy(
            src_ref=source,
            dst_ref=target,
            send_sem=self.send_sems.at[n],
            recv_sem=self.recv_sems.at[n],
            device_id=device,
            device_id_type=pl.DeviceIdType.MESH,
        )
        one.start()
        self.made.append(one)
        return one


def wait_in(copies):
    for one in copies:
        one.wait_recv()


def forward_kernel(
    moves,
    tokens,
    mine,
    own_in,
    their_in,
    own_out,
    seg_row,
    seg_col,
    out_qkv,
    out_attn,
    out_params,
    first_in,
    first_out,
    column_in,
    column_out,
    normed,
    projected,
    mixed,
    stats,
    weights,
    bias,
    send_sems,
    recv_sems,
    local_sems,
):
    nz, nf = moves.nz, moves.nf
    dp, flat = lax.axis_index("dp"), lax.axis_index("fsdp")
    zed, core = dp // 2, lax.rem(dp, 2)
    rows, wide = tokens.shape
    sibling = (zed * 2 + 1 - core, flat)
    others = [(lax.rem(zed + k, nz) * 2 + core, flat) for k in range(1, nz)]
    hops = {bit: (dp, flat ^ bit) for bit in moves.orders[0]}

    barrier = pltpu.get_barrier_semaphore()
    for device in [sibling] + others + list(hops.values()):
        pl.semaphore_signal(barrier, inc=1, device_id=device, device_id_type=pl.DeviceIdType.MESH)
    pl.semaphore_wait(barrier, 1 + len(others) + len(hops))

    remote = Copies(send_sems, recv_sems)
    local = []

    def local_start(source, target):
        one = pltpu.make_async_copy(source, target, local_sems.at[len(local)])
        one.start()
        local.append(one)
        return one

    own = local_start(mine, weights.at[zed, core, flat])
    column = [remote.start(mine, weights.at[zed, core, flat], device) for device in others]
    crossed = [
        remote.start(their_in.at[0], first_in.at[zed, core, flat], sibling),
        remote.start(their_in.at[1], column_in.at[zed, core], sibling),
    ]
    blocks = [
        local_start(own_in.at[0], first_in.at[zed, core, flat]),
        local_start(own_out.at[0], first_out.at[zed, flat]),
        local_start(own_in.at[1], column_in.at[zed, core]),
        local_start(own_out.at[1], column_out.at[zed]),
    ]

    for i in range(rows // TILE):
        span = (i + 1) * TILE
        place = slice(i * TILE, span)
        query = lax.broadcasted_iota(jnp.int32, (TILE, span), 0) + i * TILE
        key = lax.broadcasted_iota(jnp.int32, (TILE, span), 1)
        same = seg_col[place, 0:1] == seg_row[0:1, :span]
        bias[place, :span] = jnp.where(same & (key <= query), 0.0, MASKED)
    stats[...] = jnp.zeros_like(stats)

    def stream_columns(stream):
        return slice(0, 2 * wide) if stream == 0 else slice(2 * wide, 4 * wide + BLOCK)

    def send_weights(stream, owner, device):
        place = weights.at[:, core, owner, :, stream_columns(stream)]
        return remote.start(place, place, device)

    own.wait()
    wait_in(column)
    near = [tuple(reversed(moves.orders[n]))[0] for n in range(2)]
    far = [moves.orders[n][0] for n in range(2)]
    hop_near = [send_weights(n, flat, hops[near[n]]) for n in range(2)]
    hop_far = [send_weights(n, flat, hops[far[n]]) for n in range(2)]
    place = weights.at[:, core, flat]
    across = [remote.start(place, place, sibling)]

    wait_in(crossed)
    for one in blocks:
        one.wait()
    first_column = []
    for device in others:
        place = first_in.at[zed, :, flat]
        first_column.append(remote.start(place, place, device))
        first_column.append(remote.start(own_out.at[0], first_out.at[zed, flat], device))

    wait_in(hop_near)
    hop_last = [send_weights(n, flat ^ near[n], hops[far[n]]) for n in range(2)]
    across += [send_weights(n, flat ^ near[n], sibling) for n in range(2)]
    wait_in(hop_far)
    across += [send_weights(n, flat ^ far[n], sibling) for n in range(2)]
    wait_in(hop_last)
    across += [send_weights(n, flat ^ near[n] ^ far[n], sibling) for n in range(2)]

    def send_first(stream, owner, device):
        place = first_in.at[:, :, owner] if stream == 0 else first_out.at[:, owner]
        return remote.start(place, place, device)

    wait_in(first_column)
    first_near = [send_first(n, flat, hops[near[n]]) for n in range(2)]
    first_far = [send_first(n, flat, hops[far[n]]) for n in range(2)]
    second_column = []
    for device in others:
        place = column_in.at[zed]
        second_column.append(remote.start(place, place, device))
        second_column.append(remote.start(own_out.at[1], column_out.at[zed], device))

    wait_in(across)
    whole = 2 * nz * nf * mine.shape[0]
    writes = [
        local_start(weights.at[:, :, :, :, pl.ds(0, 3 * wide)], out_qkv),
        local_start(weights.at[:, :, :, :, pl.ds(3 * wide, wide)], out_attn),
        local_start(weights.at[:, :, :, :, pl.ds(4 * wide, BLOCK)], out_params),
    ]
    turned = weights[:, :, :, :, pl.ds(4 * wide, BLOCK)].reshape(whole, BLOCK).astype(F32).T
    gain, shift = turned[0:1, :], turned[1:2, :]

    @pl.loop(0, rows // TILE)
    def _(t):
        place = pl.ds(pl.multiple_of(t * TILE, TILE), TILE)
        scaled, _ = norm_parts(tokens[place, :].astype(F32))
        normed[place, :] = (scaled * gain + shift).astype(BF16)
        for part in range(3):
            columns = pl.ds(part * wide, wide)
            matrix = weights[:, :, :, :, columns].reshape(whole, wide)
            projected[place, columns] = dot(normed[place, :], matrix).astype(BF16)

    lane = lax.broadcasted_iota(jnp.int32, (1, BLOCK), 1)
    pairs = wide // BLOCK

    def attend_pair(pair):
        columns = [
            pl.ds(pl.multiple_of(n * wide + pair * BLOCK, BLOCK), BLOCK) for n in range(3)
        ]
        for i in range(rows // TILE):
            span = (i + 1) * TILE
            place = slice(i * TILE, span)
            query = projected[place, columns[0]] * jnp.asarray(HEAD_DIM**-0.5, BF16)
            result = jnp.zeros((TILE, BLOCK), F32)
            held = stats[place, :]
            for side in range(2):
                ours = (lane // HEAD_DIM) == side
                part = jnp.where(ours, query, jnp.zeros_like(query))
                scores = dot_nt(part, projected[:span, columns[1]]) + bias[place, :span]
                highest = jnp.max(scores, axis=1, keepdims=True)
                terms = jnp.exp(scores - highest)
                total = jnp.sum(terms, axis=1, keepdims=True)
                attend = (terms * (1.0 / total)).astype(BF16)
                result = jnp.where(ours, dot(attend, projected[:span, columns[2]]), result)
                held = jnp.where(lane == 2 * pair + side, highest + jnp.log(total), held)
            stats[place, :] = held
            mixed[place, columns[0]] = result.astype(BF16)

    @pl.loop(0, pairs // 4)
    def _(pair):
        attend_pair(pair)

    wait_in(first_near)
    first_last = [send_first(n, flat ^ near[n], hops[far[n]]) for n in range(2)]

    @pl.loop(pairs // 4, pairs)
    def _(pair):
        attend_pair(pair)

    wait_in(first_far)
    wait_in(first_last)
    wait_in(second_column)
    for one in remote.made:
        one.wait_send()
    for one in writes:
        one.wait()


def forward_pass(moves, tokens, mine, own_in, their_in, own_out, seg_row, seg_col):
    nz, nf = moves.nz, moves.nf
    rows, wide = tokens.shape
    deep, half = own_in.shape[1:]
    part = own_out.shape[1]
    anywhere = pl.BlockSpec(memory_space=pl.ANY)
    inside = pl.BlockSpec(memory_space=pltpu.VMEM)
    shape = jax.ShapeDtypeStruct
    remote = 3 * (nz - 1) + 2 + 2 * 3 + 7 + 2 * (nz - 1) + 2 * 3
    return pl.pallas_call(
        functools.partial(forward_kernel, moves),
        in_specs=[inside] * 7,
        out_specs=[anywhere] * 7 + [inside] * 4,
        out_shape=[
            shape((nz, 2, nf, deep, 3 * wide), BF16),
            shape((nz, 2, nf, deep, wide), BF16),
            shape((nz, 2, nf, deep, BLOCK), BF16),
            shape((nz, 2, nf, deep, half), BF16),
            shape((nz, nf, part, wide), BF16),
            shape((nz, 2, deep, half), BF16),
            shape((nz, part, wide), BF16),
            shape((rows, wide), BF16),
            shape((rows, 3 * wide), BF16),
            shape((rows, wide), BF16),
            shape((rows, BLOCK), F32),
        ],
        scratch_shapes=[
            pltpu.VMEM((nz, 2, nf, deep, 4 * wide + BLOCK), BF16),
            pltpu.VMEM((rows, rows), F32),
            pltpu.SemaphoreType.DMA((remote,)),
            pltpu.SemaphoreType.DMA((remote,)),
            pltpu.SemaphoreType.DMA((8,)),
        ],
        compiler_params=pltpu.CompilerParams(
            collective_id=0, has_side_effects=True, vmem_limit_bytes=56 * MIB
        ),
        cost_estimate=pl.CostEstimate(
            flops=10 * rows * wide * wide, bytes_accessed=80 * wide * wide, transcendentals=0
        ),
        name="forward_pass",
    )(tokens, mine, own_in, their_in, own_out, seg_row, seg_col)


def attention_grads_kernel(
    moves, stream, deep, share, place, normed, mixed, dq, dk, dv, branch, near, far, low, sems
):
    zed, core, flat = place[0], place[1], place[2]
    for d in range(normed.shape[1] // TILE):
        rows = pl.ds(d * TILE, TILE)
        turned = normed[:, rows].T
        for n, part in enumerate((dq, dk, dv)):
            low[rows, pl.ds(n * share, share)] = dot(turned, part[...]).astype(BF16)
        low[rows, pl.ds(3 * share, share)] = dot(mixed[:, rows].T, branch[...]).astype(BF16)
    begun = []
    for number, offset in enumerate(moves.relative(stream)):
        for k in range(moves.nz):
            z_of = lax.rem(zed + k, moves.nz)
            for other in range(2):
                owner = core if other == 0 else 1 - core
                start = ((z_of * 2 + owner) * moves.nf + (flat ^ offset)) * deep
                rows = pl.ds(pl.multiple_of(start, deep), deep)
                target = (far if other else near).at[number, k]
                begun.append(
                    pltpu.make_async_copy(low.at[rows], target, sems.at[len(begun)])
                )
    for one in begun:
        one.start()
    for one in begun:
        one.wait()


def attention_grads(moves, stream, place, normed, mixed, dq, dk, dv, branch, deep):
    rows, wide = normed.shape
    share = dq.shape[1]
    anywhere = pl.BlockSpec(memory_space=pl.ANY)
    inside = pl.BlockSpec(memory_space=pltpu.VMEM)
    piece = jax.ShapeDtypeStruct((moves.nf, moves.nz, deep, 4 * share), BF16)
    return pl.pallas_call(
        functools.partial(attention_grads_kernel, moves, stream, deep, share),
        in_specs=[pl.BlockSpec(memory_space=pltpu.SMEM)] + [inside] * 6,
        out_specs=[anywhere] * 2,
        out_shape=[piece, piece],
        scratch_shapes=[
            pltpu.VMEM((wide, 4 * share), BF16),
            pltpu.SemaphoreType.DMA((2 * moves.nz * moves.nf,)),
        ],
        compiler_params=pltpu.CompilerParams(vmem_limit_bytes=40 * MIB),
        cost_estimate=pl.CostEstimate(
            flops=8 * rows * wide * share, bytes_accessed=20 * wide * share, transcendentals=0
        ),
        name="attention_grads",
    )(place, normed, mixed, dq, dk, dv, branch)


def gelu_both(value):
    square = value * value
    bent = jnp.tanh(ROOT_2_PI * value * (1.0 + CUBIC * square))
    half = 0.5 + 0.5 * bent
    slope = half + (0.5 * ROOT_2_PI) * value * (1.0 - bent * bent) * (1.0 + 3.0 * CUBIC * square)
    return (value * half, slope)


def expert_kernel(plan, *refs):
    moves, deep, chunk, chunks = plan[:4]
    expert, place, x_own, x_other, g_own, g_other = (plan[4],) + refs[:5]
    x_own, x_other, g_own, g_other = [
        one.at[expert] for one in (x_own, x_other, g_own, g_other)
    ]
    loaded = plan[5]
    weights, refs = refs[5 : 5 + loaded], refs[5 + loaded :]
    count = 4 if moves is not None else 2
    rows_out, refs = [refs[n // 2].at[n % 2] for n in range(4)], refs[2:]
    grads, refs = refs[:count], refs[count:]
    (win, wout, x, x_turned, g, branch, back, sum_in, sum_out, low_in, low_out, empty) = refs[:12]
    w_sems, x_sem, out_sems, row_sem = refs[12:]
    width = x.shape[1]
    most = x_own.shape[0] // BLOCK
    zed, flat, own_n, other_n = place[0], place[1], place[2], place[3]
    blocks = own_n + other_n
    tiles = (blocks + 1) // 2

    def block_rows(i):
        return pl.ds(pl.multiple_of(i * BLOCK, BLOCK), BLOCK)

    def each_block(act):
        for n, skip, a, b in ((own_n, 0, x_own, g_own), (other_n, own_n, x_other, g_other)):

            @pl.loop(0, n)
            def _(i):
                for outer, inner in ((a, x), (b, g)):
                    act(
                        pltpu.make_async_copy(
                            outer.at[block_rows(i)], inner.at[block_rows(skip + i)], x_sem
                        )
                    )

    each_block(lambda one: one.start())

    copies = []
    if loaded == 2:
        copies = [(weights[0], win), (weights[1], wout)]
    else:
        part_rows = chunk // moves.nf
        for stream in range(2):
            offsets = moves.relative(stream)
            half = len(offsets) // 2
            for number, offset in enumerate(offsets):
                piece = weights[stream * 2 + number // half].at[number % half]
                owner = flat ^ offset
                for k in range(moves.nz):
                    if stream == 0:
                        for part in range(2):
                            start = ((k * 2 + part) * moves.nf + owner) * deep
                            rows = pl.ds(pl.multiple_of(start, deep), deep)
                            copies.append((piece.at[k, part], win.at[rows]))
                    else:
                        start = (k * moves.nf + owner) * part_rows
                        rows = pl.ds(pl.multiple_of(start, part_rows), part_rows)
                        copies.append((piece.at[k], wout.at[rows]))
    begun = [
        pltpu.make_async_copy(source, target, w_sems.at[n])
        for n, (source, target) in enumerate(copies)
    ]
    for one in begun:
        one.start()
    empty[...] = jnp.zeros_like(empty)
    branch[...] = jnp.zeros_like(branch)
    back[...] = jnp.zeros_like(back)
    each_block(lambda one: one.wait())

    @pl.when(lax.rem(blocks, 2) == 1)
    def _():
        x[block_rows(blocks), :] = jnp.zeros((BLOCK, width), BF16)
        g[block_rows(blocks), :] = jnp.zeros((BLOCK, width), BF16)

    @pl.loop(0, tiles)
    def _(t):
        rows = pl.ds(pl.multiple_of(t * TILE, TILE), TILE)
        x_turned[:, rows] = x[rows, :].T

    for one in begun:
        one.wait()

    def grad_copies(j):
        columns = pl.ds(pl.multiple_of(j * chunk, chunk), chunk)
        if moves is None:
            made = [(low_in, grads[0].at[:, columns]), (low_out, grads[1].at[columns])]
        else:
            made = []
            k_of = zed ^ j
            half_deep = chunk // moves.nf // 2
            for stream in range(2):
                offsets = moves.relative(stream)
                half = len(offsets) // 2
                for number, offset in enumerate(offsets):
                    target = grads[stream * 2 + number // half].at[number % half]
                    owner = flat ^ offset
                    for part in range(2):
                        if stream == 0:
                            for k in range(moves.nz):
                                start = (((zed ^ k) * 2 + part) * moves.nf + owner) * deep
                                rows = pl.ds(pl.multiple_of(start, deep), deep)
                                place_of = target.at[k, pl.ds(part * deep, deep), columns]
                                made.append((low_in.at[rows], place_of))
                        else:
                            start = (owner * 2 + part) * half_deep
                            rows = pl.ds(pl.multiple_of(start, half_deep), half_deep)
                            place_of = target.at[k_of, :, pl.ds(part * width, width)]
                            made.append((low_out.at[rows], place_of))
        return [
            pltpu.make_async_copy(source, target, out_sems.at[n])
            for n, (source, target) in enumerate(made)
        ]

    @pl.loop(0, chunks)
    def _(j):
        columns = pl.ds(pl.multiple_of(j * chunk, chunk), chunk)
        sum_in[...] = jnp.zeros_like(sum_in)
        sum_out[...] = jnp.zeros_like(sum_out)

        @pl.loop(0, tiles)
        def _(t):
            rows = pl.ds(pl.multiple_of(t * TILE, TILE), TILE)
            g_tile = g[rows, :]
            inner = dot(x[rows, :], win[:, columns])
            grad_active = dot_nt(g_tile, wout[columns, :])
            active, slope = gelu_both(inner)
            active_low = active.astype(BF16)
            grad_inner = (grad_active * slope).astype(BF16)
            branch[rows, :] += dot(active_low, wout[columns, :])
            back[rows, :] += dot_nt(grad_inner, win[:, columns])
            sum_in[...] += dot(x_turned[:, rows], grad_inner)
            sum_out[...] += dot_tn(active_low, g_tile)

        @pl.when(j > 0)
        def _():
            for one in grad_copies(j - 1):
                one.wait()

        low_in[...] = sum_in[...].astype(BF16)
        low_out[...] = sum_out[...].astype(BF16)
        for one in grad_copies(j):
            one.start()

    @pl.loop(0, tiles)
    def _(t):
        rows = pl.ds(pl.multiple_of(t * TILE, TILE), TILE)
        x[rows, :] = branch[rows, :].astype(BF16)
        g[rows, :] = back[rows, :].astype(BF16)

    def each_result(act):
        for n, skip, a, b in (
            (own_n, 0, rows_out[0], rows_out[1]),
            (other_n, own_n, rows_out[2], rows_out[3]),
        ):

            @pl.loop(0, n)
            def _(i):
                for outer, inner in ((a, x), (b, g)):
                    act(
                        pltpu.make_async_copy(
                            inner.at[block_rows(skip + i)], outer.at[block_rows(i)], row_sem
                        )
                    )

            @pl.loop(n, most)
            def _(i):
                for outer in (a, b):
                    act(pltpu.make_async_copy(empty, outer.at[block_rows(i)], row_sem))

    each_result(lambda one: one.start())
    each_result(lambda one: one.wait())
    for one in grad_copies(chunks - 1):
        one.wait()


def expert_block(moves, expert, place, sorted_rows, weights, deep, half_hidden):
    capacity, width = sorted_rows[0].shape[1:]
    most = 2 * capacity
    if moves is not None:
        chunks = moves.nz
        copies = 4 * moves.nz * moves.nf
    else:
        chunks = 4
        copies = 2
    chunk = half_hidden // chunks
    anywhere = pl.BlockSpec(memory_space=pl.ANY)
    row_shape = jax.ShapeDtypeStruct((2, capacity, width), BF16)
    if moves is not None:
        block = (moves.nf // 2, moves.nz, 2 * deep, half_hidden)
        grads = [jax.ShapeDtypeStruct(block, BF16)] * 4
    else:
        grads = [jax.ShapeDtypeStruct(w.shape, BF16) for w in weights]
    return pl.pallas_call(
        functools.partial(expert_kernel, (moves, deep, chunk, chunks, expert, len(weights))),
        in_specs=[pl.BlockSpec(memory_space=pltpu.SMEM)] + [anywhere] * (4 + len(weights)),
        out_specs=[anywhere] * (2 + len(grads)),
        out_shape=[row_shape] * 2 + grads,
        scratch_shapes=[
            pltpu.VMEM((width, half_hidden), BF16),
            pltpu.VMEM((half_hidden, width), BF16),
            pltpu.VMEM((most, width), BF16),
            pltpu.VMEM((width, most), BF16),
            pltpu.VMEM((most, width), BF16),
            pltpu.VMEM((most, width), F32),
            pltpu.VMEM((most, width), F32),
            pltpu.VMEM((width, chunk), F32),
            pltpu.VMEM((chunk, width), F32),
            pltpu.VMEM((width, chunk), BF16),
            pltpu.VMEM((chunk, width), BF16),
            pltpu.VMEM((BLOCK, width), BF16),
            pltpu.SemaphoreType.DMA((copies,)),
            pltpu.SemaphoreType.DMA,
            pltpu.SemaphoreType.DMA((copies,)),
            pltpu.SemaphoreType.DMA,
        ],
        compiler_params=pltpu.CompilerParams(vmem_limit_bytes=56 * MIB),
        cost_estimate=pl.CostEstimate(
            flops=12 * 1024 * width * half_hidden,
            bytes_accessed=8 * width * half_hidden + 32 * 1024 * width,
            transcendentals=1024 * half_hidden,
        ),
        name="expert_block",
    )(place, *sorted_rows, *weights)


def gather_experts_whole(w_expert_in, w_expert_out, core, nz):
    width, hidden = w_expert_out.shape[2], w_expert_in.shape[2]
    all_in = lax.all_gather(w_expert_in, AXES, axis=1, tiled=True)
    all_out = lax.all_gather(w_expert_out, AXES, axis=1, tiled=True)
    all_in = all_in.reshape(EXPERTS, width, nz, 2, hidden // (2 * nz))
    all_in = lax.dynamic_index_in_dim(all_in, core, 3, False)
    all_in = all_in.reshape(EXPERTS, width, hidden // 2)
    all_out = all_out.reshape(EXPERTS, nz, 2, hidden // (2 * nz), width)
    all_out = lax.dynamic_index_in_dim(all_out, core, 2, False)
    all_out = all_out.reshape(EXPERTS, hidden // 2, width)
    return [[all_in[e], all_out[e]] for e in range(EXPERTS)]


def reduce_expert(moves, pieces):
    sum_in = moves.reduce_flat(pieces[0], pieces[1], 0)
    sum_out = moves.reduce_flat(pieces[2], pieces[3], 1)
    sums = moves.reduce_z_pair(jnp.stack([sum_in, sum_out], axis=1))
    wide = sums.shape[2] // 2
    return sums[0], jnp.concatenate([sums[1, :, :wide], sums[1, :, wide:]], axis=0)


def join_cores(moves, shares_in, core, deep):
    both = jnp.stack(shares_in)
    both = both.reshape(EXPERTS, 2, deep, both.shape[2])
    ours = lax.dynamic_index_in_dim(both, core, 1, False)
    theirs = moves.core(lax.dynamic_index_in_dim(both, 1 - core, 1, False))
    low_core = jnp.where(core == 0, ours, theirs).reshape(EXPERTS, deep, moves.nz, 1, -1)
    high_core = jnp.where(core == 0, theirs, ours).reshape(EXPERTS, deep, moves.nz, 1, -1)
    return jnp.concatenate([low_core, high_core], axis=3).reshape(EXPERTS, deep, -1)


def reduce_vectors(moves, vectors, place, deep):
    zed, core, flat = place
    held = vectors.reshape(4, moves.nz, 2, moves.nf, deep)
    held = lax.dynamic_index_in_dim(held, core, 2, False) + moves.core(
        lax.dynamic_index_in_dim(held, 1 - core, 2, False)
    )
    held = jnp.moveaxis(held, 2, 0)
    bit = moves.nf // 2
    while bit:
        pair = held.reshape((2, bit) + held.shape[1:])
        side = lax.rem(flat // bit, 2)
        held = lax.dynamic_index_in_dim(pair, side, 0, False) + moves.flat(
            lax.dynamic_index_in_dim(pair, 1 - side, 0, False), bit
        )
        bit //= 2
    held = held[0]
    total = lax.dynamic_index_in_dim(held, zed, 1, False)
    for k in range(1, moves.nz):
        other = lax.dynamic_index_in_dim(held, lax.rem(zed + k, moves.nz), 1, False)
        total = total + moves.along(other, k)
    return total


def local(
    nd,
    nf,
    tokens,
    seq_lengths,
    expert_ids,
    grad_out,
    ln1_gain,
    ln1_bias,
    w_qkv,
    w_attn_out,
    ln2_gain,
    ln2_bias,
    w_expert_in,
    w_expert_out,
):
    rows, width = tokens.shape
    deep = w_qkv.shape[0]
    hidden = w_expert_in.shape[2]
    half_hidden = hidden // 2
    half = width // 2
    moves = Moves(nd, nf)
    nz = moves.nz
    staged = deep % 32 == 0
    core = lax.rem(lax.axis_index("dp"), 2)
    zed = lax.axis_index("dp") // 2
    flat = lax.axis_index("fsdp")
    place = jnp.stack([zed, core, flat]).astype(jnp.int32)

    params = jnp.stack([ln1_gain, ln1_bias, ln2_gain, ln2_bias], axis=1)
    params = jnp.pad(params, ((0, 0), (0, BLOCK - 4)))
    mine = jnp.concatenate([w_qkv, w_attn_out, params], axis=1)
    tokens_wide = tokens.astype(F32)
    positions = jnp.arange(rows, dtype=jnp.int32)
    bounds = jnp.cumsum(seq_lengths[0])
    segment = jnp.sum((positions[:, None] >= bounds[None, :]).astype(jnp.int32), axis=1)
    seg_row = jnp.broadcast_to(segment[None, :], (8, rows))
    seg_col = jnp.broadcast_to(segment[:, None], (rows, BLOCK))
    if staged:
        by_core = w_expert_in.reshape(EXPERTS, deep, nz, 2, hidden // (2 * nz))
        own_in, their_in = [
            lax.dynamic_index_in_dim(by_core, which, 3, False).reshape(EXPERTS, deep, half_hidden)
            for which in (core, 1 - core)
        ]
        outs = forward_pass(moves, tokens, mine, own_in, their_in, w_expert_out, seg_row, seg_col)
        whole_qkv, whole_attn, params, first_in = [
            one.reshape(-1, one.shape[-1]) for one in outs[:4]
        ]
        first_out = outs[4].reshape(half_hidden, width)
        column_in, column_out, normed_one, projected, mixed, stats = outs[5:]
        held = [moves.gather_first(column_in, 0), moves.gather_first(column_out, 1)]
        last = [moves.gather_last(held[0], 0), moves.gather_last(held[1], 1)]
        expert_weights = [[first_in, first_out], [held[0], last[0], held[1], last[1]]]
    else:
        whole = lax.all_gather(mine, AXES, axis=0, tiled=True)
        whole_qkv, whole_attn = whole[:, : 3 * width], whole[:, 3 * width : 4 * width]
        params = whole[:, 4 * width :]
        expert_weights = gather_experts_whole(w_expert_in, w_expert_out, core, nz)
    gain_one, bias_one, gain_two, bias_two = [
        params[:, n].astype(F32)[None, :] for n in range(4)
    ]
    scaled_one, inverse_one = norm_parts(tokens_wide)
    if not staged:
        normed_one = (scaled_one * gain_one + bias_one).astype(BF16)
        projected = dot(normed_one, whole_qkv).astype(BF16)
        mixed, stats = attention_forward(projected, seg_row, seg_col, 0, width // BLOCK)

    routed = expert_ids[:, 0]
    second = (routed == 1).astype(jnp.int32)
    rank_second = jnp.cumsum(second) - second
    second_n = jnp.sum(second)
    rank = jnp.where(routed == 1, rank_second, positions - rank_second)
    capacity = 3 * rows // 4
    slots = jnp.arange(capacity, dtype=jnp.int32)[:, None]
    spread = [
        ((rank[None, :] == slots) & (routed[None, :] == e)).astype(BF16) for e in range(EXPERTS)
    ]
    split = jnp.stack([rows - second_n, second_n]).astype(jnp.int32)
    split = (split + BLOCK - 1) // BLOCK
    spread_all = jnp.concatenate(spread, axis=0)
    grad_sorted = dot(spread_all, grad_out).astype(BF16)
    grad_sorted = after(grad_sorted, projected)
    note = jnp.broadcast_to(split[:, None].astype(BF16), (2, width))
    note = jnp.pad(note, ((0, 14), (0, 0)))
    noted = moves.core(jnp.concatenate([grad_sorted, note], axis=0))
    split_other = noted[2 * capacity : 2 * capacity + 2, 0].astype(jnp.int32)
    grad_sorted = grad_sorted.reshape(EXPERTS, capacity, width)
    grad_sorted_other = noted[: 2 * capacity].reshape(EXPERTS, capacity, width)

    pairs = width // BLOCK
    parts = [(0, pairs // 2), (pairs // 2, pairs // 2)]
    stats_turned = stats.T
    hidden_one = tokens_wide + dot(mixed, whole_attn)
    scaled_two, inverse_two = norm_parts(hidden_one)
    normed_two = (scaled_two * gain_two + bias_two).astype(BF16)

    sorted_rows = dot(spread_all, normed_two).astype(BF16)
    sorted_other = moves.core(sorted_rows).reshape(EXPERTS, capacity, width)
    sorted_rows = sorted_rows.reshape(EXPERTS, capacity, width)
    results, grad_pieces = [], []
    for e in range(EXPERTS):
        table = jnp.stack([zed, flat, split[e], split_other[e]]).astype(jnp.int32)
        outs = expert_block(
            moves if staged else None,
            e,
            table,
            [sorted_rows, sorted_other, grad_sorted, grad_sorted_other],
            list(expert_weights[e]),
            deep,
            half_hidden,
        )
        results.append(add_low(outs[0], moves.core(outs[1])))
        grad_pieces.append(outs[2:])
    both = jnp.concatenate(results, axis=1)
    grad_normed_two = dot_tn(spread_all, both[1])
    branch = dot_tn(spread_all, both[0])
    block_result = (hidden_one + branch).astype(BF16)

    grad_gain_two = jnp.sum(grad_normed_two * scaled_two, axis=0)
    grad_bias_two = jnp.sum(grad_normed_two, axis=0)
    grad_hidden = grad_out.astype(F32) + norm_back(
        grad_normed_two, scaled_two, inverse_two, gain_two
    )
    grad_branch = grad_hidden.astype(BF16)
    grad_mixed = dot_nt(grad_branch, whole_attn).astype(BF16)

    grad_parts, shares = [], []
    for n, (first, count) in enumerate(parts):
        trio = attention_backward(
            projected, grad_mixed, stats_turned, seg_row, seg_col, first, count
        )
        grad_parts.append(trio)
        if staged:
            near, far = attention_grads(
                moves,
                n,
                place,
                normed_one,
                mixed,
                *trio,
                grad_branch[:, first * BLOCK : (first + count) * BLOCK],
                deep,
            )
            pieces = add_low(near, moves.core(far))
            shares.append(moves.reduce_flat(pieces[: nf // 2], pieces[nf // 2 :], n))
    grad_projected = jnp.concatenate(
        [grad_parts[n][m] for m in range(3) for n in range(2)], axis=1
    )
    grad_normed_one = dot_nt(grad_projected, whole_qkv)
    grad_gain_one = jnp.sum(grad_normed_one * scaled_one, axis=0)
    grad_bias_one = jnp.sum(grad_normed_one, axis=0)
    grad_input = grad_hidden + norm_back(grad_normed_one, scaled_one, inverse_one, gain_one)
    vectors = jnp.stack([grad_gain_one, grad_bias_one, grad_gain_two, grad_bias_two])

    if staged:
        sums = [reduce_expert(moves, pieces) for pieces in grad_pieces]
        share_in = join_cores(moves, [one[0] for one in sums], core, deep)
        share_out = jnp.stack([one[1] for one in sums])
        vectors = reduce_vectors(moves, vectors, (zed, core, flat), deep)
        share = moves.reduce_z(jnp.stack(shares, axis=1)).reshape(2, deep, 4, half)
        share = jnp.moveaxis(share, 0, 2).reshape(deep, 4 * width)
        share_qkv, share_attn = share[:, : 3 * width], share[:, 3 * width :]
    else:
        share_qkv = lax.psum_scatter(
            dot_tn(normed_one, grad_projected), AXES, scatter_dimension=0, tiled=True
        )
        share_attn = lax.psum_scatter(
            dot_tn(mixed, grad_branch), AXES, scatter_dimension=0, tiled=True
        )
        vectors = lax.psum_scatter(vectors, AXES, scatter_dimension=1, tiled=True)
        full_in = jnp.stack([pieces[0] for pieces in grad_pieces])
        full_out = jnp.stack([pieces[1] for pieces in grad_pieces])
        full_in = full_in.reshape(EXPERTS, width, nz, 1, -1).astype(F32)
        full_out = full_out.reshape(EXPERTS, nz, 1, -1, width).astype(F32)
        chosen = jnp.arange(2) == core
        full_in = jnp.where(chosen[None, None, None, :, None], full_in, 0.0)
        full_out = jnp.where(chosen[None, None, :, None, None], full_out, 0.0)
        share_in = lax.psum_scatter(
            full_in.reshape(EXPERTS, width, hidden), AXES, scatter_dimension=1, tiled=True
        )
        share_out = lax.psum_scatter(
            full_out.reshape(EXPERTS, hidden, width), AXES, scatter_dimension=1, tiled=True
        )
    return (
        block_result,
        grad_input,
        vectors[0],
        vectors[1],
        share_qkv,
        share_attn,
        vectors[2],
        vectors[3],
        share_in,
        share_out,
    )


def solution(mesh):
    rows = P(AXES, None)
    vector = P(AXES)
    expert = P(None, AXES, None)
    return jax.shard_map(
        functools.partial(local, mesh.shape["dp"], mesh.shape["fsdp"]),
        mesh=mesh,
        in_specs=(
            rows, rows, rows, rows, vector, vector, rows, rows, vector, vector, expert, expert
        ),
        out_specs=(
            rows, rows, vector, vector, rows, rows, vector, vector, expert, expert
        ),
        check_vma=False,
    )
```

time: 2340 us -> 636 us (0.27)
  waiting for transfers between devices: 1550 us -> 146 us
  matrix products: 430 us -> 41.7 us
  Pallas kernels: 0 us -> 290 us
  local copies, waits for them, and re-layouts: 124 us -> 34.3 us
  blocking collectives: 81.5 us -> 0 us
  other arithmetic: 128 us -> 58.9 us
  starting transfers between devices: 0.31 us -> 51.6 us
    reduce_scatter x4 -> x0, waiting for transfers between devices: 1440 us -> none  [the longest x1 711 us: local(): lax.psum_scatter(grad_in_weight, ('dp', 'fsdp'), scatter_dimension=1, til...]
    dot_general x26 -> x7, matrix products: 430 us -> 41.7 us  [the longest x3 15.6 us: dot(): return jnp.dot(a, b, preferred_element_type=F32)]
    pallas_call x0 -> x7, Pallas kernels: none -> 290 us  [the longest x1 139 us: forward_pass(): pl.pallas_call(functools.partial(forward_kernel, moves), in_specs=[inside...]
    ppermute x0 -> x36, waiting for transfers between devices: none -> 146 us  [send(): return lax.ppermute(value, AXES, pairs)]
    all_gather x4 -> x0, waiting for transfers between devices: 108 us -> none  [the longest x1 92.9 us: local(): lax.all_gather(w_expert_out, ('dp', 'fsdp'), axis=1, tiled=True)]
    unnamed x2 -> x0, blocking collectives: 81.5 us -> none
    ppermute x0 -> x36, starting transfers between devices: none -> 51.6 us  [send(): return lax.ppermute(value, AXES, pairs)]
    reduce_sum x7 -> x2, other arithmetic: 42.5 us -> 0.72 us  [the longest x1 0.64 us: local(): second_n = jnp.sum(second)]
  transfers between devices with their start and end apart: 8 -> 36, of which waited for: 5 -> 13; matrix products, arithmetic and copies ran while one was open for 23% -> 17% of each run, Pallas kernels for 0% -> 24%
where the time goes in v1:
time: 636 us; the launch traced here: 625 us
  Pallas kernels  290 us (46%)
  waiting for transfers between devices  146 us (23%)
  other arithmetic  58.9 us (9%)
  starting transfers between devices  51.6 us (8%)
  matrix products  41.7 us (7%)
  local copies, waits for them, and re-layouts  34.3 us (5%)
    ppermute x36, waiting for transfers between devices, send(): return lax.ppermute(value, AXES, pairs)  146 us
    pallas_call x1, Pallas kernels, forward_pass(): pl.pallas_call(functools.partial(forward_kernel, moves), in_specs=[inside...  139 us
    pallas_call x2, Pallas kernels, expert_block(): pl.pallas_call(functools.partial(expert_kernel, (moves, deep, chunk, chun...  86.2 us
    ppermute x36, starting transfers between devices, send(): return lax.ppermute(value, AXES, pairs)  51.6 us
    pallas_call x2, Pallas kernels, attention_backward(): pl.pallas_call(functools.partial(attention_backward_kernel, first), grid=...  42.5 us
    pallas_call x2, Pallas kernels, attention_grads(): pl.pallas_call(functools.partial(attention_grads_kernel, moves, stream, d...  21.8 us
    convert_element_type x12, other arithmetic, add_low(): return (a.astype(F32) + b.astype(F32)).astype(BF16)  19.5 us
    dot_general x3, matrix products, dot(): return jnp.dot(a, b, preferred_element_type=F32)  15.6 us
  transfers between devices with their start and end apart: 36, of which 13 were waited for; matrix products, arithmetic and copies ran while one was open for 17% of the time, Pallas kernels for 24%

profile of v1, /device:TPU:0, one launch (start us, length us, event | category | flops | bytes accessed | tf_op | source)
XLA Modules:
  0.0 624.7 jit_solution(3679220387674582528)
XLA Ops:
  2.3 3.3 dynamic-slice_reduce_fusion
  10.8 5.2 convolution_convert_fusion.1
  17.6 139.3 %forward_pass.1 = (bf16[4,2,4,32,3072]{4,3,2,1,0:T(8,128)(2,1)}, bf16[4,2,4,32,1024]{4,3,2,1,0:T(8,128)(2,1)}, bf16[4,2,4,32,128]{4,3,2,1,0:T(8,128)(2,1)}, bf16...) custom-call(bf16[1024,1024]{1,0:T(8,128)(2,1)} %tokens.1, ...), custom_call_target="tpu_custom_call" | custom-call | flops 10737418240 | bytes 83886080 | tf_op jit(solution)/shard_map/forward_pass/pallas_call | solution.py:508
  158.3 4.3 pad_maximum_fusion
  162.6 2.4 fusion.55
  168.6 7.9 %convolution_convert_fusion = bf16[1536,1024]{1,0:T(8,128)(2,1)} fusion(f32[1024,1024]{1,0:T(8,128)} %copy-done.17, f32[1024]{0:T(1024)S(1)} %bitcast.158, f32[1024]{0:T(1024)S(1)} %bitcast.154, f32[1024]{0:T(1024)S(1)} %add_rsqrt_fusion.1, f32[1024]{0:T(1024)S(1)} %broadcast_multiply_fusion.5, pred[768,1024]{1,0:T(32,128)(4,1)} %copy-done.42, ...), kind=kOutput, calls=%fused_computation.32 | convolution fusion | flops 3229614080 | bytes 8929280 | tf_op jit(solution)/shard_map/dot_general | solution.py:28
  177.1 2.0 collective-permute-start.3
  179.7 23.1 %collective-permute-done.3 = bf16[1,4,2,32,2048]{4,3,2,1,0:T(8,128)(2,1)} collective-permute-done((bf16[1,4,2,32,2048]{4,3,2,1,0:T(8,128)(2,1)}, bf16[1,4,2,32,2048]{4,3,2,1,0:T(8,128)(2,1)}, u32[]{:S(2)}, u32[]{:S(2)}) %collective-permute-start.3) | collective-permute-done | bytes 1048608 | tf_op jit(solution)/shard_map/ppermute | solution.py:76
  202.7 1.7 pad_maximum_fusion.2.refs_5_
  204.5 1.8 collective-permute-start.4
  206.3 1.7 pad_maximum_fusion.3.refs_7_
  208.8 3.9 slice.233
  213.9 1.9 pad_add_fusion.1.refs_0_
  215.8 43.0 %expert_block.2 = (bf16[2,768,1024]{2,1,0:T(8,128)(2,1)}, bf16[2,768,1024]{2,1,0:T(8,128)(2,1)}, bf16[2,4,64,2048]{3,2,1,0:T(8,128)(2,1)}, bf16[2,4,64,2048]{3,2...) custom-call(s32[4]{0:T(128)} %pad_add_fusion.1.refs_0_, ...), custom_call_target="tpu_custom_call" | custom-call | flops 25769803776 | bytes 50331648 | tf_op jit(solution)/shard_map/expert_block/pallas_call | solution.py:792
  260.9 1.9 pad_add_fusion.3.refs_0_
  262.8 43.1 %expert_block.3 = (bf16[2,768,1024]{2,1,0:T(8,128)(2,1)}, bf16[2,768,1024]{2,1,0:T(8,128)(2,1)}, bf16[2,4,64,2048]{3,2,1,0:T(8,128)(2,1)}, bf16[2,4,64,2048]{3,2...) custom-call(s32[4]{0:T(128)} %pad_add_fusion.3.refs_0_, ...), custom_call_target="tpu_custom_call" | custom-call | flops 25769803776 | bytes 50331648 | tf_op jit(solution)/shard_map/expert_block/pallas_call | solution.py:792
  307.2 9.3 %collective-permute-start.31 = (bf16[2,4,64,2048]{3,2,1,0:T(8,128)(2,1)}, bf16[2,4,64,2048]{3,2,1,0:T(8,128)(2,1)S(1)}, u32[]{:S(2)}, u32[]{:S(2)}) collective-permute-start(bf16[2,4,64,2048]{3,2,1,0:T(8,128)(2,1)} %get-tuple-element.77), channel_id=1, source_target_pairs={{0,2},{1,3},{2,0},{3,1},{4,6},{5,7},{6,4},{7,5},{8,10},{9,11},{10,... | collective-permute-start | bytes 6291464 | tf_op jit(solution)/shard_map/ppermute | solution.py:76
  318.6 3.2 add_convert_fusion.5
  322.0 2.5 add_convert_fusion.4
  324.6 27.6 %collective-permute-done.29 = bf16[2,4,64,2048]{3,2,1,0:T(8,128)(2,1)} collective-permute-done((bf16[2,4,64,2048]{3,2,1,0:T(8,128)(2,1)}, bf16[2,4,64,2048]{3,2,1,0:T(8,128)(2,1)}, u32[]{:S(2)}, u32[]{:S(2)}) %collective-permute-start.29) | collective-permute-done | bytes 2097184 | tf_op jit(solution)/shard_map/ppermute | solution.py:76
  352.6 2.6 add_convert_fusion.3
  356.3 6.9 %collective-permute-done.31 = bf16[2,4,64,2048]{3,2,1,0:T(8,128)(2,1)S(1)} collective-permute-done((bf16[2,4,64,2048]{3,2,1,0:T(8,128)(2,1)}, bf16[2,4,64,2048]{3,2,1,0:T(8,128)(2,1)S(1)}, u32[]{:S(2)}, u32[]{:S(2)}) %collective-permute-start.31) | collective-permute-done | bytes 2097184 | tf_op jit(solution)/shard_map/ppermute | solution.py:76
  363.2 2.0 collective-permute-start.30
  367.2 18.6 %collective-permute-done.24 = bf16[1,4,64,2048]{3,2,1,0:T(8,128)(2,1)S(1)} collective-permute-done((bf16[1,4,64,2048]{3,2,1,0:T(8,128)(2,1)S(1)}, bf16[1,4,64,2048]{3,2,1,0:T(8,128)(2,1)S(1)}, u32[]{:S(2)}, u32[]{:S(2)}) %collective-permute-start.24) | collective-permute-done | bytes 1048608 | tf_op jit(solution)/shard_map/ppermute | solution.py:76
  385.7 2.0 collective-permute-start.32
  389.6 2.4 collective-permute-start.27
  393.9 3.3 add_convert_fusion.1
  398.6 6.4 %multiply_reduce_fusion = (f32[1024]{0:T(1024)S(1)}, f32[1024]{0:T(1024)S(1)}, f32[1024]{0:T(1024)S(1)}, f32[1024]{0:T(1024)S(1)}, f32[1024,1024]{1,0:T(8,128)S(1)}) fusion(f32[1024,1024]{1,0:T(8,128)S(1)} %copy-done.18, f32[1024]{0:T(1024)S(1)} %add_rsqrt_fusion.1, f32[1024]{0:T(1024)S(1)} %broadcast_multiply_fusion.5, f32[1024]{0:T(1024)S(1)} %bitcast.155, ...), kind=kOutput, calls=%fused_computation.25 | convolution fusion | flops 3238522880 | bytes 16281600 | tf_op jit(solution)/shard_map/dot_general | solution.py:36
  405.0 3.0 fusion.50
  408.0 2.4 convolution_convert_fusion.2.g
  410.8 21.0 %attention_backward.3 = (bf16[1024,512]{1,0:T(8,128)(2,1)S(1)}, bf16[1024,512]{1,0:T(8,128)(2,1)S(1)}, bf16[1024,512]{1,0:T(8,128)(2,1)S(1)}) custom-call(s32[8,1024]{1,0:T(8,128)S(1)} %copy-done.11, s32[1024,128]{1,0:T(8,128)S(1)} %copy-done, f32[128,1024]{1,0:T(8,128)S(1)} %bitcast.139, bf16[1024,3072]{1,0:T(8,128)(2,1)S(1)} %bitcast.138, ...), custom_call_target="tpu_custom_call" | custom-call | flops 5368709120 | bytes 7340032 | tf_op jit(solution)/shard_map/attention_backward/pallas_call | solution.py:264
  431.8 21.5 %attention_backward.2 = (bf16[1024,512]{1,0:T(8,128)(2,1)S(1)}, bf16[1024,512]{1,0:T(8,128)(2,1)S(1)}, bf16[1024,512]{1,0:T(8,128)(2,1)S(1)}) custom-call(s32[8,1024]{1,0:T(8,128)S(1)} %copy-done.11, s32[1024,128]{1,0:T(8,128)S(1)} %copy-done, f32[128,1024]{1,0:T(8,128)S(1)} %bitcast.140, bf16[1024,3072]{1,0:T(8,128)(2,1)S(1)} %bitcast.138, ...), custom_call_target="tpu_custom_call" | custom-call | flops 5368709120 | bytes 7340032 | tf_op jit(solution)/shard_map/attention_backward/pallas_call | solution.py:264
  453.3 2.0 fusion.29
  457.5 6.3 %add_convert_fusion.8 = bf16[1024,1024]{1,0:T(8,128)(2,1)} fusion(f32[1024,1024]{1,0:T(8,128)S(1)} %copy-done.18, bf16[2,768,1024]{2,1,0:T(8,128)(2,1)} %add_convert_fusion.1, bf16[2,768,1024]{2,1,0:T(8,128)(2,1)S(1)} %copy-done.30, pred[768,1024]{1,0:T(32,128)(4,1)S(1)} %copy-done.44, pred[768,1024]{1,0:T(32,128)(4,1)S(1)} %copy-done.41), kind=kOutput, calls=%fused_computation.28 | convolution fusion | flops 3231186944 | bytes 14155776 | tf_op jit(solution)/shard_map/dot_general | solution.py:36
  470.2 11.1 %fusion.9 = (f32[1024]{0:T(1024)S(1)}, f32[1024]{0:T(1024)S(1)}, f32[1024]{0:T(1024)S(1)}, f32[1024]{0:T(1024)S(1)}, f32[1024,1024]{1,0:T(8,128)}) fusion(bf16[1024,1024]{1,0:T(8,128)(2,1)S(1)} %copy-done.16, f32[1024]{0:T(1024)S(1)} %add_rsqrt_fusion, f32[1024]{0:T(1024)S(1)} %broadcast_multiply_fusion.2, f32[1024]{0:T(1024)S(1)} %bitcast.151, ...), kind=kOutput, calls=%fused_computation.17 | convolution fusion | flops 6452932608 | bytes 18903040 | tf_op jit(solution)/shard_map/dot_general | solution.py:32
  484.1 6.3 %fusion.8 = f32[1024,1024]{1,0:T(8,128)} fusion(f32[1024,1024]{1,0:T(8,128)} %get-tuple-element.91, bf16[1024,1024]{1,0:T(8,128)(2,1)} %tokens.1, f32[1024,1024]{1,0:T(8,128)} %get-tuple-element.128, f32[1024]{0:T(1024)S(1)} %broadcast_multiply_fusion, f32[1024]{0:T(1024)S(1)} %broadcast_multiply_fusion.1, f32[1024]{0:T(1024)S(1)} %bitcast.152, ...), kind=kLoop, calls=%fused_computation.16 | loop fusion | flops 9437184 | bytes 14700544 | tf_op jit(solution)/shard_map/add | solution.py:1030
  492.2 10.9 %attention_grads.3 = (bf16[4,4,32,2048]{3,2,1,0:T(8,128)(2,1)S(1)}, bf16[4,4,32,2048]{3,2,1,0:T(8,128)(2,1)S(1)}) custom-call(s32[3]{0:T(128)S(1)} %pad_add_fusion.4.place, bf16[1024,1024]{1,0:T(8,128)(2,1)S(1)} %copy-done.14, bf16[1024,1024]{1,0:T(8,128)(2,1)S(1)} %copy-done.13, bf16[1024,512]{1,0:T(8,128)(2,1)S(1)} %copy-done.4, ...), custom_call_target="tpu_custom_call" | custom-call | flops 4294967296 | bytes 10485760 | tf_op jit(solution)/shard_map/attention_grads/pallas_call | solution.py:576
  503.1 11.8 %collective-permute-start.11 = (f32[4,32]{1,0:T(4,128)S(1)}, f32[4,32]{1,0:T(4,128)S(1)}, u32[]{:S(2)}, u32[]{:S(2)}) collective-permute-start(f32[4,32]{1,0:T(4,128)S(1)} %bitcast.161), channel_id=1, source_target_pairs={{0,8},{1,9},{2,10},{3,11},{4,12},{5,13},{6,14},{7,15},{8,16},{9,17... | collective-permute-start | bytes 1544 | tf_op jit(solution)/shard_map/ppermute | solution.py:76
  517.6 10.9 %attention_grads.2 = (bf16[4,4,32,2048]{3,2,1,0:T(8,128)(2,1)S(1)}, bf16[4,4,32,2048]{3,2,1,0:T(8,128)(2,1)S(1)}) custom-call(s32[3]{0:T(128)S(1)} %pad_add_fusion.4.place, bf16[1024,1024]{1,0:T(8,128)(2,1)S(1)} %copy-done.14, bf16[1024,1024]{1,0:T(8,128)(2,1)S(1)} %copy-done.13, bf16[1024,512]{1,0:T(8,128)(2,1)S(1)} %get-tuple-element.58.dq, ...), custom_call_target="tpu_custom_call" | custom-call | flops 4294967296 | bytes 10485760 | tf_op jit(solution)/shard_map/attention_grads/pallas_call | solution.py:576
  535.2 10.5 %collective-permute-done.28 = bf16[2,64,2048]{2,1,0:T(8,128)(2,1)S(1)} collective-permute-done((bf16[2,64,2048]{2,1,0:T(8,128)(2,1)S(1)}, bf16[2,64,2048]{2,1,0:T(8,128)(2,1)S(1)}, u32[]{:S(2)}, u32[]{:S(2)}) %collective-permute-start.28) | collective-permute-done | bytes 524320 | tf_op jit(solution)/shard_map/ppermute | solution.py:76
  545.9 10.2 %collective-permute-done.34 = bf16[2,64,2048]{2,1,0:T(8,128)(2,1)S(1)} collective-permute-done((bf16[2,64,2048]{2,1,0:T(8,128)(2,1)S(1)}, bf16[2,64,2048]{2,1,0:T(8,128)(2,1)S(1)}, u32[]{:S(2)}, u32[]{:S(2)}) %collective-permute-start.34) | collective-permute-done | bytes 524320 | tf_op jit(solution)/shard_map/ppermute | solution.py:76
  557.4 2.0 collective-permute-start.18
  560.9 22.3 %collective-permute-done.18 = bf16[2,4,32,2048]{3,2,1,0:T(8,128)(2,1)S(1)} collective-permute-done((bf16[2,4,32,2048]{3,2,1,0:T(8,128)(2,1)S(1)}, bf16[2,4,32,2048]{3,2,1,0:T(8,128)(2,1)S(1)}, u32[]{:S(2)}, u32[]{:S(2)}) %collective-permute-start.18) | collective-permute-done | bytes 1048608 | tf_op jit(solution)/shard_map/ppermute | solution.py:76
  587.5 10.0 %collective-permute-done.19 = bf16[1,4,32,2048]{3,2,1,0:T(8,128)(2,1)S(1)} collective-permute-done((bf16[1,4,32,2048]{3,2,1,0:T(8,128)(2,1)S(1)}, bf16[1,4,32,2048]{3,2,1,0:T(8,128)(2,1)S(1)}, u32[]{:S(2)}, u32[]{:S(2)}) %collective-permute-start.19) | collective-permute-done | bytes 524320 | tf_op jit(solution)/shard_map/ppermute | solution.py:76
  597.6 1.8 collective-permute-done.16
  606.8 1.9 reshape.307
  608.7 3.1 collective-permute-done.20
  611.8 8.8 %collective-permute-done.21 = bf16[2,32,2048]{2,1,0:T(8,128)(2,1)} collective-permute-done((bf16[2,32,2048]{2,1,0:T(8,128)(2,1)}, bf16[2,32,2048]{2,1,0:T(8,128)(2,1)}, u32[]{:S(2)}, u32[]{:S(2)}) %collective-permute-start.21) | collective-permute-done | bytes 262176 | tf_op jit(solution)/shard_map/ppermute | solution.py:76
  (277 shorter events, 70.5 us)
Async XLA Ops:
  0.7 9.2 %copy-start.45 = (bf16[32,3072]{1,0:T(8,128)(2,1)S(1)}, bf16[32,3072]{1,0:T(8,128)(2,1)}, u32[]{:S(2)}) copy-start(bf16[32,3072]{1,0:T(8,128)(2,1)} %param.18) | copy-start | bytes 589828
  0.7 10.0 %copy-start.37 = (bf16[1024,1024]{1,0:T(8,128)(2,1)S(1)}, bf16[1024,1024]{1,0:T(8,128)(2,1)}, u32[]{:S(2)}) copy-start(bf16[1024,1024]{1,0:T(8,128)(2,1)} %param.15) | copy-start | bytes 6291460
  162.6 46.2 %collective-permute-start = (bf16[1552,1024]{1,0:T(8,128)(2,1)}, bf16[1552,1024]{1,0:T(8,128)(2,1)}, u32[]{:S(2)}, u32[]{:S(2)}) collective-permute-start(bf16[1552,1024]{1,0:T(8,128)(2,1)} %pad_maximum_fusion), channel_id=1, source_target_pairs={{0,4},{1,5},{2,6},{3,7},{4,0},{5,1},{6,2},{7,3},{8,12},{9,13},{10,... | collective-permute-start | bytes 9535496 | tf_op jit(solution)/shard_map/ppermute | solution.py:76
  176.6 39.2 %collective-permute-start.1 = (bf16[1536,1024]{1,0:T(8,128)(2,1)}, bf16[1536,1024]{1,0:T(8,128)(2,1)}, u32[]{:S(2)}, u32[]{:S(2)}) collective-permute-start(bf16[1536,1024]{1,0:T(8,128)(2,1)} %convolution_convert_fusion), channel_id=1, source_target_pairs={{0,4},{1,5},{2,6},{3,7},{4,0},{5,1},{6,2},{7,3},{8,12},{9,13},{10,... | collective-permute-start | bytes 9437192 | tf_op jit(solution)/shard_map/ppermute | solution.py:76
  177.1 25.7 %collective-permute-start.3 = (bf16[1,4,2,32,2048]{4,3,2,1,0:T(8,128)(2,1)}, bf16[1,4,2,32,2048]{4,3,2,1,0:T(8,128)(2,1)}, u32[]{:S(2)}, u32[]{:S(2)}) collective-permute-start(bf16[1,4,2,32,2048]{4,3,2,1,0:T(8,128)(2,1)} %bitcast.24), channel_id=1, source_target_pairs={{0,2},{1,3},{2,0},{3,1},{4,6},{5,7},{6,4},{7,5},{8,10},{9,11},{10,... | collective-permute-start | bytes 3145736 | tf_op jit(solution)/shard_map/ppermute | solution.py:76
  179.1 27.2 %collective-permute-start.5 = (bf16[1,4,128,1024]{3,2,1,0:T(8,128)(2,1)}, bf16[1,4,128,1024]{3,2,1,0:T(8,128)(2,1)}, u32[]{:S(2)}, u32[]{:S(2)}) collective-permute-start(bf16[1,4,128,1024]{3,2,1,0:T(8,128)(2,1)} %bitcast.25), channel_id=1, source_target_pairs={{0,1},{1,0},{2,3},{3,2},{4,5},{5,4},{6,7},{7,6},{8,9},{9,8},{10,11... | collective-permute-start | bytes 3145736 | tf_op jit(solution)/shard_map/ppermute | solution.py:76
  204.5 58.3 %collective-permute-start.4 = (bf16[2,4,2,32,2048]{4,3,2,1,0:T(8,128)(2,1)S(1)}, bf16[2,4,2,32,2048]{4,3,2,1,0:T(8,128)(2,1)}, u32[]{:S(2)}, u32[]{:S(2)}) collective-permute-start(bf16[2,4,2,32,2048]{4,3,2,1,0:T(8,128)(2,1)S(1)} %pad_maximum_fusion.2.refs_5_), channel_id=1, source_target_pairs={{0,1},{1,0},{2,3},{3,2},{4,5},{5,4},{6,7},{7,6},{8,9},{9,8},{10,11... | collective-permute-start | bytes 6291464 | tf_op jit(solution)/shard_map/ppermute | solution.py:76
  208.1 54.8 %collective-permute-start.6 = (bf16[2,4,128,1024]{3,2,1,0:T(8,128)(2,1)S(1)}, bf16[2,4,128,1024]{3,2,1,0:T(8,128)(2,1)}, u32[]{:S(2)}, u32[]{:S(2)}) collective-permute-start(bf16[2,4,128,1024]{3,2,1,0:T(8,128)(2,1)S(1)} %pad_maximum_fusion.3.refs_7_), channel_id=1, source_target_pairs={{0,2},{1,3},{2,0},{3,1},{4,6},{5,7},{6,4},{7,5},{8,10},{9,11},{10,... | collective-permute-start | bytes 6291464 | tf_op jit(solution)/shard_map/ppermute | solution.py:76
  258.8 59.3 %collective-permute-start.23 = (bf16[2,4,64,2048]{3,2,1,0:T(8,128)(2,1)}, bf16[2,4,64,2048]{3,2,1,0:T(8,128)(2,1)}, u32[]{:S(2)}, u32[]{:S(2)}) collective-permute-start(bf16[2,4,64,2048]{3,2,1,0:T(8,128)(2,1)} %get-tuple-element.71), channel_id=1, source_target_pairs={{0,1},{1,0},{2,3},{3,2},{4,5},{5,4},{6,7},{7,6},{8,9},{9,8},{10,11... | collective-permute-start | bytes 6291464 | tf_op jit(solution)/shard_map/ppermute | solution.py:76
  260.3 61.6 %collective-permute-start.25 = (bf16[2,4,64,2048]{3,2,1,0:T(8,128)(2,1)}, bf16[2,4,64,2048]{3,2,1,0:T(8,128)(2,1)}, u32[]{:S(2)}, u32[]{:S(2)}) collective-permute-start(bf16[2,4,64,2048]{3,2,1,0:T(8,128)(2,1)} %get-tuple-element.73), channel_id=1, source_target_pairs={{0,2},{1,3},{2,0},{3,1},{4,6},{5,7},{6,4},{7,5},{8,10},{9,11},{10,... | collective-permute-start | bytes 6291464 | tf_op jit(solution)/shard_map/ppermute | solution.py:76
  306.0 46.3 %collective-permute-start.29 = (bf16[2,4,64,2048]{3,2,1,0:T(8,128)(2,1)}, bf16[2,4,64,2048]{3,2,1,0:T(8,128)(2,1)}, u32[]{:S(2)}, u32[]{:S(2)}) collective-permute-start(bf16[2,4,64,2048]{3,2,1,0:T(8,128)(2,1)} %get-tuple-element.75), channel_id=1, source_target_pairs={{0,1},{1,0},{2,3},{3,2},{4,5},{5,4},{6,7},{7,6},{8,9},{9,8},{10,11... | collective-permute-start | bytes 6291464 | tf_op jit(solution)/shard_map/ppermute | solution.py:76
  307.2 56.1 %collective-permute-start.31 = (bf16[2,4,64,2048]{3,2,1,0:T(8,128)(2,1)}, bf16[2,4,64,2048]{3,2,1,0:T(8,128)(2,1)S(1)}, u32[]{:S(2)}, u32[]{:S(2)}) collective-permute-start(bf16[2,4,64,2048]{3,2,1,0:T(8,128)(2,1)} %get-tuple-element.77), channel_id=1, source_target_pairs={{0,2},{1,3},{2,0},{3,1},{4,6},{5,7},{6,4},{7,5},{8,10},{9,11},{10,... | collective-permute-start | bytes 6291464 | tf_op jit(solution)/shard_map/ppermute | solution.py:76
  318.0 74.0 %collective-permute-start.7 = (bf16[2,768,1024]{2,1,0:T(8,128)(2,1)}, bf16[2,768,1024]{2,1,0:T(8,128)(2,1)S(1)}, u32[]{:S(2)}, u32[]{:S(2)}) collective-permute-start(bf16[2,768,1024]{2,1,0:T(8,128)(2,1)} %get-tuple-element.56), channel_id=1, source_target_pairs={{0,4},{1,5},{2,6},{3,7},{4,0},{5,1},{6,2},{7,3},{8,12},{9,13},{10,... | collective-permute-start | bytes 9437192 | tf_op jit(solution)/shard_map/ppermute | solution.py:76
  318.1 75.6 %collective-permute-start.2 = (bf16[2,768,1024]{2,1,0:T(8,128)(2,1)}, bf16[2,768,1024]{2,1,0:T(8,128)(2,1)S(1)}, u32[]{:S(2)}, u32[]{:S(2)}) collective-permute-start(bf16[2,768,1024]{2,1,0:T(8,128)(2,1)} %get-tuple-element.52), channel_id=1, source_target_pairs={{0,4},{1,5},{2,6},{3,7},{4,0},{5,1},{6,2},{7,3},{8,12},{9,13},{10,... | collective-permute-start | bytes 9437192 | tf_op jit(solution)/shard_map/ppermute | solution.py:76
  321.9 63.8 %collective-permute-start.24 = (bf16[1,4,64,2048]{3,2,1,0:T(8,128)(2,1)S(1)}, bf16[1,4,64,2048]{3,2,1,0:T(8,128)(2,1)S(1)}, u32[]{:S(2)}, u32[]{:S(2)}) collective-permute-start(bf16[1,4,64,2048]{3,2,1,0:T(8,128)(2,1)S(1)} %slice.256), channel_id=1, source_target_pairs={{0,2},{1,3},{2,0},{3,1},{4,6},{5,7},{6,4},{7,5},{8,10},{9,11},{10,... | collective-permute-start | bytes 3145736 | tf_op jit(solution)/shard_map/ppermute | solution.py:76
  322.0 30.6 %copy-start.34 = (bf16[2,4,64,2048]{3,2,1,0:T(8,128)(2,1)S(1)}, bf16[2,4,64,2048]{3,2,1,0:T(8,128)(2,1)}, u32[]{:S(2)}) copy-start(bf16[2,4,64,2048]{3,2,1,0:T(8,128)(2,1)} %get-tuple-element.74) | copy-start | bytes 6291460
  352.2 35.9 %collective-permute-start.26 = (bf16[1,4,64,2048]{3,2,1,0:T(8,128)(2,1)S(1)}, bf16[1,4,64,2048]{3,2,1,0:T(8,128)(2,1)S(1)}, u32[]{:S(2)}, u32[]{:S(2)}) collective-permute-start(bf16[1,4,64,2048]{3,2,1,0:T(8,128)(2,1)S(1)} %slice.258), channel_id=1, source_target_pairs={{0,1},{1,0},{2,3},{3,2},{4,5},{5,4},{6,7},{7,6},{8,9},{9,8},{10,11... | collective-permute-start | bytes 3145736 | tf_op jit(solution)/shard_map/ppermute | solution.py:76
  352.6 12.7 %copy-start.33 = (bf16[2,4,64,2048]{3,2,1,0:T(8,128)(2,1)S(1)}, bf16[2,4,64,2048]{3,2,1,0:T(8,128)(2,1)}, u32[]{:S(2)}) copy-start(bf16[2,4,64,2048]{3,2,1,0:T(8,128)(2,1)} %get-tuple-element.76) | copy-start | bytes 6291460
  363.2 90.1 %collective-permute-start.30 = (bf16[1,4,64,2048]{3,2,1,0:T(8,128)(2,1)}, bf16[1,4,64,2048]{3,2,1,0:T(8,128)(2,1)}, u32[]{:S(2)}, u32[]{:S(2)}) collective-permute-start(bf16[1,4,64,2048]{3,2,1,0:T(8,128)(2,1)} %slice.265), channel_id=1, source_target_pairs={{0,2},{1,3},{2,0},{3,1},{4,6},{5,7},{6,4},{7,5},{8,10},{9,11},{10,... | collective-permute-start | bytes 3145736 | tf_op jit(solution)/shard_map/ppermute | solution.py:76
  385.7 78.1 %collective-permute-start.32 = (bf16[1,4,64,2048]{3,2,1,0:T(8,128)(2,1)}, bf16[1,4,64,2048]{3,2,1,0:T(8,128)(2,1)}, u32[]{:S(2)}, u32[]{:S(2)}) collective-permute-start(bf16[1,4,64,2048]{3,2,1,0:T(8,128)(2,1)} %slice.267), channel_id=1, source_target_pairs={{0,1},{1,0},{2,3},{3,2},{4,5},{5,4},{6,7},{7,6},{8,9},{9,8},{10,11... | collective-permute-start | bytes 3145736 | tf_op jit(solution)/shard_map/ppermute | solution.py:76
  389.6 139.5 %collective-permute-start.27 = (bf16[2,2,64,2048]{3,2,1,0:T(8,128)(2,1)}, bf16[2,2,64,2048]{3,2,1,0:T(8,128)(2,1)}, u32[]{:S(2)}, u32[]{:S(2)}) collective-permute-start(bf16[2,2,64,2048]{3,2,1,0:T(8,128)(2,1)} %pad_maximum_fusion.5), channel_id=1, source_target_pairs={{0,16},{1,17},{2,18},{3,19},{4,20},{5,21},{6,22},{7,23},{8,24},{9,... | collective-permute-start | bytes 3145736 | tf_op jit(solution)/shard_map/ppermute | solution.py:76
  431.8 36.6 %copy-start.3 = (bf16[1024,512]{1,0:T(8,128)(2,1)}, bf16[1024,512]{1,0:T(8,128)(2,1)S(1)}, u32[]{:S(2)}) copy-start(bf16[1024,512]{1,0:T(8,128)(2,1)S(1)} %get-tuple-element.59.dq) | copy-start | bytes 3145732
  431.8 36.9 %copy-start.5 = (bf16[1024,512]{1,0:T(8,128)(2,1)}, bf16[1024,512]{1,0:T(8,128)(2,1)S(1)}, u32[]{:S(2)}) copy-start(bf16[1024,512]{1,0:T(8,128)(2,1)S(1)} %get-tuple-element.61.dk) | copy-start | bytes 3145732
  431.8 37.2 %copy-start.7 = (bf16[1024,512]{1,0:T(8,128)(2,1)}, bf16[1024,512]{1,0:T(8,128)(2,1)S(1)}, u32[]{:S(2)}) copy-start(bf16[1024,512]{1,0:T(8,128)(2,1)S(1)} %get-tuple-element.63.dv) | copy-start | bytes 3145732
  453.3 15.5 %copy-start.1 = (bf16[1024,512]{1,0:T(8,128)(2,1)}, bf16[1024,512]{1,0:T(8,128)(2,1)S(1)}, u32[]{:S(2)}) copy-start(bf16[1024,512]{1,0:T(8,128)(2,1)S(1)} %get-tuple-element.62.dv) | copy-start | bytes 3145732
  466.7 65.4 %collective-permute-start.33 = (bf16[2,2,64,2048]{3,2,0,1:T(8,128)(2,1)}, bf16[2,2,64,2048]{3,2,0,1:T(8,128)(2,1)}, u32[]{:S(2)}, u32[]{:S(2)}) collective-permute-start(bf16[2,2,64,2048]{3,2,0,1:T(8,128)(2,1)} %pad_maximum_fusion.4), channel_id=1, source_target_pairs={{0,16},{1,17},{2,18},{3,19},{4,20},{5,21},{6,22},{7,23},{8,24},{9,... | collective-permute-start | bytes 3145736 | tf_op jit(solution)/shard_map/ppermute | solution.py:76
  481.7 1.3 collective-permute-start.8
  483.0 7.4 %collective-permute-start.9 = (f32[2,4,4,32]{3,2,1,0:T(4,128)S(1)}, f32[2,4,4,32]{3,2,1,0:T(4,128)S(1)}, u32[]{:S(2)}, u32[]{:S(2)}) collective-permute-start(f32[2,4,4,32]{3,2,1,0:T(4,128)S(1)} %dynamic-slice_bitcast_fusion.2), channel_id=1, source_target_pairs={{0,2},{1,3},{2,0},{3,1},{4,6},{5,7},{6,4},{7,5},{8,10},{9,11},{10,... | collective-permute-start | bytes 12296 | tf_op jit(solution)/shard_map/ppermute | solution.py:76
  490.5 12.6 %collective-permute-start.10 = (f32[1,4,4,32]{3,2,1,0:T(4,128)S(1)}, f32[1,4,4,32]{3,2,1,0:T(4,128)S(1)}, u32[]{:S(2)}, u32[]{:S(2)}) collective-permute-start(f32[1,4,4,32]{3,2,1,0:T(4,128)S(1)} %constant_dynamic-slice_fusion.4), channel_id=1, source_target_pairs={{0,1},{1,0},{2,3},{3,2},{4,5},{5,4},{6,7},{7,6},{8,9},{9,8},{10,11... | collective-permute-start | bytes 6152 | tf_op jit(solution)/shard_map/ppermute | solution.py:76
  492.2 25.4 %copy-start.2 = (bf16[1024,512]{1,0:T(8,128)(2,1)S(1)}, bf16[1024,512]{1,0:T(8,128)(2,1)}, u32[]{:S(2)}) copy-start(bf16[1024,512]{1,0:T(8,128)(2,1)} %copy-done.1) | copy-start | bytes 3145732
  492.2 25.4 %copy-start.9 = (bf16[1024,512]{1,0:T(8,128)(2,1)S(1)}, bf16[1024,512]{1,0:T(8,128)(2,1)}, u32[]{:S(2)}) copy-start(bf16[1024,512]{1,0:T(8,128)(2,1)} %get-tuple-element.94.branch) | copy-start | bytes 3145732
  503.1 25.4 %collective-permute-start.11 = (f32[4,32]{1,0:T(4,128)S(1)}, f32[4,32]{1,0:T(4,128)S(1)}, u32[]{:S(2)}, u32[]{:S(2)}) collective-permute-start(f32[4,32]{1,0:T(4,128)S(1)} %bitcast.161), channel_id=1, source_target_pairs={{0,8},{1,9},{2,10},{3,11},{4,12},{5,13},{6,14},{7,15},{8,16},{9,17... | collective-permute-start | bytes 1544 | tf_op jit(solution)/shard_map/ppermute | solution.py:76
  515.0 13.7 %collective-permute-start.12 = (f32[4,32]{1,0:T(4,128)S(1)}, f32[4,32]{1,0:T(4,128)S(1)}, u32[]{:S(2)}, u32[]{:S(2)}) collective-permute-start(f32[4,32]{1,0:T(4,128)S(1)} %bitcast.160), channel_id=1, source_target_pairs={{0,16},{1,17},{2,18},{3,19},{4,20},{5,21},{6,22},{7,23},{8,24},{9,... | collective-permute-start | bytes 1544 | tf_op jit(solution)/shard_map/ppermute | solution.py:76
  516.5 12.7 %collective-permute-start.13 = (f32[4,32]{1,0:T(4,128)S(1)}, f32[4,32]{1,0:T(4,128)S(1)}, u32[]{:S(2)}, u32[]{:S(2)}) collective-permute-start(f32[4,32]{1,0:T(4,128)S(1)} %bitcast.159), channel_id=1, source_target_pairs={{0,24},{1,25},{2,26},{3,27},{4,28},{5,29},{6,30},{7,31},{8,0},{9,1... | collective-permute-start | bytes 1544 | tf_op jit(solution)/shard_map/ppermute | solution.py:76
  517.6 11.6 %copy-start.20 = (bf16[4,1,64,2048]{3,2,1,0:T(8,128)(2,1)S(1)}, bf16[4,1,64,2048]{3,2,1,0:T(8,128)(2,1)}, u32[]{:S(2)}) copy-start(bf16[4,1,64,2048]{3,2,1,0:T(8,128)(2,1)} %copy-done.19) | copy-start | bytes 3145732
  517.6 11.6 %copy-start.22 = (bf16[4,1,64,2048]{3,2,1,0:T(8,128)(2,1)S(1)}, bf16[4,1,64,2048]{3,2,1,0:T(8,128)(2,1)}, u32[]{:S(2)}) copy-start(bf16[4,1,64,2048]{3,2,1,0:T(8,128)(2,1)} %copy-done.21) | copy-start | bytes 3145732
  528.6 27.9 %collective-permute-start.17 = (bf16[4,4,32,2048]{3,2,1,0:T(8,128)(2,1)S(1)}, bf16[4,4,32,2048]{3,2,1,0:T(8,128)(2,1)S(1)}, u32[]{:S(2)}, u32[]{:S(2)}) collective-permute-start(bf16[4,4,32,2048]{3,2,1,0:T(8,128)(2,1)S(1)} %get-tuple-element.69), channel_id=1, source_target_pairs={{0,4},{1,5},{2,6},{3,7},{4,0},{5,1},{6,2},{7,3},{8,12},{9,13},{10,... | collective-permute-start | bytes 6291464 | tf_op jit(solution)/shard_map/ppermute | solution.py:76
  528.7 30.8 %collective-permute-start.14 = (bf16[4,4,32,2048]{3,2,1,0:T(8,128)(2,1)S(1)}, bf16[4,4,32,2048]{3,2,1,0:T(8,128)(2,1)S(1)}, u32[]{:S(2)}, u32[]{:S(2)}) collective-permute-start(bf16[4,4,32,2048]{3,2,1,0:T(8,128)(2,1)S(1)} %get-tuple-element.67), channel_id=1, source_target_pairs={{0,4},{1,5},{2,6},{3,7},{4,0},{5,1},{6,2},{7,3},{8,12},{9,13},{10,... | collective-permute-start | bytes 6291464 | tf_op jit(solution)/shard_map/ppermute | solution.py:76
  530.9 14.8 %collective-permute-start.28 = (bf16[2,64,2048]{2,1,0:T(8,128)(2,1)S(1)}, bf16[2,64,2048]{2,1,0:T(8,128)(2,1)S(1)}, u32[]{:S(2)}, u32[]{:S(2)}) collective-permute-start(bf16[2,64,2048]{2,1,0:T(8,128)(2,1)S(1)} %slice_bitcast_fusion.2), channel_id=1, source_target_pairs={{0,8},{1,9},{2,10},{3,11},{4,12},{5,13},{6,14},{7,15},{8,0},{9,1},... | collective-permute-start | bytes 1572872 | tf_op jit(solution)/shard_map/ppermute | solution.py:76
  533.7 22.4 %collective-permute-start.34 = (bf16[2,64,2048]{2,1,0:T(8,128)(2,1)S(1)}, bf16[2,64,2048]{2,1,0:T(8,128)(2,1)S(1)}, u32[]{:S(2)}, u32[]{:S(2)}) collective-permute-start(bf16[2,64,2048]{2,1,0:T(8,128)(2,1)S(1)} %slice_bitcast_fusion), channel_id=1, source_target_pairs={{0,8},{1,9},{2,10},{3,11},{4,12},{5,13},{6,14},{7,15},{8,0},{9,1},... | collective-permute-start | bytes 1572872 | tf_op jit(solution)/shard_map/ppermute | solution.py:76
  556.4 48.1 %collective-permute-start.35 = (f32[2,32,2048]{2,1,0:T(8,128)S(1)}, f32[2,32,2048]{2,1,0:T(8,128)S(1)}, u32[]{:S(2)}, u32[]{:S(2)}) collective-permute-start(f32[2,32,2048]{2,1,0:T(8,128)S(1)} %dynamic-slice_bitcast_fusion), channel_id=1, source_target_pairs={{0,4},{1,5},{2,6},{3,7},{4,0},{5,1},{6,2},{7,3},{8,12},{9,13},{10,... | collective-permute-start | bytes 1572872 | tf_op jit(solution)/shard_map/ppermute | solution.py:76
  557.4 25.9 %collective-permute-start.18 = (bf16[2,4,32,2048]{3,2,1,0:T(8,128)(2,1)S(1)}, bf16[2,4,32,2048]{3,2,1,0:T(8,128)(2,1)S(1)}, u32[]{:S(2)}, u32[]{:S(2)}) collective-permute-start(bf16[2,4,32,2048]{3,2,1,0:T(8,128)(2,1)S(1)} %slice.244), channel_id=1, source_target_pairs={{0,2},{1,3},{2,0},{3,1},{4,6},{5,7},{6,4},{7,5},{8,10},{9,11},{10,... | collective-permute-start | bytes 3145736 | tf_op jit(solution)/shard_map/ppermute | solution.py:76
  560.3 25.3 %collective-permute-start.15 = (bf16[2,4,32,2048]{3,2,1,0:T(8,128)(2,1)S(1)}, bf16[2,4,32,2048]{3,2,1,0:T(8,128)(2,1)S(1)}, u32[]{:S(2)}, u32[]{:S(2)}) collective-permute-start(bf16[2,4,32,2048]{3,2,1,0:T(8,128)(2,1)S(1)} %slice.239), channel_id=1, source_target_pairs={{0,1},{1,0},{2,3},{3,2},{4,5},{5,4},{6,7},{7,6},{8,9},{9,8},{10,11... | collective-permute-start | bytes 3145736 | tf_op jit(solution)/shard_map/ppermute | solution.py:76
  583.7 13.8 %collective-permute-start.19 = (bf16[1,4,32,2048]{3,2,1,0:T(8,128)(2,1)S(1)}, bf16[1,4,32,2048]{3,2,1,0:T(8,128)(2,1)S(1)}, u32[]{:S(2)}, u32[]{:S(2)}) collective-permute-start(bf16[1,4,32,2048]{3,2,1,0:T(8,128)(2,1)S(1)} %slice.246), channel_id=1, source_target_pairs={{0,1},{1,0},{2,3},{3,2},{4,5},{5,4},{6,7},{7,6},{8,9},{9,8},{10,11... | collective-permute-start | bytes 1572872 | tf_op jit(solution)/shard_map/ppermute | solution.py:76
  586.1 13.3 %collective-permute-start.16 = (bf16[1,4,32,2048]{3,2,1,0:T(8,128)(2,1)S(1)}, bf16[1,4,32,2048]{3,2,1,0:T(8,128)(2,1)S(1)}, u32[]{:S(2)}, u32[]{:S(2)}) collective-permute-start(bf16[1,4,32,2048]{3,2,1,0:T(8,128)(2,1)S(1)} %slice.241), channel_id=1, source_target_pairs={{0,2},{1,3},{2,0},{3,1},{4,6},{5,7},{6,4},{7,5},{8,10},{9,11},{10,... | collective-permute-start | bytes 1572872 | tf_op jit(solution)/shard_map/ppermute | solution.py:76
  600.4 11.4 %collective-permute-start.20 = (bf16[2,32,2048]{2,1,0:T(8,128)(2,1)}, bf16[2,32,2048]{2,1,0:T(8,128)(2,1)S(1)}, u32[]{:S(2)}, u32[]{:S(2)}) collective-permute-start(bf16[2,32,2048]{2,1,0:T(8,128)(2,1)} %get-tuple-element.102), channel_id=1, source_target_pairs={{0,8},{1,9},{2,10},{3,11},{4,12},{5,13},{6,14},{7,15},{8,16},{9,17... | collective-permute-start | bytes 786440 | tf_op jit(solution)/shard_map/ppermute | solution.py:76
  601.4 19.2 %collective-permute-start.21 = (bf16[2,32,2048]{2,1,0:T(8,128)(2,1)}, bf16[2,32,2048]{2,1,0:T(8,128)(2,1)}, u32[]{:S(2)}, u32[]{:S(2)}) collective-permute-start(bf16[2,32,2048]{2,1,0:T(8,128)(2,1)} %get-tuple-element.104), channel_id=1, source_target_pairs={{0,16},{1,17},{2,18},{3,19},{4,20},{5,21},{6,22},{7,23},{8,24},{9,... | collective-permute-start | bytes 786440 | tf_op jit(solution)/shard_map/ppermute | solution.py:76
  602.9 17.7 %collective-permute-start.22 = (bf16[2,32,2048]{2,1,0:T(8,128)(2,1)}, bf16[2,32,2048]{2,1,0:T(8,128)(2,1)}, u32[]{:S(2)}, u32[]{:S(2)}) collective-permute-start(bf16[2,32,2048]{2,1,0:T(8,128)(2,1)} %get-tuple-element.103), channel_id=1, source_target_pairs={{0,24},{1,25},{2,26},{3,27},{4,28},{5,29},{6,30},{7,31},{8,0},{9,1... | collective-permute-start | bytes 786440 | tf_op jit(solution)/shard_map/ppermute | solution.py:76
  (45 other events, 213.8 us)

commit v2 on v1

--- a/solution.py
+++ b/solution.py
@@ -319,23 +319,32 @@
     tokens,
     mine,
     own_in,
-    their_in,
     own_out,
     seg_row,
     seg_col,
+    slot_row,
+    grad_out,
+    note,
     out_qkv,
     out_attn,
     out_params,
     first_in,
     first_out,
-    column_in,
-    column_out,
+    held_in,
+    held_out,
+    sorted_other,
+    grad_other,
+    noted,
     normed,
     projected,
     mixed,
     stats,
+    hidden,
+    sorted_rows,
+    grad_sorted,
     weights,
     bias,
+    normed_two,
     send_sems,
     recv_sems,
     local_sems,
@@ -364,17 +373,31 @@
 
     own = local_start(mine, weights.at[zed, core, flat])
     column = [remote.start(mine, weights.at[zed, core, flat], device) for device in others]
-    crossed = [
-        remote.start(their_in.at[0], first_in.at[zed, core, flat], sibling),
-        remote.start(their_in.at[1], column_in.at[zed, core], sibling),
-    ]
-    blocks = [
-        local_start(own_in.at[0], first_in.at[zed, core, flat]),
-        local_start(own_out.at[0], first_out.at[zed, flat]),
-        local_start(own_in.at[1], column_in.at[zed, core]),
-        local_start(own_out.at[1], column_out.at[zed]),
-    ]
-
+    column_in, column_out = held_in.at[0], held_out.at[0]
+    targets = (first_in.at[zed, core, flat], column_in.at[zed, core])
+    cut = own_in.shape[2] // (2 * nz)
+    crossed, blocks = [remote.start(note, noted, sibling)], []
+    for e in range(EXPERTS):
+        for z_of in range(nz):
+            target = targets[e].at[:, pl.ds(z_of * cut, cut)]
+            theirs, ours = [
+                own_in.at[e, :, pl.ds(pl.multiple_of((2 * z_of + which) * cut, cut), cut)]
+                for which in (1 - core, core)
+            ]
+            crossed.append(remote.start(theirs, target, sibling))
+            blocks.append(local_start(ours, target))
+    blocks.append(local_start(own_out.at[0], first_out.at[zed, flat]))
+    blocks.append(local_start(own_out.at[1], column_out.at[zed]))
+
+    def sort_rows(source, target):
+        @pl.loop(0, target.shape[0] // TILE)
+        def _(t):
+            place = pl.ds(pl.multiple_of(t * TILE, TILE), TILE)
+            slot = lax.broadcasted_iota(jnp.int32, (TILE, rows), 0) + t * TILE
+            chosen = (slot == slot_row[0:1, :]).astype(F32).astype(BF16)
+            target[place, :] = dot(chosen, source[...]).astype(BF16)
+
+    sort_rows(grad_out, grad_sorted)
     for i in range(rows // TILE):
         span = (i + 1) * TILE
         place = slice(i * TILE, span)
@@ -393,6 +416,7 @@
 
     own.wait()
     wait_in(column)
+    exchanged = [remote.start(grad_sorted, grad_other, sibling)]
     near = [tuple(reversed(moves.orders[n]))[0] for n in range(2)]
     far = [moves.orders[n][0] for n in range(2)]
     hop_near = [send_weights(n, flat, hops[near[n]]) for n in range(2)]
@@ -487,107 +511,626 @@
     def _(pair):
         attend_pair(pair)
 
+    wait_in(second_column)
+    second_near = [
+        remote.start(held.at[0], held.at[1], hops[near[n]])
+        for n, held in enumerate((held_in, held_out))
+    ]
+
+    gain_two, shift_two = turned[2:3, :], turned[3:4, :]
+
+    @pl.loop(0, rows // TILE)
+    def _(t):
+        place = pl.ds(pl.multiple_of(t * TILE, TILE), TILE)
+        matrix = weights[:, :, :, :, pl.ds(3 * wide, wide)].reshape(whole, wide)
+        total = tokens[place, :].astype(F32) + dot(mixed[place, :], matrix)
+        hidden[place, :] = total
+        scaled, _ = norm_parts(total)
+        normed_two[place, :] = (scaled * gain_two + shift_two).astype(BF16)
+
+    sort_rows(normed_two, sorted_rows)
+    exchanged.append(remote.start(sorted_rows, sorted_other, sibling))
     wait_in(first_far)
     wait_in(first_last)
-    wait_in(second_column)
+    wait_in(second_near)
+    wait_in(exchanged)
     for one in remote.made:
         one.wait_send()
     for one in writes:
         one.wait()
 
 
-def forward_pass(moves, tokens, mine, own_in, their_in, own_out, seg_row, seg_col):
+def forward_pass(moves, tokens, mine, own_in, own_out, seg_row, seg_col, slot_row, grad_out, note):
     nz, nf = moves.nz, moves.nf
     rows, wide = tokens.shape
-    deep, half = own_in.shape[1:]
+    deep, half = own_in.shape[1], own_in.shape[2] // 2
     part = own_out.shape[1]
+    capacity = 3 * rows // 4
     anywhere = pl.BlockSpec(memory_space=pl.ANY)
     inside = pl.BlockSpec(memory_space=pltpu.VMEM)
     shape = jax.ShapeDtypeStruct
-    remote = 3 * (nz - 1) + 2 + 2 * 3 + 7 + 2 * (nz - 1) + 2 * 3
+    remote = 7 * (nz - 1) + 2 * nz + 24
     return pl.pallas_call(
         functools.partial(forward_kernel, moves),
-        in_specs=[inside] * 7,
-        out_specs=[anywhere] * 7 + [inside] * 4,
+        in_specs=[inside] * 9,
+        out_specs=[anywhere] * 10 + [inside] * 7,
         out_shape=[
             shape((nz, 2, nf, deep, 3 * wide), BF16),
             shape((nz, 2, nf, deep, wide), BF16),
             shape((nz, 2, nf, deep, BLOCK), BF16),
             shape((nz, 2, nf, deep, half), BF16),
             shape((nz, nf, part, wide), BF16),
-            shape((nz, 2, deep, half), BF16),
-            shape((nz, part, wide), BF16),
+            shape((2, nz, 2, deep, half), BF16),
+            shape((2, nz, part, wide), BF16),
+            shape((EXPERTS * capacity, wide), BF16),
+            shape((EXPERTS * capacity, wide), BF16),
+            shape(note.shape, BF16),
             shape((rows, wide), BF16),
             shape((rows, 3 * wide), BF16),
             shape((rows, wide), BF16),
             shape((rows, BLOCK), F32),
+            shape((rows, wide), F32),
+            shape((EXPERTS * capacity, wide), BF16),
+            shape((EXPERTS * capacity, wide), BF16),
         ],
         scratch_shapes=[
             pltpu.VMEM((nz, 2, nf, deep, 4 * wide + BLOCK), BF16),
             pltpu.VMEM((rows, rows), F32),
+            pltpu.VMEM((rows, wide), BF16),
             pltpu.SemaphoreType.DMA((remote,)),
             pltpu.SemaphoreType.DMA((remote,)),
-            pltpu.SemaphoreType.DMA((8,)),
+            pltpu.SemaphoreType.DMA((2 * nz + 6,)),
         ],
         compiler_params=pltpu.CompilerParams(
-            collective_id=0, has_side_effects=True, vmem_limit_bytes=56 * MIB
+            collective_id=0, has_side_effects=True, vmem_limit_bytes=60 * MIB
         ),
         cost_estimate=pl.CostEstimate(
             flops=10 * rows * wide * wide, bytes_accessed=80 * wide * wide, transcendentals=0
         ),
         name="forward_pass",
-    )(tokens, mine, own_in, their_in, own_out, seg_row, seg_col)
-
-
-def attention_grads_kernel(
-    moves, stream, deep, share, place, normed, mixed, dq, dk, dv, branch, near, far, low, sems
+    )(tokens, mine, own_in, own_out, seg_row, seg_col, slot_row, grad_out, note)
+
+
+def sum_low(*values):
+    total = values[0].astype(F32)
+    for one in values[1:]:
+        total = total + one.astype(F32)
+    return total
+
+
+def backward_kernel(
+    moves,
+    deep,
+    projected,
+    whole_qkv,
+    whole_attn,
+    hidden,
+    normed_out,
+    tokens_in,
+    grad_out,
+    rows_first,
+    rows_second,
+    other_first,
+    other_second,
+    keep_first_in,
+    keep_first_out,
+    arrived_in,
+    arrived_out,
+    keep_in,
+    sent_in,
+    keep_out,
+    sent_out,
+    stats,
+    seg_row,
+    seg_col,
+    slot_col,
+    mixed,
+    params,
+    block_out,
+    grad_tokens,
+    share_in,
+    share_out,
+    share_qkv,
+    share_attn,
+    share_vectors,
+    got_in,
+    got_out,
+    hop_in,
+    hop_out,
+    first_hop_in,
+    first_hop_out,
+    landed,
+    wide_low,
+    wide_f32,
+    grad_projected,
+    grad_mixed,
+    branch,
+    normed,
+    tokens,
+    key_sums,
+    value_sums,
+    low,
+    cross,
+    got_q,
+    hop_q,
+    z_q,
+    up_q,
+    vec,
+    cross_vec,
+    got_vec,
+    hop_vec,
+    z_vec,
+    up,
+    spare,
+    up_first,
+    z_first,
+    z_second,
+    final,
+    send_sems,
+    recv_sems,
+    local_sems,
 ):
-    zed, core, flat = place[0], place[1], place[2]
-    for d in range(normed.shape[1] // TILE):
-        rows = pl.ds(d * TILE, TILE)
-        turned = normed[:, rows].T
-        for n, part in enumerate((dq, dk, dv)):
-            low[rows, pl.ds(n * share, share)] = dot(turned, part[...]).astype(BF16)
-        low[rows, pl.ds(3 * share, share)] = dot(mixed[:, rows].T, branch[...]).astype(BF16)
-    begun = []
-    for number, offset in enumerate(moves.relative(stream)):
-        for k in range(moves.nz):
-            z_of = lax.rem(zed + k, moves.nz)
-            for other in range(2):
-                owner = core if other == 0 else 1 - core
-                start = ((z_of * 2 + owner) * moves.nf + (flat ^ offset)) * deep
-                rows = pl.ds(pl.multiple_of(start, deep), deep)
-                target = (far if other else near).at[number, k]
-                begun.append(
-                    pltpu.make_async_copy(low.at[rows], target, sems.at[len(begun)])
+    nz, nf = moves.nz, moves.nf
+    dp, flat = lax.axis_index("dp"), lax.axis_index("fsdp")
+    zed, core = dp // 2, lax.rem(dp, 2)
+    rows, wide = tokens.shape
+    half = wide // 2
+    sibling = (zed * 2 + 1 - core, flat)
+    others = [((zed ^ k) * 2 + core, flat) for k in range(1, nz)]
+    hops = {bit: (dp, flat ^ bit) for bit in moves.orders[0]}
+
+    barrier = pltpu.get_barrier_semaphore()
+    for device in [sibling] + others + list(hops.values()):
+        pl.semaphore_signal(barrier, inc=1, device_id=device, device_id_type=pl.DeviceIdType.MESH)
+    pl.semaphore_wait(barrier, 1 + len(others) + len(hops))
+
+    remote = Copies(send_sems, recv_sems)
+    local = []
+
+    def local_start(source, target):
+        one = pltpu.make_async_copy(source, target, local_sems.at[len(local)])
+        one.start()
+        local.append(one)
+        return one
+
+    def load(*pairs):
+        for one in [local_start(source, target) for source, target in pairs]:
+            one.wait()
+
+    capacity = rows_first.shape[1]
+    crossed_rows = [
+        remote.start(other_first.at[1], grad_projected.at[pl.ds(0, capacity), pl.ds(2 * wide, wide)], sibling),
+        remote.start(other_second.at[1], grad_mixed.at[pl.ds(0, capacity)], sibling),
+    ]
+    crossed_late = [
+        remote.start(other.at[0], landed.at[e], sibling)
+        for e, other in enumerate((other_first, other_second))
+    ]
+    row_loads = [
+        local_start(source.at[1], grad_projected.at[pl.ds(0, capacity), pl.ds(e * wide, wide)])
+        for e, source in enumerate((rows_first, rows_second))
+    ]
+    loaded = local_start(projected, wide_low)
+    phase_loads = [
+        local_start(hidden, wide_f32),
+        local_start(whole_attn, normed),
+        local_start(grad_out, tokens),
+    ]
+    one_way = [moves.orders[n][0] for n in range(2)]
+    other_way = [moves.orders[n][1] for n in range(2)]
+    keep_first, arrived = (keep_first_in, keep_first_out), (arrived_in, arrived_out)
+    first_hop = (first_hop_in, first_hop_out)
+
+    def first_next(n):
+        load((keep_first[n].at[1], up_first.at[n]), (arrived[n].at[1], spare.at[0]))
+
+        @pl.loop(0, nz)
+        def _(k):
+            up_first[n, k] = sum_low(up_first[n, k], spare[0, k]).astype(BF16)
+
+        return remote.start(up_first.at[n], first_hop[n], hops[other_way[n]])
+
+    first_hops = [first_next(n) for n in range(2)]
+    keep, sent = (keep_in, keep_out), (sent_in, sent_out)
+    got, hop = (got_in, got_out), (hop_in, hop_out)
+    second_got = {}
+    for index in (1, 0):
+        for n in range(2):
+            second_got[n, index] = remote.start(
+                sent[n].at[index], got[n].at[index], hops[one_way[n]]
+            )
+
+    for one in row_loads + phase_loads:
+        one.wait()
+    wait_in(crossed_rows)
+
+    def add_rows(target, source, columns):
+        @pl.loop(0, capacity // TILE)
+        def _(t):
+            place = pl.ds(pl.multiple_of(t * TILE, TILE), TILE)
+            total = sum_low(grad_projected[place, target], source[place, columns])
+            grad_projected[place, target] = total.astype(BF16)
+
+    first_columns, second_columns = pl.ds(0, wide), pl.ds(wide, wide)
+    add_rows(first_columns, grad_projected, pl.ds(2 * wide, wide))
+    add_rows(second_columns, grad_mixed, first_columns)
+
+    def tokens_order(place):
+        total = jnp.zeros((TILE, wide), F32)
+        for e in range(EXPERTS):
+            slot = lax.broadcasted_iota(jnp.int32, (TILE, capacity), 1) + e * capacity
+            chosen = (slot == slot_col[place, 0:1]).astype(F32).astype(BF16)
+            total = total + dot(chosen, grad_projected[pl.ds(0, capacity), pl.ds(e * wide, wide)])
+        return total
+
+    turned = params[...].astype(F32).T
+    gain_one, gain_two = turned[0:1, :], turned[2:3, :]
+    empty = jnp.zeros((1, wide), F32)
+
+    def second_norm_tile(t, sums):
+        place = pl.ds(pl.multiple_of(t * TILE, TILE), TILE)
+        grad = tokens_order(place)
+        scaled, inverse = norm_parts(wide_f32[place, :])
+        total = tokens[place, :].astype(F32) + norm_back(grad, scaled, inverse, gain_two)
+        wide_f32[place, :] = total
+        low_total = total.astype(BF16)
+        branch[place, :] = low_total
+        grad_mixed[place, :] = dot_nt(low_total, normed[...]).astype(BF16)
+        return (
+            sums[0] + jnp.sum(grad * scaled, axis=0, keepdims=True),
+            sums[1] + jnp.sum(grad, axis=0, keepdims=True),
+        )
+
+    sums_two = lax.fori_loop(0, rows // TILE, second_norm_tile, (empty, empty))
+    load((wide_f32, grad_tokens), (normed_out, normed), (tokens_in, tokens))
+
+    def first_sums(n):
+        load(
+            (keep_first[n].at[0], up_first.at[n]),
+            (arrived[n].at[0], spare.at[0]),
+            (first_hop[n], spare.at[1]),
+        )
+
+        @pl.loop(0, nz)
+        def _(k):
+            total = sum_low(up_first[n, k], spare[0, k], spare[1, k])
+            up_first[n, k] = total.astype(BF16)
+
+        return [
+            remote.start(up_first.at[n, k], z_first.at[n, k - 1], others[k - 1])
+            for k in range(1, nz)
+        ]
+
+    wait_in(first_hops)
+    for one in first_hops:
+        one.wait_send()
+    first_z = first_sums(0) + first_sums(1)
+
+    lane = lax.broadcasted_iota(jnp.int32, (1, BLOCK), 1)
+    row = lax.broadcasted_iota(jnp.int32, (BLOCK, 1), 0)
+    for i in range(rows // TILE):
+        span = (i + 1) * TILE
+        place = slice(i * TILE, span)
+        query = lax.broadcasted_iota(jnp.int32, (span, TILE), 1) + i * TILE
+        key = lax.broadcasted_iota(jnp.int32, (span, TILE), 0)
+        same = seg_col[:span, 0:1] == seg_row[0:1, place]
+        wide_f32[:span, place] = jnp.where(same & (key <= query), 0.0, MASKED)
+    loaded.wait()
+    pairs = wide // BLOCK
+
+    def attend_pair(pair):
+        columns = [
+            pl.ds(pl.multiple_of(n * wide + pair * BLOCK, BLOCK), BLOCK) for n in range(3)
+        ]
+        key_sums[...] = jnp.zeros_like(key_sums)
+        value_sums[...] = jnp.zeros_like(value_sums)
+        keys_turned = wide_low[:, columns[1]].T
+        for i in range(rows // TILE):
+            span = (i + 1) * TILE
+            place = slice(i * TILE, span)
+            query = wide_low[place, columns[0]] * jnp.asarray(HEAD_DIM**-0.5, BF16)
+            grad = grad_mixed[place, columns[0]]
+            turned = jnp.zeros((BLOCK, TILE), F32)
+            for side in range(2):
+                ours = (lane // HEAD_DIM) == side
+                part = jnp.where(ours, query, jnp.zeros_like(query))
+                grad_part = jnp.where(ours, grad, jnp.zeros_like(grad))
+                level = stats[pl.ds(2 * pair + side, 1), place]
+                scores = dot_nt(wide_low[:span, columns[1]], part) + wide_f32[:span, place]
+                attend = jnp.exp(scores - level)
+                grad_attend = dot_nt(wide_low[:span, columns[2]], grad_part)
+                inner = jnp.sum(attend * grad_attend, axis=0, keepdims=True)
+                grad_scores = (attend * (grad_attend - inner)).astype(BF16)
+                key_sums[:span, :] += dot(grad_scores, part)
+                value_sums[:span, :] += dot(attend.astype(BF16), grad_part)
+                turned = jnp.where(
+                    (row // HEAD_DIM) == side, dot(keys_turned[:, :span], grad_scores), turned
                 )
-    for one in begun:
-        one.start()
-    for one in begun:
+            grad_projected[place, columns[0]] = (turned.T * HEAD_DIM**-0.5).astype(BF16)
+        grad_projected[:, columns[1]] = key_sums[...].astype(BF16)
+        grad_projected[:, columns[2]] = value_sums[...].astype(BF16)
+
+    def attend_pairs(start, stop):
+        @pl.loop(start, stop)
+        def _(pair):
+            attend_pair(pair)
+
+    def weight_grads(n):
+        @pl.loop(0, nz)
+        def _(z_of):
+            span = 2 * nf * deep
+            place = pl.ds(pl.multiple_of(z_of * span, span), span)
+            turned = normed[:, place].T
+            mixed_turned = mixed[:, place].T
+            for part in range(4):
+                if part < 3:
+                    columns = pl.ds(part * wide + n * half, half)
+                    made = dot(turned, grad_projected[:, columns])
+                else:
+                    made = dot(mixed_turned, branch[:, pl.ds(n * half, half)])
+                made = made.astype(BF16).reshape(2, nf, deep, half)
+                low[n, z_of, :, :, :, pl.ds(part * half, half)] = made
+
+    def cross_start(source, target):
+        return remote.start(source.at[:, 1 - core], target, sibling)
+
+    def cross_add(source, target):
+        @pl.loop(0, nz)
+        def _(k):
+            source[k, core] = sum_low(source[k, core], target[k]).astype(source.dtype)
+
+    def hop_start(source, target, n):
+        bits = one_way[n], other_way[n]
+        return [
+            remote.start(
+                source.at[:, core, flat ^ bits[0] ^ (bits[1] * index)],
+                target.at[index],
+                hops[bits[0]],
+            )
+            for index in (1, 0)
+        ]
+
+    def hop_next(source, arrived, target, landing, n):
+        @pl.loop(0, nz)
+        def _(k):
+            mine = source[k, core, flat ^ other_way[n]]
+            target[k] = sum_low(mine, arrived[1, k]).astype(target.dtype)
+
+        return remote.start(target, landing, hops[other_way[n]])
+
+    def z_start(source, arrived, landing, z_landing):
+        @pl.loop(0, nz)
+        def _(k):
+            total = sum_low(source[k, core, flat], arrived[0, k], landing[k])
+            source[k, core, flat] = total.astype(source.dtype)
+
+        return [
+            remote.start(source.at[zed ^ k, core, flat], z_landing.at[k - 1], others[k - 1])
+            for k in range(1, nz)
+        ]
+
+    def z_total(source, z_landing):
+        return sum_low(source[zed, core, flat], *[z_landing[k] for k in range(nz - 1)])
+
+    def second_next(n):
+        load((keep[n].at[1], up.at[n]), (got[n].at[1], spare.at[0]))
+
+        @pl.loop(0, nz)
+        def _(k):
+            up[n, k] = sum_low(up[n, k], spare[0, k]).astype(BF16)
+
+        return remote.start(up.at[n], hop[n], hops[other_way[n]])
+
+    def second_z(n):
+        load((keep[n].at[0], up.at[n]), (got[n].at[0], spare.at[0]), (hop[n], spare.at[1]))
+
+        @pl.loop(0, nz)
+        def _(k):
+            up[n, k] = sum_low(up[n, k], spare[0, k], spare[1, k]).astype(BF16)
+
+        return [
+            remote.start(up.at[n, k], z_second.at[n, k - 1], others[k - 1]) for k in range(1, nz)
+        ]
+
+    def finish_expert(e, own, z_landing, writes):
+        for n in range(2):
+            final[2 * e + n] = sum_low(own[n], *[z_landing[n, k] for k in range(nz - 1)])
+        cut = share_in.shape[2] // (2 * nz)
+        for z_of in range(nz):
+            place = pl.ds(pl.multiple_of((z_of * 2 + core) * cut, cut), cut)
+            target = share_in.at[e, :, place]
+            source = final.at[2 * e]
+            there = source.at[pl.ds(pl.multiple_of((1 - core) * deep, deep), deep)]
+            here = source.at[pl.ds(pl.multiple_of(core * deep, deep), deep)]
+            writes.append(remote.start(there.at[:, pl.ds(z_of * cut, cut)], target, sibling))
+            stored.append(local_start(here.at[:, pl.ds(z_of * cut, cut)], target))
+        part = share_out.shape[1] // 2
+        for index in range(2):
+            stored.append(
+                local_start(
+                    final.at[2 * e + 1, :, pl.ds(index * wide, wide)],
+                    share_out.at[e, pl.ds(index * part, part)],
+                )
+            )
+
+    def put_share(n, total):
+        for part in range(4):
+            piece = total[:, part * half : (part + 1) * half]
+            if part < 3:
+                share_qkv[:, pl.ds(part * wide + n * half, half)] = piece
+            else:
+                share_attn[:, pl.ds(n * half, half)] = piece
+
+    stored = []
+    attend_pairs(0, pairs // 2)
+    weight_grads(0)
+    crossed = [cross_start(low.at[0], cross.at[0])]
+    wait_in([second_got[n, 1] for n in range(2)])
+    second_hop = [second_next(n) for n in range(2)]
+    attend_pairs(pairs // 2, 3 * pairs // 4)
+    wait_in(crossed)
+    cross_add(low.at[0], cross.at[0])
+    hops_a = hop_start(low.at[0], got_q.at[0], 0)
+    attend_pairs(3 * pairs // 4, pairs)
+    reload = local_start(whole_qkv, wide_low)
+    restore = local_start(grad_tokens, wide_f32)
+    weight_grads(1)
+    crossed = [cross_start(low.at[1], cross.at[1])]
+    wait_in(hops_a)
+    next_a = hop_next(low.at[0], got_q.at[0], up_q.at[0], hop_q.at[0], 0)
+    wait_in([second_got[n, 0] for n in range(2)] + second_hop)
+    for one in second_hop:
+        one.wait_send()
+    second_zs = second_z(0) + second_z(1)
+    wait_in(crossed)
+    cross_add(low.at[1], cross.at[1])
+    hops_b = hop_start(low.at[1], got_q.at[1], 1)
+
+    reload.wait()
+    restore.wait()
+    def norm_tile(t, sums):
+        place = pl.ds(pl.multiple_of(t * TILE, TILE), TILE)
+        grad = dot_nt(grad_projected[place, :], wide_low[...])
+        scaled, inverse = norm_parts(tokens[place, :].astype(F32))
+        wide_f32[place, :] += norm_back(grad, scaled, inverse, gain_one)
+        return (
+            sums[0] + jnp.sum(grad * scaled, axis=0, keepdims=True),
+            sums[1] + jnp.sum(grad, axis=0, keepdims=True),
+        )
+
+    sums = lax.fori_loop(0, rows // TILE, norm_tile, (empty, empty))
+    result = local_start(wide_f32, grad_tokens)
+    index = lax.broadcasted_iota(jnp.int32, (BLOCK, 1), 0)
+    stacked = jnp.zeros((BLOCK, wide), F32)
+    for n, one in enumerate(sums + sums_two):
+        stacked = jnp.where(index == n, one, stacked)
+    vec[...] = stacked.T.reshape(nz, 2, nf, deep, BLOCK)
+    crossed = [cross_start(vec, cross_vec)]
+
+    wait_in([next_a])
+    z_a = z_start(low.at[0], got_q.at[0], hop_q.at[0], z_q.at[0])
+    wait_in(crossed)
+    cross_add(vec, cross_vec)
+    hops_v = hop_start(vec, got_vec, 0)
+    writes = []
+    wait_in(first_z)
+    finish_expert(0, [up_first[n, 0] for n in range(2)], z_first, writes)
+    wait_in(hops_v)
+    next_v = hop_next(vec, got_vec, hop_vec.at[1], hop_vec.at[0], 0)
+    wait_in(hops_b)
+    next_b = hop_next(low.at[1], got_q.at[1], up_q.at[1], hop_q.at[1], 1)
+    wait_in([next_v])
+    z_v = z_start(vec, got_vec, hop_vec.at[0], z_vec)
+    wait_in([next_b])
+    z_b = z_start(low.at[1], got_q.at[1], hop_q.at[1], z_q.at[1])
+
+    result.wait()
+    wait_in(crossed_late)
+    load(
+        (hidden, wide_f32),
+        *[
+            (source.at[0], grad_projected.at[pl.ds(0, capacity), pl.ds(e * wide, wide)])
+            for e, source in enumerate((rows_first, rows_second))
+        ],
+        (landed.at[0], grad_projected.at[pl.ds(0, capacity), pl.ds(2 * wide, wide)]),
+        (landed.at[1], grad_mixed.at[pl.ds(0, capacity)]),
+    )
+    add_rows(first_columns, grad_projected, pl.ds(2 * wide, wide))
+    add_rows(second_columns, grad_mixed, first_columns)
+
+    @pl.loop(0, rows // TILE)
+    def _(t):
+        place = pl.ds(pl.multiple_of(t * TILE, TILE), TILE)
+        branch[place, :] = (wide_f32[place, :] + tokens_order(place)).astype(BF16)
+
+    stored.append(local_start(branch, block_out))
+    wait_in(z_a)
+    put_share(0, z_total(low.at[0], z_q.at[0]))
+    wait_in(z_v)
+    share_vectors[...] = z_total(vec, z_vec)
+    wait_in(second_zs)
+    finish_expert(1, [up[n, 0] for n in range(2)], z_second, writes)
+    wait_in(z_b)
+    put_share(1, z_total(low.at[1], z_q.at[1]))
+    wait_in(writes)
+    for one in remote.made:
+        if not any(one is other for other in second_hop + first_hops):
+            one.wait_send()
+    for one in stored:
         one.wait()
 
 
-def attention_grads(moves, stream, place, normed, mixed, dq, dk, dv, branch, deep):
-    rows, wide = normed.shape
-    share = dq.shape[1]
+def backward_pass(moves, deep, big, row_parts, sums, stats, seg, slot_col, mixed, params):
+    nz, nf = moves.nz, moves.nf
+    rows, wide = mixed.shape
+    half = wide // 2
+    block = sums[0].shape[2:]
+    capacity = row_parts[0].shape[1]
     anywhere = pl.BlockSpec(memory_space=pl.ANY)
     inside = pl.BlockSpec(memory_space=pltpu.VMEM)
-    piece = jax.ShapeDtypeStruct((moves.nf, moves.nz, deep, 4 * share), BF16)
+    shape = jax.ShapeDtypeStruct
+    landing = (2, nz) + block
+    remote = 24 + 7 * (nz - 1) + 2 * nz
+    inputs = list(big) + list(row_parts) + list(sums)
     return pl.pallas_call(
-        functools.partial(attention_grads_kernel, moves, stream, deep, share),
-        in_specs=[pl.BlockSpec(memory_space=pltpu.SMEM)] + [inside] * 6,
-        out_specs=[anywhere] * 2,
-        out_shape=[piece, piece],
+        functools.partial(backward_kernel, moves, deep),
+        in_specs=[anywhere] * len(inputs) + [inside] * 6,
+        out_specs=[anywhere] * 4 + [inside] * 3 + [anywhere] * 7,
+        out_shape=[
+            shape((rows, wide), BF16),
+            shape((rows, wide), F32),
+            shape((EXPERTS, deep, 2 * block[1]), F32),
+            shape((EXPERTS, block[0] * block[1] // wide, wide), F32),
+            shape((deep, 3 * wide), F32),
+            shape((deep, wide), F32),
+            shape((deep, BLOCK), F32),
+            shape(landing, BF16),
+            shape(landing, BF16),
+            shape(landing[1:], BF16),
+            shape(landing[1:], BF16),
+            shape(landing[1:], BF16),
+            shape(landing[1:], BF16),
+            shape((EXPERTS, capacity, wide), BF16),
+        ],
         scratch_shapes=[
-            pltpu.VMEM((wide, 4 * share), BF16),
-            pltpu.SemaphoreType.DMA((2 * moves.nz * moves.nf,)),
+            pltpu.VMEM((rows, 3 * wide), BF16),
+            pltpu.VMEM((rows, rows), F32),
+            pltpu.VMEM((rows, 3 * wide), BF16),
+            pltpu.VMEM((rows, wide), BF16),
+            pltpu.VMEM((rows, wide), BF16),
+            pltpu.VMEM((rows, wide), BF16),
+            pltpu.VMEM((rows, wide), BF16),
+            pltpu.VMEM((rows, BLOCK), F32),
+            pltpu.VMEM((rows, BLOCK), F32),
+            pltpu.VMEM((2, nz, 2, nf, deep, 4 * half), BF16),
+            pltpu.VMEM((2, nz, nf, deep, 4 * half), BF16),
+            pltpu.VMEM((2, 2, nz, deep, 4 * half), BF16),
+            pltpu.VMEM((2, nz, deep, 4 * half), BF16),
+            pltpu.VMEM((2, nz - 1, deep, 4 * half), BF16),
+            pltpu.VMEM((2, nz, deep, 4 * half), BF16),
+            pltpu.VMEM((nz, 2, nf, deep, BLOCK), F32),
+            pltpu.VMEM((nz, nf, deep, BLOCK), F32),
+            pltpu.VMEM((2, nz, deep, BLOCK), F32),
+            pltpu.VMEM((2, nz, deep, BLOCK), F32),
+            pltpu.VMEM((nz - 1, deep, BLOCK), F32),
+            pltpu.VMEM((2, nz) + block, BF16),
+            pltpu.VMEM((2, nz) + block, BF16),
+            pltpu.VMEM((2, nz) + block, BF16),
+            pltpu.VMEM((2, nz - 1) + block, BF16),
+            pltpu.VMEM((2, nz - 1) + block, BF16),
+            pltpu.VMEM((4,) + block, F32),
+            pltpu.SemaphoreType.DMA((remote,)),
+            pltpu.SemaphoreType.DMA((remote,)),
+            pltpu.SemaphoreType.DMA((44 + 2 * nz,)),
         ],
-        compiler_params=pltpu.CompilerParams(vmem_limit_bytes=40 * MIB),
+        compiler_params=pltpu.CompilerParams(
+            collective_id=1, has_side_effects=True, vmem_limit_bytes=62 * MIB
+        ),
         cost_estimate=pl.CostEstimate(
-            flops=8 * rows * wide * share, bytes_accessed=20 * wide * share, transcendentals=0
+            flops=30 * rows * wide * wide, bytes_accessed=80 * wide * wide, transcendentals=0
         ),
-        name="attention_grads",
-    )(place, normed, mixed, dq, dk, dv, branch)
+        name="backward_pass",
+    )(*inputs, stats, *seg, slot_col, mixed, params)
 
 
 def gelu_both(value):
@@ -835,47 +1378,6 @@
     return [[all_in[e], all_out[e]] for e in range(EXPERTS)]
 
 
-def reduce_expert(moves, pieces):
-    sum_in = moves.reduce_flat(pieces[0], pieces[1], 0)
-    sum_out = moves.reduce_flat(pieces[2], pieces[3], 1)
-    sums = moves.reduce_z_pair(jnp.stack([sum_in, sum_out], axis=1))
-    wide = sums.shape[2] // 2
-    return sums[0], jnp.concatenate([sums[1, :, :wide], sums[1, :, wide:]], axis=0)
-
-
-def join_cores(moves, shares_in, core, deep):
-    both = jnp.stack(shares_in)
-    both = both.reshape(EXPERTS, 2, deep, both.shape[2])
-    ours = lax.dynamic_index_in_dim(both, core, 1, False)
-    theirs = moves.core(lax.dynamic_index_in_dim(both, 1 - core, 1, False))
-    low_core = jnp.where(core == 0, ours, theirs).reshape(EXPERTS, deep, moves.nz, 1, -1)
-    high_core = jnp.where(core == 0, theirs, ours).reshape(EXPERTS, deep, moves.nz, 1, -1)
-    return jnp.concatenate([low_core, high_core], axis=3).reshape(EXPERTS, deep, -1)
-
-
-def reduce_vectors(moves, vectors, place, deep):
-    zed, core, flat = place
-    held = vectors.reshape(4, moves.nz, 2, moves.nf, deep)
-    held = lax.dynamic_index_in_dim(held, core, 2, False) + moves.core(
-        lax.dynamic_index_in_dim(held, 1 - core, 2, False)
-    )
-    held = jnp.moveaxis(held, 2, 0)
-    bit = moves.nf // 2
-    while bit:
-        pair = held.reshape((2, bit) + held.shape[1:])
-        side = lax.rem(flat // bit, 2)
-        held = lax.dynamic_index_in_dim(pair, side, 0, False) + moves.flat(
-            lax.dynamic_index_in_dim(pair, 1 - side, 0, False), bit
-        )
-        bit //= 2
-    held = held[0]
-    total = lax.dynamic_index_in_dim(held, zed, 1, False)
-    for k in range(1, moves.nz):
-        other = lax.dynamic_index_in_dim(held, lax.rem(zed + k, moves.nz), 1, False)
-        total = total + moves.along(other, k)
-    return total
-
-
 def local(
     nd,
     nf,
@@ -905,160 +1407,72 @@
     flat = lax.axis_index("fsdp")
     place = jnp.stack([zed, core, flat]).astype(jnp.int32)
 
-    params = jnp.stack([ln1_gain, ln1_bias, ln2_gain, ln2_bias], axis=1)
-    params = jnp.pad(params, ((0, 0), (0, BLOCK - 4)))
-    mine = jnp.concatenate([w_qkv, w_attn_out, params], axis=1)
-    tokens_wide = tokens.astype(F32)
     positions = jnp.arange(rows, dtype=jnp.int32)
     bounds = jnp.cumsum(seq_lengths[0])
     segment = jnp.sum((positions[:, None] >= bounds[None, :]).astype(jnp.int32), axis=1)
     seg_row = jnp.broadcast_to(segment[None, :], (8, rows))
     seg_col = jnp.broadcast_to(segment[:, None], (rows, BLOCK))
-    if staged:
-        by_core = w_expert_in.reshape(EXPERTS, deep, nz, 2, hidden // (2 * nz))
-        own_in, their_in = [
-            lax.dynamic_index_in_dim(by_core, which, 3, False).reshape(EXPERTS, deep, half_hidden)
-            for which in (core, 1 - core)
-        ]
-        outs = forward_pass(moves, tokens, mine, own_in, their_in, w_expert_out, seg_row, seg_col)
-        whole_qkv, whole_attn, params, first_in = [
-            one.reshape(-1, one.shape[-1]) for one in outs[:4]
-        ]
-        first_out = outs[4].reshape(half_hidden, width)
-        column_in, column_out, normed_one, projected, mixed, stats = outs[5:]
-        held = [moves.gather_first(column_in, 0), moves.gather_first(column_out, 1)]
-        last = [moves.gather_last(held[0], 0), moves.gather_last(held[1], 1)]
-        expert_weights = [[first_in, first_out], [held[0], last[0], held[1], last[1]]]
-    else:
-        whole = lax.all_gather(mine, AXES, axis=0, tiled=True)
-        whole_qkv, whole_attn = whole[:, : 3 * width], whole[:, 3 * width : 4 * width]
-        params = whole[:, 4 * width :]
-        expert_weights = gather_experts_whole(w_expert_in, w_expert_out, core, nz)
-    gain_one, bias_one, gain_two, bias_two = [
-        params[:, n].astype(F32)[None, :] for n in range(4)
-    ]
-    scaled_one, inverse_one = norm_parts(tokens_wide)
-    if not staged:
-        normed_one = (scaled_one * gain_one + bias_one).astype(BF16)
-        projected = dot(normed_one, whole_qkv).astype(BF16)
-        mixed, stats = attention_forward(projected, seg_row, seg_col, 0, width // BLOCK)
-
     routed = expert_ids[:, 0]
-    second = (routed == 1).astype(jnp.int32)
-    rank_second = jnp.cumsum(second) - second
-    second_n = jnp.sum(second)
-    rank = jnp.where(routed == 1, rank_second, positions - rank_second)
+    rank_second = jnp.cumsum(routed) - routed
+    second_n = jnp.sum(routed)
     capacity = 3 * rows // 4
-    slots = jnp.arange(capacity, dtype=jnp.int32)[:, None]
-    spread = [
-        ((rank[None, :] == slots) & (routed[None, :] == e)).astype(BF16) for e in range(EXPERTS)
-    ]
+    slot = jnp.where(routed == 1, capacity + rank_second, positions - rank_second)
     split = jnp.stack([rows - second_n, second_n]).astype(jnp.int32)
     split = (split + BLOCK - 1) // BLOCK
-    spread_all = jnp.concatenate(spread, axis=0)
-    grad_sorted = dot(spread_all, grad_out).astype(BF16)
-    grad_sorted = after(grad_sorted, projected)
-    note = jnp.broadcast_to(split[:, None].astype(BF16), (2, width))
+
+    params = jnp.stack([ln1_gain, ln1_bias, ln2_gain, ln2_bias], axis=1)
+    params = jnp.pad(params, ((0, 0), (0, BLOCK - 4)))
+    mine = jnp.concatenate([w_qkv, w_attn_out, params], axis=1)
+    arguments = (tokens, grad_out, mine, w_expert_in, w_expert_out)
+    if staged:
+        return staged_block(moves, arguments, seg_row, seg_col, slot, split, (zed, core, flat))
+    return plain_block(moves, arguments, seg_row, seg_col, slot, split, (zed, core, flat))
+
+
+def staged_block(moves, arguments, seg_row, seg_col, slot, split, place):
+    tokens, grad_out, mine, w_expert_in, w_expert_out = arguments
+    rows, width = tokens.shape
+    deep, hidden = w_expert_in.shape[1:]
+    half_hidden = hidden // 2
+    capacity = 3 * rows // 4
+    zed, core, flat = place
+    note = jnp.broadcast_to(split[:, None].astype(BF16), (2, BLOCK))
     note = jnp.pad(note, ((0, 14), (0, 0)))
-    noted = moves.core(jnp.concatenate([grad_sorted, note], axis=0))
-    split_other = noted[2 * capacity : 2 * capacity + 2, 0].astype(jnp.int32)
-    grad_sorted = grad_sorted.reshape(EXPERTS, capacity, width)
-    grad_sorted_other = noted[: 2 * capacity].reshape(EXPERTS, capacity, width)
-
-    pairs = width // BLOCK
-    parts = [(0, pairs // 2), (pairs // 2, pairs // 2)]
-    stats_turned = stats.T
-    hidden_one = tokens_wide + dot(mixed, whole_attn)
-    scaled_two, inverse_two = norm_parts(hidden_one)
-    normed_two = (scaled_two * gain_two + bias_two).astype(BF16)
-
-    sorted_rows = dot(spread_all, normed_two).astype(BF16)
-    sorted_other = moves.core(sorted_rows).reshape(EXPERTS, capacity, width)
-    sorted_rows = sorted_rows.reshape(EXPERTS, capacity, width)
-    results, grad_pieces = [], []
+    slot_row = jnp.broadcast_to(slot[None, :], (8, rows))
+    slot_col = jnp.broadcast_to(slot[:, None], (rows, BLOCK))
+    outs = forward_pass(
+        moves, tokens, mine, w_expert_in, w_expert_out, seg_row, seg_col, slot_row, grad_out, note
+    )
+    whole_qkv, whole_attn, params, first_in = [one.reshape(-1, one.shape[-1]) for one in outs[:4]]
+    first_out = outs[4].reshape(half_hidden, width)
+    held = outs[5:7]
+    sorted_other, grad_other, noted = outs[7:10]
+    normed_one, projected, mixed, stats, hidden_one, sorted_rows, grad_sorted = outs[10:]
+    last = [moves.gather_last(held[0], 0), moves.gather_last(held[1], 1)]
+    weights = [[first_in, first_out], [held[0], last[0], held[1], last[1]]]
+    by_expert = lambda value: value.reshape(EXPERTS, capacity, width)
+    row_inputs = [by_expert(one) for one in (sorted_rows, sorted_other, grad_sorted, grad_other)]
+    split_other = noted[:2, 0].astype(jnp.int32)
+    made = []
     for e in range(EXPERTS):
         table = jnp.stack([zed, flat, split[e], split_other[e]]).astype(jnp.int32)
-        outs = expert_block(
-            moves if staged else None,
-            e,
-            table,
-            [sorted_rows, sorted_other, grad_sorted, grad_sorted_other],
-            list(expert_weights[e]),
-            deep,
-            half_hidden,
-        )
-        results.append(add_low(outs[0], moves.core(outs[1])))
-        grad_pieces.append(outs[2:])
-    both = jnp.concatenate(results, axis=1)
-    grad_normed_two = dot_tn(spread_all, both[1])
-    branch = dot_tn(spread_all, both[0])
-    block_result = (hidden_one + branch).astype(BF16)
-
-    grad_gain_two = jnp.sum(grad_normed_two * scaled_two, axis=0)
-    grad_bias_two = jnp.sum(grad_normed_two, axis=0)
-    grad_hidden = grad_out.astype(F32) + norm_back(
-        grad_normed_two, scaled_two, inverse_two, gain_two
+        made.append(expert_block(moves, e, table, row_inputs, weights[e], deep, half_hidden))
+        if e == 0:
+            arrived = [moves.flat(made[0][3 + 2 * n], moves.orders[n][0]) for n in range(2)]
+    results = backward_pass(
+        moves,
+        deep,
+        [projected, whole_qkv, whole_attn, hidden_one, normed_one, tokens, grad_out],
+        [made[0][0], made[1][0], made[0][1], made[1][1]],
+        [made[0][2], made[0][4]] + arrived + list(made[1][2:]),
+        stats.T,
+        [seg_row, seg_col],
+        slot_col,
+        mixed,
+        params,
     )
-    grad_branch = grad_hidden.astype(BF16)
-    grad_mixed = dot_nt(grad_branch, whole_attn).astype(BF16)
-
-    grad_parts, shares = [], []
-    for n, (first, count) in enumerate(parts):
-        trio = attention_backward(
-            projected, grad_mixed, stats_turned, seg_row, seg_col, first, count
-        )
-        grad_parts.append(trio)
-        if staged:
-            near, far = attention_grads(
-                moves,
-                n,
-                place,
-                normed_one,
-                mixed,
-                *trio,
-                grad_branch[:, first * BLOCK : (first + count) * BLOCK],
-                deep,
-            )
-            pieces = add_low(near, moves.core(far))
-            shares.append(moves.reduce_flat(pieces[: nf // 2], pieces[nf // 2 :], n))
-    grad_projected = jnp.concatenate(
-        [grad_parts[n][m] for m in range(3) for n in range(2)], axis=1
-    )
-    grad_normed_one = dot_nt(grad_projected, whole_qkv)
-    grad_gain_one = jnp.sum(grad_normed_one * scaled_one, axis=0)
-    grad_bias_one = jnp.sum(grad_normed_one, axis=0)
-    grad_input = grad_hidden + norm_back(grad_normed_one, scaled_one, inverse_one, gain_one)
-    vectors = jnp.stack([grad_gain_one, grad_bias_one, grad_gain_two, grad_bias_two])
-
-    if staged:
-        sums = [reduce_expert(moves, pieces) for pieces in grad_pieces]
-        share_in = join_cores(moves, [one[0] for one in sums], core, deep)
-        share_out = jnp.stack([one[1] for one in sums])
-        vectors = reduce_vectors(moves, vectors, (zed, core, flat), deep)
-        share = moves.reduce_z(jnp.stack(shares, axis=1)).reshape(2, deep, 4, half)
-        share = jnp.moveaxis(share, 0, 2).reshape(deep, 4 * width)
-        share_qkv, share_attn = share[:, : 3 * width], share[:, 3 * width :]
-    else:
-        share_qkv = lax.psum_scatter(
-            dot_tn(normed_one, grad_projected), AXES, scatter_dimension=0, tiled=True
-        )
-        share_attn = lax.psum_scatter(
-            dot_tn(mixed, grad_branch), AXES, scatter_dimension=0, tiled=True
-        )
-        vectors = lax.psum_scatter(vectors, AXES, scatter_dimension=1, tiled=True)
-        full_in = jnp.stack([pieces[0] for pieces in grad_pieces])
-        full_out = jnp.stack([pieces[1] for pieces in grad_pieces])
-        full_in = full_in.reshape(EXPERTS, width, nz, 1, -1).astype(F32)
-        full_out = full_out.reshape(EXPERTS, nz, 1, -1, width).astype(F32)
-        chosen = jnp.arange(2) == core
-        full_in = jnp.where(chosen[None, None, None, :, None], full_in, 0.0)
-        full_out = jnp.where(chosen[None, None, :, None, None], full_out, 0.0)
-        share_in = lax.psum_scatter(
-            full_in.reshape(EXPERTS, width, hidden), AXES, scatter_dimension=1, tiled=True
-        )
-        share_out = lax.psum_scatter(
-            full_out.reshape(EXPERTS, hidden, width), AXES, scatter_dimension=1, tiled=True
-        )
+    block_result, grad_input, share_in, share_out, share_qkv, share_attn, vectors = results[:7]
+    vectors = vectors[:, :4].T
     return (
         block_result,
         grad_input,
@@ -1070,6 +1484,88 @@
         vectors[3],
         share_in,
         share_out,
+    )
+
+
+def plain_block(moves, arguments, seg_row, seg_col, slot, split, place):
+    tokens, grad_out, mine, w_expert_in, w_expert_out = arguments
+    rows, width = tokens.shape
+    hidden = w_expert_in.shape[2]
+    deep = mine.shape[0]
+    nz = moves.nz
+    zed, core, flat = place
+    capacity = 3 * rows // 4
+    whole = lax.all_gather(mine, AXES, axis=0, tiled=True)
+    whole_qkv, whole_attn = whole[:, : 3 * width], whole[:, 3 * width : 4 * width]
+    params = whole[:, 4 * width :]
+    expert_weights = gather_experts_whole(w_expert_in, w_expert_out, core, nz)
+    gain_one, bias_one, gain_two, bias_two = [
+        params[:, n].astype(F32)[None, :] for n in range(4)
+    ]
+    tokens_wide = tokens.astype(F32)
+    scaled_one, inverse_one = norm_parts(tokens_wide)
+    normed_one = (scaled_one * gain_one + bias_one).astype(BF16)
+    projected = dot(normed_one, whole_qkv).astype(BF16)
+    mixed, stats = attention_forward(projected, seg_row, seg_col, 0, width // BLOCK)
+    hidden_one = tokens_wide + dot(mixed, whole_attn)
+    scaled_two, inverse_two = norm_parts(hidden_one)
+    normed_two = (scaled_two * gain_two + bias_two).astype(BF16)
+    slots = jnp.arange(EXPERTS * capacity, dtype=jnp.int32)[:, None]
+    spread = (slots == slot[None, :]).astype(BF16)
+    by_expert = lambda value: value.reshape(EXPERTS, capacity, width)
+    row_inputs = []
+    for value in (normed_two, grad_out):
+        ordered = dot(spread, value).astype(BF16)
+        row_inputs += [by_expert(ordered), by_expert(moves.core(ordered))]
+    split_other = moves.core(jnp.broadcast_to(split[:, None], (2, BLOCK)))[:, 0]
+    results, grad_pieces = [], []
+    for e in range(EXPERTS):
+        table = jnp.stack([zed, flat, split[e], split_other[e]]).astype(jnp.int32)
+        outs = expert_block(None, e, table, row_inputs, expert_weights[e], deep, hidden // 2)
+        results.append(add_low(outs[0], moves.core(outs[1])))
+        grad_pieces.append(outs[2:])
+    both = jnp.concatenate(results, axis=1)
+    grad_normed_two = dot_tn(spread, both[1])
+    block_result = (hidden_one + dot_tn(spread, both[0])).astype(BF16)
+    grad_hidden = grad_out.astype(F32) + norm_back(
+        grad_normed_two, scaled_two, inverse_two, gain_two
+    )
+    grad_branch = grad_hidden.astype(BF16)
+    grad_mixed = dot_nt(grad_branch, whole_attn).astype(BF16)
+    trio = attention_backward(
+        projected, grad_mixed, stats.T, seg_row, seg_col, 0, width // BLOCK
+    )
+    grad_projected = jnp.concatenate(trio, axis=1)
+    grad_normed_one = dot_nt(grad_projected, whole_qkv)
+    grad_input = grad_hidden + norm_back(grad_normed_one, scaled_one, inverse_one, gain_one)
+    vectors = jnp.stack(
+        [
+            jnp.sum(grad_normed_one * scaled_one, axis=0),
+            jnp.sum(grad_normed_one, axis=0),
+            jnp.sum(grad_normed_two * scaled_two, axis=0),
+            jnp.sum(grad_normed_two, axis=0),
+        ]
+    )
+    own = lambda value, dim: lax.psum_scatter(value, AXES, scatter_dimension=dim, tiled=True)
+    vectors = own(vectors, 1)
+    full_in = jnp.stack([pieces[0] for pieces in grad_pieces])
+    full_out = jnp.stack([pieces[1] for pieces in grad_pieces])
+    full_in = full_in.reshape(EXPERTS, width, nz, 1, -1).astype(F32)
+    full_out = full_out.reshape(EXPERTS, nz, 1, -1, width).astype(F32)
+    chosen = jnp.arange(2) == core
+    full_in = jnp.where(chosen[None, None, None, :, None], full_in, 0.0)
+    full_out = jnp.where(chosen[None, None, :, None, None], full_out, 0.0)
+    return (
+        block_result,
+        grad_input,
+        vectors[0],
+        vectors[1],
+        own(dot_tn(normed_one, grad_projected), 0),
+        own(dot_tn(mixed, grad_branch), 0),
+        vectors[2],
+        vectors[3],
+        own(full_in.reshape(EXPERTS, width, hidden), 1),
+        own(full_out.reshape(EXPERTS, hidden, width), 1),
     )
 
 

time: 636 us -> 517 us (0.81)
  Pallas kernels: 290 us -> 475 us
  waiting for transfers between devices: 146 us -> 0.01 us
  starting transfers between devices: 51.6 us -> 4.26 us
  other arithmetic: 58.9 us -> 11.6 us
  matrix products: 41.7 us -> 0 us
  local copies, waits for them, and re-layouts: 34.3 us -> 17.7 us
    pallas_call x4 -> x1, Pallas kernels: 64.3 us -> 222 us  [backward_pass(): pl.pallas_call(functools.partial(backward_kernel, moves, deep), in_specs=...]
    ppermute x36 -> x4, waiting for transfers between devices: 146 us -> 0.01 us  [send(): return lax.ppermute(value, AXES, pairs)]
    ppermute x36 -> x4, starting transfers between devices: 51.6 us -> 4.26 us  [send(): return lax.ppermute(value, AXES, pairs)]
    dot_general x7 -> x0, matrix products: 41.7 us -> none  [the longest x3 15.6 us: dot(): return jnp.dot(a, b, preferred_element_type=F32)]
    pallas_call x1, Pallas kernels: 139 us -> 166 us  [forward_pass(): pl.pallas_call(functools.partial(forward_kernel, moves), in_specs=[inside...]
    convert_element_type x16 -> x2, other arithmetic: 25 us -> 1.4 us  [the longest x1 0.73 us: staged_block(): note = jnp.broadcast_to(split[:, None].astype(BF16), (2, BLOCK))]
    slice x17 -> x4, local copies, waits for them, and re-layouts: 10.7 us -> 1.91 us  [the longest x2 1.1 us: staged_block(): table = jnp.stack([zed, flat, split[e], split_other[e]]).astype(jnp.int32)]
    concatenate x5 -> x0, other arithmetic: 8.69 us -> none  [the longest x2 4.27 us: local(): noted = moves.core(jnp.concatenate([grad_sorted, note], axis=0))]
  transfers between devices with their start and end apart: 36 -> 4, of which waited for: 13 -> 0; matrix products, arithmetic and copies ran while one was open for 17% -> 1% of each run, Pallas kernels for 24% -> 17%
where the time goes in v2:
time: 517 us; the launch traced here: 510 us
  Pallas kernels  475 us (92%)
  local copies, waits for them, and re-layouts  17.7 us (3%)
  other arithmetic  11.6 us (2%)
    pallas_call x1, Pallas kernels, backward_pass(): pl.pallas_call(functools.partial(backward_kernel, moves, deep), in_specs=...  222 us
    pallas_call x1, Pallas kernels, forward_pass(): pl.pallas_call(functools.partial(forward_kernel, moves), in_specs=[inside...  166 us
    pallas_call x2, Pallas kernels, expert_block(): pl.pallas_call(functools.partial(expert_kernel, (moves, deep, chunk, chun...  86.7 us
  transfers between devices with their start and end apart: 4, of which 0 were waited for; matrix products, arithmetic and copies ran while one was open for 1% of the time, Pallas kernels for 17%

profile of v2, /device:TPU:0, one launch (start us, length us, event | category | flops | bytes accessed | tf_op | source)
XLA Modules:
  0.0 509.8 jit_solution(16243097986032800715)
XLA Ops:
  0.6 1.0 reduce-window.20
  1.6 0.1 slice.43
  1.7 0.1 slice_reduce_fusion.4
  1.8 0.8 subtract_select_fusion
  2.6 1.3 compare_select_fusion
  3.9 0.8 reduce-window.19
  4.8 0.1 convert_reduce_fusion
  4.8 0.7 pad_maximum_fusion
  5.6 0.1 copy.34
  6.3 0.7 fusion.2
  7.1 1.7 fusion.1.mine
  8.7 0.7 pad.12.note
  9.4 0.6 broadcast_in_dim.12.slot_row
  10.0 1.0 broadcast_in_dim.11.seg_col
  11.0 0.6 broadcast_in_dim.10.seg_row
  11.6 165.8 %forward_pass.1 = (bf16[4,2,4,32,3072]{4,3,2,1,0:T(8,128)(2,1)}, bf16[4,2,4,32,1024]{4,3,2,1,0:T(8,128)(2,1)}, bf16[4,2,4,32,128]{4,3,2,1,0:T(8,128)(2,1)}, bf16...) custom-call(bf16[1024,1024]{1,0:T(8,128)(2,1)} %tokens_in.1, ...), custom_call_target="tpu_custom_call" | custom-call | flops 10737418240 | bytes 83886080 | tf_op jit(solution)/shard_map/forward_pass/pallas_call | solution.py:553
  177.5 2.1 collective-permute-start
  179.5 0.1 collective-permute-start.1
  179.6 0.7 slice_convert_fusion
  180.3 0.5 fusion.3
  180.8 0.6 fusion.4
  181.4 1.9 pad_add_fusion.refs_0_
  183.3 43.2 %expert_block.2 = (bf16[2,768,1024]{2,1,0:T(8,128)(2,1)}, bf16[2,768,1024]{2,1,0:T(8,128)(2,1)}, bf16[2,4,64,2048]{3,2,1,0:T(8,128)(2,1)}, bf16[2,4,64,2048]{3,2...) custom-call(s32[4]{0:T(128)} %pad_add_fusion.refs_0_, ...), custom_call_target="tpu_custom_call" | custom-call | flops 25769803776 | bytes 50331648 | tf_op jit(solution)/shard_map/expert_block/pallas_call | solution.py:1335
  226.5 2.0 collective-permute-start.2
  228.5 0.1 collective-permute-start.3
  228.6 0.0 copy-done.3
  228.6 1.0 copy.35
  229.6 1.9 pad_add_fusion.2.refs_0_
  231.5 0.0 collective-permute-done.refs_6_
  231.5 0.0 collective-permute-done.1.refs_8_
  231.5 1.4 copy-done.6
  232.9 43.4 %expert_block.3 = (bf16[2,768,1024]{2,1,0:T(8,128)(2,1)}, bf16[2,768,1024]{2,1,0:T(8,128)(2,1)}, bf16[2,4,64,2048]{3,2,1,0:T(8,128)(2,1)}, bf16[2,4,64,2048]{3,2...) custom-call(s32[4]{0:T(128)} %pad_add_fusion.2.refs_0_, ...), custom_call_target="tpu_custom_call" | custom-call | flops 25769803776 | bytes 50331648 | tf_op jit(solution)/shard_map/expert_block/pallas_call | solution.py:1335
  276.3 0.0 collective-permute-done.2.arrived_in
  276.3 0.0 collective-permute-done.3.arrived_out
  276.3 1.0 broadcast_in_dim.14.slot_col
  277.3 222.2 %backward_pass.1 = (bf16[1024,1024]{1,0:T(8,128)(2,1)}, f32[1024,1024]{1,0:T(8,128)}, f32[2,32,4096]{2,1,0:T(8,128)}, f32[2,128,1024]{2,1,0:T(8,128)}, f32[32,30...) custom-call(bf16[1024,3072]{1,0:T(8,128)(2,1)} %get-tuple-element.46, ...), custom_call_target="tpu_custom_call" | custom-call | flops 32212254720 | bytes 83886080 | tf_op jit(solution)/shard_map/backward_pass/pallas_call | solution.py:1075
  499.5 0.7 slice_bitcast_fusion
  500.2 0.7 slice_reduce_fusion
  501.0 3.2 copy.42
  504.2 0.0 copy-done
  504.2 2.0 copy.43
  506.2 0.0 copy-done.4
  506.2 0.7 copy.44
  507.0 0.0 copy-done.5
  507.0 0.7 copy.45
  507.6 0.0 copy-done.2
  507.6 1.0 copy.46
  508.6 1.0 copy.47
  (10 shorter events, 0.0 us)
Async XLA Ops:
  177.5 54.0 %collective-permute-start = (bf16[2,4,2,32,2048]{4,3,2,1,0:T(8,128)(2,1)}, bf16[2,4,2,32,2048]{4,3,2,1,0:T(8,128)(2,1)S(1)}, u32[]{:S(2)}, u32[]{:S(2)}) collective-permute-start(bf16[2,4,2,32,2048]{4,3,2,1,0:T(8,128)(2,1)} %get-tuple-element.59.refs_5_), channel_id=1, source_target_pairs={{0,1},{1,0},{2,3},{3,2},{4,5},{5,4},{6,7},{7,6},{8,9},{9,8},{10,11... | collective-permute-start | bytes 6291464 | tf_op jit(solution)/shard_map/ppermute | solution.py:76
  179.5 52.0 %collective-permute-start.1 = (bf16[2,4,128,1024]{3,2,1,0:T(8,128)(2,1)}, bf16[2,4,128,1024]{3,2,1,0:T(8,128)(2,1)}, u32[]{:S(2)}, u32[]{:S(2)}) collective-permute-start(bf16[2,4,128,1024]{3,2,1,0:T(8,128)(2,1)} %get-tuple-element.60.refs_7_), channel_id=1, source_target_pairs={{0,2},{1,3},{2,0},{3,1},{4,6},{5,7},{6,4},{7,5},{8,10},{9,11},{10,... | collective-permute-start | bytes 6291464 | tf_op jit(solution)/shard_map/ppermute | solution.py:76
  183.3 45.3 %copy-start.3 = (f32[1024,128]{1,0:T(8,128)S(1)}, f32[1024,128]{1,0:T(8,128)}, u32[]{:S(2)}) copy-start(f32[1024,128]{1,0:T(8,128)} %get-tuple-element.72) | copy-start | bytes 1572868
  226.5 49.8 %collective-permute-start.2 = (bf16[2,4,64,2048]{3,2,1,0:T(8,128)(2,1)}, bf16[2,4,64,2048]{3,2,1,0:T(8,128)(2,1)}, u32[]{:S(2)}, u32[]{:S(2)}) collective-permute-start(bf16[2,4,64,2048]{3,2,1,0:T(8,128)(2,1)} %get-tuple-element.66), channel_id=1, source_target_pairs={{0,1},{1,0},{2,3},{3,2},{4,5},{5,4},{6,7},{7,6},{8,9},{9,8},{10,11... | collective-permute-start | bytes 6291464 | tf_op jit(solution)/shard_map/ppermute | solution.py:76
  228.5 47.8 %collective-permute-start.3 = (bf16[2,4,64,2048]{3,2,1,0:T(8,128)(2,1)}, bf16[2,4,64,2048]{3,2,1,0:T(8,128)(2,1)}, u32[]{:S(2)}, u32[]{:S(2)}) collective-permute-start(bf16[2,4,64,2048]{3,2,1,0:T(8,128)(2,1)} %get-tuple-element.67), channel_id=1, source_target_pairs={{0,2},{1,3},{2,0},{3,1},{4,6},{5,7},{6,4},{7,5},{8,10},{9,11},{10,... | collective-permute-start | bytes 6291464 | tf_op jit(solution)/shard_map/ppermute | solution.py:76
  231.5 1.4 copy-start.6
  501.0 3.2 copy-start
  504.2 2.0 copy-start.4
  504.2 2.8 copy-start.5
  504.2 3.4 copy-start.2
  506.2 2.4 copy-start.1

commit v3 on v2

--- a/solution.py
+++ b/solution.py
@@ -16,6 +16,7 @@
 BLOCK = 128
 TILE = 256
 MIB = 1024 * 1024
+PARTS = 4
 F32 = jnp.float32
 BF16 = jnp.bfloat16
 NT = (((1,), (1,)), ((), ()))
@@ -324,17 +325,15 @@
     seg_col,
     slot_row,
     grad_out,
-    note,
     out_qkv,
     out_attn,
     out_params,
     first_in,
     first_out,
-    held_in,
-    held_out,
+    column_in,
+    column_out,
     sorted_other,
     grad_other,
-    noted,
     normed,
     projected,
     mixed,
@@ -372,11 +371,21 @@
         return one
 
     own = local_start(mine, weights.at[zed, core, flat])
-    column = [remote.start(mine, weights.at[zed, core, flat], device) for device in others]
-    column_in, column_out = held_in.at[0], held_out.at[0]
+    stream_columns = (slice(0, 2 * wide), slice(2 * wide, 4 * wide + BLOCK))
+
+    def send_column(stream):
+        columns = stream_columns[stream]
+        return [
+            remote.start(
+                mine.at[:, columns], weights.at[zed, core, flat, :, columns], device
+            )
+            for device in others
+        ]
+
+    column = [send_column(0)]
     targets = (first_in.at[zed, core, flat], column_in.at[zed, core])
     cut = own_in.shape[2] // (2 * nz)
-    crossed, blocks = [remote.start(note, noted, sibling)], []
+    crossed, blocks = [], []
     for e in range(EXPERTS):
         for z_of in range(nz):
             target = targets[e].at[:, pl.ds(z_of * cut, cut)]
@@ -407,53 +416,52 @@
         bias[place, :span] = jnp.where(same & (key <= query), 0.0, MASKED)
     stats[...] = jnp.zeros_like(stats)
 
-    def stream_columns(stream):
-        return slice(0, 2 * wide) if stream == 0 else slice(2 * wide, 4 * wide + BLOCK)
-
     def send_weights(stream, owner, device):
-        place = weights.at[:, core, owner, :, stream_columns(stream)]
+        place = weights.at[:, core, owner, :, stream_columns[stream]]
         return remote.start(place, place, device)
 
-    own.wait()
-    wait_in(column)
-    exchanged = [remote.start(grad_sorted, grad_other, sibling)]
     near = [tuple(reversed(moves.orders[n]))[0] for n in range(2)]
     far = [moves.orders[n][0] for n in range(2)]
-    hop_near = [send_weights(n, flat, hops[near[n]]) for n in range(2)]
-    hop_far = [send_weights(n, flat, hops[far[n]]) for n in range(2)]
-    place = weights.at[:, core, flat]
-    across = [remote.start(place, place, sibling)]
+    hop_near, hop_far, across = [], [], []
+    own.wait()
+    wait_in(column[0])
+    column.append(send_column(1))
+    hop_near.append(send_weights(0, flat, hops[near[0]]))
+    hop_far.append(send_weights(0, flat, hops[far[0]]))
+    across.append(send_weights(0, flat, sibling))
 
     wait_in(crossed)
     for one in blocks:
         one.wait()
-    first_column = []
-    for device in others:
-        place = first_in.at[zed, :, flat]
-        first_column.append(remote.start(place, place, device))
-        first_column.append(remote.start(own_out.at[0], first_out.at[zed, flat], device))
-
+    wait_in(column[1])
+    place = first_in.at[zed, :, flat]
+    first_column = [[remote.start(place, place, device) for device in others]]
+    hop_near.append(send_weights(1, flat, hops[near[1]]))
+    hop_far.append(send_weights(1, flat, hops[far[1]]))
+    across.append(send_weights(1, flat, sibling))
     wait_in(hop_near)
     hop_last = [send_weights(n, flat ^ near[n], hops[far[n]]) for n in range(2)]
     across += [send_weights(n, flat ^ near[n], sibling) for n in range(2)]
+    exchanged = [remote.start(grad_sorted, grad_other, sibling)]
+
+    def send_first(stream, owner, device):
+        place = first_in.at[:, :, owner] if stream == 0 else first_out.at[:, owner]
+        return remote.start(place, place, device)
+
+    first_near, first_far = [], []
+    wait_in(first_column[0])
+    first_column.append(
+        [
+            remote.start(own_out.at[0], first_out.at[zed, flat], device)
+            for device in others
+        ]
+    )
+    first_near.append(send_first(0, flat, hops[near[0]]))
+    first_far.append(send_first(0, flat, hops[far[0]]))
     wait_in(hop_far)
     across += [send_weights(n, flat ^ far[n], sibling) for n in range(2)]
     wait_in(hop_last)
     across += [send_weights(n, flat ^ near[n] ^ far[n], sibling) for n in range(2)]
-
-    def send_first(stream, owner, device):
-        place = first_in.at[:, :, owner] if stream == 0 else first_out.at[:, owner]
-        return remote.start(place, place, device)
-
-    wait_in(first_column)
-    first_near = [send_first(n, flat, hops[near[n]]) for n in range(2)]
-    first_far = [send_first(n, flat, hops[far[n]]) for n in range(2)]
-    second_column = []
-    for device in others:
-        place = column_in.at[zed]
-        second_column.append(remote.start(place, place, device))
-        second_column.append(remote.start(own_out.at[1], column_out.at[zed], device))
-
     wait_in(across)
     whole = 2 * nz * nf * mine.shape[0]
     writes = [
@@ -473,6 +481,15 @@
             columns = pl.ds(part * wide, wide)
             matrix = weights[:, :, :, :, columns].reshape(whole, wide)
             projected[place, columns] = dot(normed[place, :], matrix).astype(BF16)
+
+    wait_in(first_column[1])
+    first_near.append(send_first(1, flat, hops[near[1]]))
+    first_far.append(send_first(1, flat, hops[far[1]]))
+    second_column = []
+    for device in others:
+        place = column_in.at[zed]
+        second_column.append(remote.start(place, place, device))
+        second_column.append(remote.start(own_out.at[1], column_out.at[zed], device))
 
     lane = lax.broadcasted_iota(jnp.int32, (1, BLOCK), 1)
     pairs = wide // BLOCK
@@ -500,22 +517,19 @@
             stats[place, :] = held
             mixed[place, columns[0]] = result.astype(BF16)
 
-    @pl.loop(0, pairs // 4)
+    wait_in([first_near[0]])
+    first_last = [send_first(0, flat ^ near[0], hops[far[0]])]
+
+    @pl.loop(0, pairs // 2)
     def _(pair):
         attend_pair(pair)
 
-    wait_in(first_near)
-    first_last = [send_first(n, flat ^ near[n], hops[far[n]]) for n in range(2)]
-
-    @pl.loop(pairs // 4, pairs)
+    wait_in([first_near[1]])
+    first_last.append(send_first(1, flat ^ near[1], hops[far[1]]))
+
+    @pl.loop(pairs // 2, pairs)
     def _(pair):
         attend_pair(pair)
-
-    wait_in(second_column)
-    second_near = [
-        remote.start(held.at[0], held.at[1], hops[near[n]])
-        for n, held in enumerate((held_in, held_out))
-    ]
 
     gain_two, shift_two = turned[2:3, :], turned[3:4, :]
 
@@ -532,7 +546,7 @@
     exchanged.append(remote.start(sorted_rows, sorted_other, sibling))
     wait_in(first_far)
     wait_in(first_last)
-    wait_in(second_near)
+    wait_in(second_column)
     wait_in(exchanged)
     for one in remote.made:
         one.wait_send()
@@ -540,7 +554,7 @@
         one.wait()
 
 
-def forward_pass(moves, tokens, mine, own_in, own_out, seg_row, seg_col, slot_row, grad_out, note):
+def forward_pass(moves, tokens, mine, own_in, own_out, seg_row, seg_col, slot_row, grad_out):
     nz, nf = moves.nz, moves.nf
     rows, wide = tokens.shape
     deep, half = own_in.shape[1], own_in.shape[2] // 2
@@ -549,22 +563,21 @@
     anywhere = pl.BlockSpec(memory_space=pl.ANY)
     inside = pl.BlockSpec(memory_space=pltpu.VMEM)
     shape = jax.ShapeDtypeStruct
-    remote = 7 * (nz - 1) + 2 * nz + 24
+    remote = 6 * (nz - 1) + 2 * nz + 24
     return pl.pallas_call(
         functools.partial(forward_kernel, moves),
-        in_specs=[inside] * 9,
-        out_specs=[anywhere] * 10 + [inside] * 7,
+        in_specs=[inside] * 8,
+        out_specs=[anywhere] * 9 + [inside] * 7,
         out_shape=[
             shape((nz, 2, nf, deep, 3 * wide), BF16),
             shape((nz, 2, nf, deep, wide), BF16),
             shape((nz, 2, nf, deep, BLOCK), BF16),
             shape((nz, 2, nf, deep, half), BF16),
             shape((nz, nf, part, wide), BF16),
-            shape((2, nz, 2, deep, half), BF16),
-            shape((2, nz, part, wide), BF16),
+            shape((nz, 2, deep, half), BF16),
+            shape((nz, part, wide), BF16),
             shape((EXPERTS * capacity, wide), BF16),
             shape((EXPERTS * capacity, wide), BF16),
-            shape(note.shape, BF16),
             shape((rows, wide), BF16),
             shape((rows, 3 * wide), BF16),
             shape((rows, wide), BF16),
@@ -588,7 +601,7 @@
             flops=10 * rows * wide * wide, bytes_accessed=80 * wide * wide, transcendentals=0
         ),
         name="forward_pass",
-    )(tokens, mine, own_in, own_out, seg_row, seg_col, slot_row, grad_out, note)
+    )(tokens, mine, own_in, own_out, seg_row, seg_col, slot_row, grad_out)
 
 
 def sum_low(*values):
@@ -610,12 +623,16 @@
     grad_out,
     rows_first,
     rows_second,
-    other_first,
+    landed_first,
     other_second,
     keep_first_in,
     keep_first_out,
     arrived_in,
     arrived_out,
+    first_hop_in,
+    first_hop_out,
+    first_own,
+    first_landed,
     keep_in,
     sent_in,
     keep_out,
@@ -637,8 +654,6 @@
     got_out,
     hop_in,
     hop_out,
-    first_hop_in,
-    first_hop_out,
     landed,
     wide_low,
     wide_f32,
@@ -664,6 +679,7 @@
     spare,
     up_first,
     z_first,
+    early,
     z_second,
     final,
     send_sems,
@@ -674,7 +690,7 @@
     dp, flat = lax.axis_index("dp"), lax.axis_index("fsdp")
     zed, core = dp // 2, lax.rem(dp, 2)
     rows, wide = tokens.shape
-    half = wide // 2
+    share = wide // PARTS
     sibling = (zed * 2 + 1 - core, flat)
     others = [((zed ^ k) * 2 + core, flat) for k in range(1, nz)]
     hops = {bit: (dp, flat ^ bit) for bit in moves.orders[0]}
@@ -699,16 +715,12 @@
 
     capacity = rows_first.shape[1]
     crossed_rows = [
-        remote.start(other_first.at[1], grad_projected.at[pl.ds(0, capacity), pl.ds(2 * wide, wide)], sibling),
-        remote.start(other_second.at[1], grad_mixed.at[pl.ds(0, capacity)], sibling),
+        remote.start(other_second.at[1], grad_mixed.at[pl.ds(0, capacity)], sibling)
     ]
-    crossed_late = [
-        remote.start(other.at[0], landed.at[e], sibling)
-        for e, other in enumerate((other_first, other_second))
-    ]
+    crossed_late = [remote.start(other_second.at[0], landed, sibling)]
     row_loads = [
         local_start(source.at[1], grad_projected.at[pl.ds(0, capacity), pl.ds(e * wide, wide)])
-        for e, source in enumerate((rows_first, rows_second))
+        for e, source in enumerate((rows_first, rows_second, landed_first))
     ]
     loaded = local_start(projected, wide_low)
     phase_loads = [
@@ -721,24 +733,47 @@
     keep_first, arrived = (keep_first_in, keep_first_out), (arrived_in, arrived_out)
     first_hop = (first_hop_in, first_hop_out)
 
-    def first_next(n):
-        load((keep_first[n].at[1], up_first.at[n]), (arrived[n].at[1], spare.at[0]))
+    keep, sent = (keep_in, keep_out), (sent_in, sent_out)
+    got, hop = (got_in, got_out), (hop_in, hop_out)
+    half_rows = [pl.ds(h * deep, deep) for h in range(2)]
+    second_got = {}
+
+    def second_start(h):
+        for index in (1, 0):
+            for n in range(2):
+                second_got[n, index, h] = remote.start(
+                    sent[n].at[index, :, half_rows[h]],
+                    got[n].at[index, :, half_rows[h]],
+                    hops[one_way[n]],
+                )
+
+    def sum_blocks(target, sources, h):
+        pairs = []
+        for n in range(2):
+            for source, place in zip(sources[n], [target.at[n], spare.at[n, 0], spare.at[n, 1]]):
+                pairs.append((source.at[:, half_rows[h]], place))
+        load(*pairs)
 
         @pl.loop(0, nz)
         def _(k):
-            up_first[n, k] = sum_low(up_first[n, k], spare[0, k]).astype(BF16)
-
-        return remote.start(up_first.at[n], first_hop[n], hops[other_way[n]])
-
-    first_hops = [first_next(n) for n in range(2)]
-    keep, sent = (keep_in, keep_out), (sent_in, sent_out)
-    got, hop = (got_in, got_out), (hop_in, hop_out)
-    second_got = {}
-    for index in (1, 0):
-        for n in range(2):
-            second_got[n, index] = remote.start(
-                sent[n].at[index], got[n].at[index], hops[one_way[n]]
-            )
+            for n in range(2):
+                arrived = [spare[n, m, k] for m in range(len(sources[n]) - 1)]
+                target[n, k] = sum_low(target[n, k], *arrived).astype(BF16)
+
+    def z_send(source, landing):
+        return [
+            remote.start(source.at[n, k], landing.at[n, k - 1], others[k - 1])
+            for k in range(1, nz)
+            for n in range(2)
+        ]
+
+    second_start(0)
+    sum_blocks(
+        up_first,
+        [(keep_first[n].at[0], arrived[n].at[0], first_hop[n]) for n in range(2)],
+        1,
+    )
+    first_z = z_send(up_first, z_first)
 
     for one in row_loads + phase_loads:
         one.wait()
@@ -782,29 +817,29 @@
         )
 
     sums_two = lax.fori_loop(0, rows // TILE, second_norm_tile, (empty, empty))
-    load((wide_f32, grad_tokens), (normed_out, normed), (tokens_in, tokens))
-
-    def first_sums(n):
-        load(
-            (keep_first[n].at[0], up_first.at[n]),
-            (arrived[n].at[0], spare.at[0]),
-            (first_hop[n], spare.at[1]),
+    reloads = [local_start(normed_out, normed), local_start(tokens_in, tokens)]
+    saved = local_start(wide_f32, grad_tokens)
+
+    def second_next(h):
+        wait_in([second_got[n, 1, h] for n in range(2)])
+        sum_blocks(up.at[h], [(keep[n].at[1], got[n].at[1]) for n in range(2)], h)
+        return [
+            remote.start(up.at[h, n], hop[n].at[:, half_rows[h]], hops[other_way[n]])
+            for n in range(2)
+        ]
+
+    def second_z(h, hopped):
+        wait_in([second_got[n, 0, h] for n in range(2)] + hopped)
+        for one in hopped:
+            one.wait_send()
+        sum_blocks(
+            up.at[h], [(keep[n].at[0], got[n].at[0], hop[n]) for n in range(2)], h
         )
-
-        @pl.loop(0, nz)
-        def _(k):
-            total = sum_low(up_first[n, k], spare[0, k], spare[1, k])
-            up_first[n, k] = total.astype(BF16)
-
-        return [
-            remote.start(up_first.at[n, k], z_first.at[n, k - 1], others[k - 1])
-            for k in range(1, nz)
-        ]
-
-    wait_in(first_hops)
-    for one in first_hops:
-        one.wait_send()
-    first_z = first_sums(0) + first_sums(1)
+        return z_send(up.at[h], z_second.at[h])
+
+    second_hop = second_next(0)
+    second_start(1)
+    saved.wait()
 
     lane = lax.broadcasted_iota(jnp.int32, (1, BLOCK), 1)
     row = lax.broadcasted_iota(jnp.int32, (BLOCK, 1), 0)
@@ -864,12 +899,12 @@
             mixed_turned = mixed[:, place].T
             for part in range(4):
                 if part < 3:
-                    columns = pl.ds(part * wide + n * half, half)
+                    columns = pl.ds(part * wide + n * share, share)
                     made = dot(turned, grad_projected[:, columns])
                 else:
-                    made = dot(mixed_turned, branch[:, pl.ds(n * half, half)])
-                made = made.astype(BF16).reshape(2, nf, deep, half)
-                low[n, z_of, :, :, :, pl.ds(part * half, half)] = made
+                    made = dot(mixed_turned, branch[:, pl.ds(n * share, share)])
+                made = made.astype(BF16).reshape(2, nf, deep, share)
+                low[n, z_of, :, :, :, pl.ds(part * share, share)] = made
 
     def cross_start(source, target):
         return remote.start(source.at[:, 1 - core], target, sibling)
@@ -912,29 +947,12 @@
     def z_total(source, z_landing):
         return sum_low(source[zed, core, flat], *[z_landing[k] for k in range(nz - 1)])
 
-    def second_next(n):
-        load((keep[n].at[1], up.at[n]), (got[n].at[1], spare.at[0]))
-
-        @pl.loop(0, nz)
-        def _(k):
-            up[n, k] = sum_low(up[n, k], spare[0, k]).astype(BF16)
-
-        return remote.start(up.at[n], hop[n], hops[other_way[n]])
-
-    def second_z(n):
-        load((keep[n].at[0], up.at[n]), (got[n].at[0], spare.at[0]), (hop[n], spare.at[1]))
-
-        @pl.loop(0, nz)
-        def _(k):
-            up[n, k] = sum_low(up[n, k], spare[0, k], spare[1, k]).astype(BF16)
-
-        return [
-            remote.start(up.at[n, k], z_second.at[n, k - 1], others[k - 1]) for k in range(1, nz)
-        ]
-
-    def finish_expert(e, own, z_landing, writes):
+    def finish_half(e, h, own, landing):
         for n in range(2):
-            final[2 * e + n] = sum_low(own[n], *[z_landing[n, k] for k in range(nz - 1)])
+            total = sum_low(own[n], *[landing[n, k] for k in range(nz - 1)])
+            final[2 * e + n, half_rows[h]] = total
+
+    def finish_expert(e, writes):
         cut = share_in.shape[2] // (2 * nz)
         for z_of in range(nz):
             place = pl.ds(pl.multiple_of((z_of * 2 + core) * cut, cut), cut)
@@ -955,39 +973,12 @@
 
     def put_share(n, total):
         for part in range(4):
-            piece = total[:, part * half : (part + 1) * half]
+            piece = total[:, part * share : (part + 1) * share]
             if part < 3:
-                share_qkv[:, pl.ds(part * wide + n * half, half)] = piece
+                share_qkv[:, pl.ds(part * wide + n * share, share)] = piece
             else:
-                share_attn[:, pl.ds(n * half, half)] = piece
-
-    stored = []
-    attend_pairs(0, pairs // 2)
-    weight_grads(0)
-    crossed = [cross_start(low.at[0], cross.at[0])]
-    wait_in([second_got[n, 1] for n in range(2)])
-    second_hop = [second_next(n) for n in range(2)]
-    attend_pairs(pairs // 2, 3 * pairs // 4)
-    wait_in(crossed)
-    cross_add(low.at[0], cross.at[0])
-    hops_a = hop_start(low.at[0], got_q.at[0], 0)
-    attend_pairs(3 * pairs // 4, pairs)
-    reload = local_start(whole_qkv, wide_low)
-    restore = local_start(grad_tokens, wide_f32)
-    weight_grads(1)
-    crossed = [cross_start(low.at[1], cross.at[1])]
-    wait_in(hops_a)
-    next_a = hop_next(low.at[0], got_q.at[0], up_q.at[0], hop_q.at[0], 0)
-    wait_in([second_got[n, 0] for n in range(2)] + second_hop)
-    for one in second_hop:
-        one.wait_send()
-    second_zs = second_z(0) + second_z(1)
-    wait_in(crossed)
-    cross_add(low.at[1], cross.at[1])
-    hops_b = hop_start(low.at[1], got_q.at[1], 1)
-
-    reload.wait()
-    restore.wait()
+                share_attn[:, pl.ds(n * share, share)] = piece
+
     def norm_tile(t, sums):
         place = pl.ds(pl.multiple_of(t * TILE, TILE), TILE)
         grad = dot_nt(grad_projected[place, :], wide_low[...])
@@ -998,31 +989,79 @@
             sums[1] + jnp.sum(grad, axis=0, keepdims=True),
         )
 
-    sums = lax.fori_loop(0, rows // TILE, norm_tile, (empty, empty))
+    stored, writes = [], []
+    step = pairs // PARTS
+    crossed, hopped, went, turned_z = {}, {}, {}, {}
+
+    def part_begin(n):
+        attend_pairs(n * step, (n + 1) * step)
+        if n == 0:
+            for one in reloads:
+                one.wait()
+        weight_grads(n)
+        crossed[n] = cross_start(low.at[n], cross.at[n])
+
+    def part_hop(n):
+        wait_in([crossed[n]])
+        cross_add(low.at[n], cross.at[n])
+        hopped[n] = hop_start(low.at[n], got_q.at[n], n % 2)
+
+    def part_next(n):
+        wait_in([hopped[n][0]])
+        went[n] = hop_next(low.at[n], got_q.at[n], up_q.at[n], hop_q.at[n], n % 2)
+
+    def part_z(n):
+        wait_in([hopped[n][1], went[n]])
+        turned_z[n] = z_start(low.at[n], got_q.at[n], hop_q.at[n], z_q.at[n])
+
+    def part_end(n):
+        wait_in(turned_z[n])
+        put_share(n, z_total(low.at[n], z_q.at[n]))
+
+    part_begin(0)
+    second_zs = second_z(0, second_hop)
+    part_begin(1)
+    part_hop(0)
+    second_hop_late = second_next(1)
+    part_begin(2)
+    part_hop(1)
+    part_next(0)
+    attend_pairs(3 * step, 4 * step)
+    reload = local_start(whole_qkv, wide_low)
+    restore = local_start(grad_tokens, wide_f32)
+    weight_grads(3)
+    crossed[3] = cross_start(low.at[3], cross.at[3])
+    part_hop(2)
+    part_next(1)
+    part_z(0)
+    part_hop(3)
+    second_zs += second_z(1, second_hop_late)
+    reload.wait()
+    restore.wait()
+    sums = lax.fori_loop(0, rows // TILE // 2, norm_tile, (empty, empty))
+    part_next(2)
+    part_z(1)
+    part_next(3)
+    sums = lax.fori_loop(rows // TILE // 2, rows // TILE, norm_tile, sums)
     result = local_start(wide_f32, grad_tokens)
     index = lax.broadcasted_iota(jnp.int32, (BLOCK, 1), 0)
     stacked = jnp.zeros((BLOCK, wide), F32)
     for n, one in enumerate(sums + sums_two):
         stacked = jnp.where(index == n, one, stacked)
     vec[...] = stacked.T.reshape(nz, 2, nf, deep, BLOCK)
-    crossed = [cross_start(vec, cross_vec)]
-
-    wait_in([next_a])
-    z_a = z_start(low.at[0], got_q.at[0], hop_q.at[0], z_q.at[0])
-    wait_in(crossed)
+    crossed_v = [cross_start(vec, cross_vec)]
+    part_z(2)
+    part_z(3)
+    wait_in(crossed_v)
     cross_add(vec, cross_vec)
     hops_v = hop_start(vec, got_vec, 0)
-    writes = []
     wait_in(first_z)
-    finish_expert(0, [up_first[n, 0] for n in range(2)], z_first, writes)
+    load((first_own, spare.at[0, 0, pl.ds(0, 2)]), (first_landed, early))
+    finish_half(0, 0, [spare[0, 0, n] for n in range(2)], early)
+    finish_half(0, 1, [up_first[n, 0] for n in range(2)], z_first)
+    finish_expert(0, writes)
     wait_in(hops_v)
     next_v = hop_next(vec, got_vec, hop_vec.at[1], hop_vec.at[0], 0)
-    wait_in(hops_b)
-    next_b = hop_next(low.at[1], got_q.at[1], up_q.at[1], hop_q.at[1], 1)
-    wait_in([next_v])
-    z_v = z_start(vec, got_vec, hop_vec.at[0], z_vec)
-    wait_in([next_b])
-    z_b = z_start(low.at[1], got_q.at[1], hop_q.at[1], z_q.at[1])
 
     result.wait()
     wait_in(crossed_late)
@@ -1030,10 +1069,9 @@
         (hidden, wide_f32),
         *[
             (source.at[0], grad_projected.at[pl.ds(0, capacity), pl.ds(e * wide, wide)])
-            for e, source in enumerate((rows_first, rows_second))
+            for e, source in enumerate((rows_first, rows_second, landed_first))
         ],
-        (landed.at[0], grad_projected.at[pl.ds(0, capacity), pl.ds(2 * wide, wide)]),
-        (landed.at[1], grad_mixed.at[pl.ds(0, capacity)]),
+        (landed, grad_mixed.at[pl.ds(0, capacity)]),
     )
     add_rows(first_columns, grad_projected, pl.ds(2 * wide, wide))
     add_rows(second_columns, grad_mixed, first_columns)
@@ -1044,17 +1082,20 @@
         branch[place, :] = (wide_f32[place, :] + tokens_order(place)).astype(BF16)
 
     stored.append(local_start(branch, block_out))
-    wait_in(z_a)
-    put_share(0, z_total(low.at[0], z_q.at[0]))
+    wait_in([next_v])
+    z_v = z_start(vec, got_vec, hop_vec.at[0], z_vec)
+    for n in range(PARTS - 1):
+        part_end(n)
+    wait_in(second_zs)
+    for h in range(2):
+        finish_half(1, h, [up[h, n, 0] for n in range(2)], z_second.at[h])
+    finish_expert(1, writes)
+    part_end(PARTS - 1)
     wait_in(z_v)
     share_vectors[...] = z_total(vec, z_vec)
-    wait_in(second_zs)
-    finish_expert(1, [up[n, 0] for n in range(2)], z_second, writes)
-    wait_in(z_b)
-    put_share(1, z_total(low.at[1], z_q.at[1]))
     wait_in(writes)
     for one in remote.made:
-        if not any(one is other for other in second_hop + first_hops):
+        if not any(one is other for other in second_hop + second_hop_late):
             one.wait_send()
     for one in stored:
         one.wait()
@@ -1063,19 +1104,20 @@
 def backward_pass(moves, deep, big, row_parts, sums, stats, seg, slot_col, mixed, params):
     nz, nf = moves.nz, moves.nf
     rows, wide = mixed.shape
-    half = wide // 2
+    share = wide // PARTS
     block = sums[0].shape[2:]
+    half_block = (deep, block[1])
     capacity = row_parts[0].shape[1]
     anywhere = pl.BlockSpec(memory_space=pl.ANY)
     inside = pl.BlockSpec(memory_space=pltpu.VMEM)
     shape = jax.ShapeDtypeStruct
     landing = (2, nz) + block
-    remote = 24 + 7 * (nz - 1) + 2 * nz
+    remote = 24 + 5 * PARTS + (PARTS + 7) * (nz - 1) + 2 * nz
     inputs = list(big) + list(row_parts) + list(sums)
     return pl.pallas_call(
         functools.partial(backward_kernel, moves, deep),
         in_specs=[anywhere] * len(inputs) + [inside] * 6,
-        out_specs=[anywhere] * 4 + [inside] * 3 + [anywhere] * 7,
+        out_specs=[anywhere] * 4 + [inside] * 3 + [anywhere] * 5,
         out_shape=[
             shape((rows, wide), BF16),
             shape((rows, wide), F32),
@@ -1088,9 +1130,7 @@
             shape(landing, BF16),
             shape(landing[1:], BF16),
             shape(landing[1:], BF16),
-            shape(landing[1:], BF16),
-            shape(landing[1:], BF16),
-            shape((EXPERTS, capacity, wide), BF16),
+            shape((capacity, wide), BF16),
         ],
         scratch_shapes=[
             pltpu.VMEM((rows, 3 * wide), BF16),
@@ -1102,26 +1142,27 @@
             pltpu.VMEM((rows, wide), BF16),
             pltpu.VMEM((rows, BLOCK), F32),
             pltpu.VMEM((rows, BLOCK), F32),
-            pltpu.VMEM((2, nz, 2, nf, deep, 4 * half), BF16),
-            pltpu.VMEM((2, nz, nf, deep, 4 * half), BF16),
-            pltpu.VMEM((2, 2, nz, deep, 4 * half), BF16),
-            pltpu.VMEM((2, nz, deep, 4 * half), BF16),
-            pltpu.VMEM((2, nz - 1, deep, 4 * half), BF16),
-            pltpu.VMEM((2, nz, deep, 4 * half), BF16),
+            pltpu.VMEM((PARTS, nz, 2, nf, deep, 4 * share), BF16),
+            pltpu.VMEM((PARTS, nz, nf, deep, 4 * share), BF16),
+            pltpu.VMEM((PARTS, 2, nz, deep, 4 * share), BF16),
+            pltpu.VMEM((PARTS, nz, deep, 4 * share), BF16),
+            pltpu.VMEM((PARTS, nz - 1, deep, 4 * share), BF16),
+            pltpu.VMEM((PARTS, nz, deep, 4 * share), BF16),
             pltpu.VMEM((nz, 2, nf, deep, BLOCK), F32),
             pltpu.VMEM((nz, nf, deep, BLOCK), F32),
             pltpu.VMEM((2, nz, deep, BLOCK), F32),
             pltpu.VMEM((2, nz, deep, BLOCK), F32),
             pltpu.VMEM((nz - 1, deep, BLOCK), F32),
-            pltpu.VMEM((2, nz) + block, BF16),
-            pltpu.VMEM((2, nz) + block, BF16),
-            pltpu.VMEM((2, nz) + block, BF16),
-            pltpu.VMEM((2, nz - 1) + block, BF16),
-            pltpu.VMEM((2, nz - 1) + block, BF16),
+            pltpu.VMEM((2, 2, nz) + half_block, BF16),
+            pltpu.VMEM((2, 2, nz) + half_block, BF16),
+            pltpu.VMEM((2, nz) + half_block, BF16),
+            pltpu.VMEM((2, nz - 1) + half_block, BF16),
+            pltpu.VMEM((2, nz - 1) + half_block, BF16),
+            pltpu.VMEM((2, 2, nz - 1) + half_block, BF16),
             pltpu.VMEM((4,) + block, F32),
             pltpu.SemaphoreType.DMA((remote,)),
             pltpu.SemaphoreType.DMA((remote,)),
-            pltpu.SemaphoreType.DMA((44 + 2 * nz,)),
+            pltpu.SemaphoreType.DMA((60 + 2 * nz,)),
         ],
         compiler_params=pltpu.CompilerParams(
             collective_id=1, has_side_effects=True, vmem_limit_bytes=62 * MIB
@@ -1141,90 +1182,154 @@
     return (value * half, slope)
 
 
-def expert_kernel(plan, *refs):
-    moves, deep, chunk, chunks = plan[:4]
-    expert, place, x_own, x_other, g_own, g_other = (plan[4],) + refs[:5]
-    x_own, x_other, g_own, g_other = [
-        one.at[expert] for one in (x_own, x_other, g_own, g_other)
-    ]
-    loaded = plan[5]
-    weights, refs = refs[5 : 5 + loaded], refs[5 + loaded :]
-    count = 4 if moves is not None else 2
-    rows_out, refs = [refs[n // 2].at[n % 2] for n in range(4)], refs[2:]
-    grads, refs = refs[:count], refs[count:]
-    (win, wout, x, x_turned, g, branch, back, sum_in, sum_out, low_in, low_out, empty) = refs[:12]
-    w_sems, x_sem, out_sems, row_sem = refs[12:]
+def expert_kernel(moves, mode, expert, deep, chunk, chunks, x_own, x_other, g_own, g_other, *refs):
+    refs = list(refs)
+
+    def take(count):
+        taken, refs[:] = refs[:count], refs[count:]
+        return taken
+
+    if mode == "first":
+        weights, columns_own = take(2), take(2)
+    elif mode == "second":
+        columns_own, pieces = take(2), take(2)
+        first_grads, first_other = take(4), take(1)[0]
+    else:
+        weights = take(2)
+    rows_own, rows_other = take(2)
+    grads = take(2 if mode == "plain" else 4)
+    if mode == "first":
+        landing = take(2)
+    elif mode == "second":
+        got, hop, landed, own_z, landed_z = take(2), take(2), take(1)[0], *take(2)
+    (win, wout, x, x_turned, g, branch, back, sum_in, sum_out, low_in, low_out) = take(11)
+    w_sems, row_sems, out_sems = take(3)
     width = x.shape[1]
-    most = x_own.shape[0] // BLOCK
-    zed, flat, own_n, other_n = place[0], place[1], place[2], place[3]
-    blocks = own_n + other_n
-    tiles = (blocks + 1) // 2
-
-    def block_rows(i):
-        return pl.ds(pl.multiple_of(i * BLOCK, BLOCK), BLOCK)
-
-    def each_block(act):
-        for n, skip, a, b in ((own_n, 0, x_own, g_own), (other_n, own_n, x_other, g_other)):
-
-            @pl.loop(0, n)
-            def _(i):
-                for outer, inner in ((a, x), (b, g)):
-                    act(
-                        pltpu.make_async_copy(
-                            outer.at[block_rows(i)], inner.at[block_rows(skip + i)], x_sem
-                        )
+    rows = x.shape[0]
+    capacity = rows // 2
+    tiles = rows // TILE
+
+    if mode != "plain":
+        dp, flat = lax.axis_index("dp"), lax.axis_index("fsdp")
+        zed, core = dp // 2, lax.rem(dp, 2)
+        one_way = [moves.orders[n][0] for n in range(2)]
+        other_way = [moves.orders[n][1] for n in range(2)]
+        hops = {bit: (dp, flat ^ bit) for bit in moves.orders[0]}
+        sibling = (zed * 2 + 1 - core, flat)
+        devices = list(hops.values())
+        if mode == "second":
+            others = [((zed ^ k) * 2 + core, flat) for k in range(1, moves.nz)]
+            devices += [sibling] + others
+            up, spare, load_sems = take(3)
+            half_rows = [pl.ds(h * deep, deep) for h in range(2)]
+        barrier = pltpu.get_barrier_semaphore()
+        for device in devices:
+            pl.semaphore_signal(
+                barrier, inc=1, device_id=device, device_id_type=pl.DeviceIdType.MESH
+            )
+        pl.semaphore_wait(barrier, len(devices))
+        remote = Copies(*take(2))
+
+    if mode == "first":
+        near = [
+            remote.start(columns_own[n], landing[n].at[other_way[n] - 1], hops[other_way[n]])
+            for n in range(2)
+        ]
+        far = [
+            remote.start(columns_own[n], landing[n].at[one_way[n] - 1], hops[one_way[n]])
+            for n in range(2)
+        ]
+    elif mode == "second":
+        hopped = {}
+
+        def first_hop(h):
+            for index in (1, 0):
+                for n in range(2):
+                    hopped[n, index, h] = remote.start(
+                        first_grads[2 * n + 1].at[index, :, half_rows[h]],
+                        got[n].at[index, :, half_rows[h]],
+                        hops[one_way[n]],
                     )
 
-    each_block(lambda one: one.start())
-
+        def half_sum(index, h, target):
+            count = 2 if index else 3
+            pairs = []
+            for n in range(2):
+                sources = [first_grads[2 * n].at[index], got[n].at[index], hop[n]][:count]
+                places = [target.at[n], spare.at[n, 0], spare.at[n, 1]]
+                for source, there in zip(sources, places):
+                    pairs.append((source.at[:, half_rows[h]], there))
+            begun = [
+                pltpu.make_async_copy(source, there, load_sems.at[m])
+                for m, (source, there) in enumerate(pairs)
+            ]
+            for one in begun:
+                one.start()
+            for one in begun:
+                one.wait()
+
+            @pl.loop(0, moves.nz)
+            def _(k):
+                for n in range(2):
+                    arrived = [spare[n, m, k] for m in range(count - 1)]
+                    target[n, k] = sum_low(target[n, k], *arrived).astype(BF16)
+
+        def second_hop(h):
+            wait_in([hopped[n, 1, h] for n in range(2)])
+            half_sum(1, h, up.at[h])
+            return [
+                remote.start(up.at[h, n], hop[n].at[:, half_rows[h]], hops[other_way[n]])
+                for n in range(2)
+            ]
+
+        first_hop(0)
+        crossed = remote.start(first_other, landed, sibling)
+
+    loads = []
+    for n, (source, target) in enumerate(((x_own, x), (g_own, g), (x_other, x), (g_other, g))):
+        place = pl.ds((n // 2) * capacity, capacity)
+        loads.append(pltpu.make_async_copy(source.at[expert], target.at[place], row_sems.at[n]))
     copies = []
-    if loaded == 2:
+    if mode == "second":
+        part_rows = chunk // moves.nf
+        for offset in range(moves.nf):
+            owner = flat ^ offset
+            for k in range(moves.nz):
+                sources = [
+                    own.at[k] if offset == 0 else piece.at[offset - 1, k]
+                    for own, piece in zip(columns_own, pieces)
+                ]
+                for part in range(2):
+                    start = ((k * 2 + part) * moves.nf + owner) * deep
+                    place = pl.ds(pl.multiple_of(start, deep), deep)
+                    copies.append((sources[0].at[part], win.at[place]))
+                start = (k * moves.nf + owner) * part_rows
+                place = pl.ds(pl.multiple_of(start, part_rows), part_rows)
+                copies.append((sources[1], wout.at[place]))
+    else:
         copies = [(weights[0], win), (weights[1], wout)]
-    else:
-        part_rows = chunk // moves.nf
-        for stream in range(2):
-            offsets = moves.relative(stream)
-            half = len(offsets) // 2
-            for number, offset in enumerate(offsets):
-                piece = weights[stream * 2 + number // half].at[number % half]
-                owner = flat ^ offset
-                for k in range(moves.nz):
-                    if stream == 0:
-                        for part in range(2):
-                            start = ((k * 2 + part) * moves.nf + owner) * deep
-                            rows = pl.ds(pl.multiple_of(start, deep), deep)
-                            copies.append((piece.at[k, part], win.at[rows]))
-                    else:
-                        start = (k * moves.nf + owner) * part_rows
-                        rows = pl.ds(pl.multiple_of(start, part_rows), part_rows)
-                        copies.append((piece.at[k], wout.at[rows]))
-    begun = [
+    loads += [
         pltpu.make_async_copy(source, target, w_sems.at[n])
         for n, (source, target) in enumerate(copies)
     ]
-    for one in begun:
+    for one in loads:
         one.start()
-    empty[...] = jnp.zeros_like(empty)
     branch[...] = jnp.zeros_like(branch)
     back[...] = jnp.zeros_like(back)
-    each_block(lambda one: one.wait())
-
-    @pl.when(lax.rem(blocks, 2) == 1)
-    def _():
-        x[block_rows(blocks), :] = jnp.zeros((BLOCK, width), BF16)
-        g[block_rows(blocks), :] = jnp.zeros((BLOCK, width), BF16)
+    for one in loads[:4]:
+        one.wait()
 
     @pl.loop(0, tiles)
     def _(t):
-        rows = pl.ds(pl.multiple_of(t * TILE, TILE), TILE)
-        x_turned[:, rows] = x[rows, :].T
-
-    for one in begun:
+        place = pl.ds(pl.multiple_of(t * TILE, TILE), TILE)
+        x_turned[:, place] = x[place, :].T
+
+    for one in loads[4:]:
         one.wait()
 
     def grad_copies(j):
         columns = pl.ds(pl.multiple_of(j * chunk, chunk), chunk)
-        if moves is None:
+        if mode == "plain":
             made = [(low_in, grads[0].at[:, columns]), (low_out, grads[1].at[columns])]
         else:
             made = []
@@ -1240,37 +1345,36 @@
                         if stream == 0:
                             for k in range(moves.nz):
                                 start = (((zed ^ k) * 2 + part) * moves.nf + owner) * deep
-                                rows = pl.ds(pl.multiple_of(start, deep), deep)
-                                place_of = target.at[k, pl.ds(part * deep, deep), columns]
-                                made.append((low_in.at[rows], place_of))
+                                place = pl.ds(pl.multiple_of(start, deep), deep)
+                                there = target.at[k, pl.ds(part * deep, deep), columns]
+                                made.append((low_in.at[place], there))
                         else:
                             start = (owner * 2 + part) * half_deep
-                            rows = pl.ds(pl.multiple_of(start, half_deep), half_deep)
-                            place_of = target.at[k_of, :, pl.ds(part * width, width)]
-                            made.append((low_out.at[rows], place_of))
+                            place = pl.ds(pl.multiple_of(start, half_deep), half_deep)
+                            there = target.at[k_of, :, pl.ds(part * width, width)]
+                            made.append((low_out.at[place], there))
         return [
             pltpu.make_async_copy(source, target, out_sems.at[n])
             for n, (source, target) in enumerate(made)
         ]
 
-    @pl.loop(0, chunks)
-    def _(j):
+    def chunk_step(j):
         columns = pl.ds(pl.multiple_of(j * chunk, chunk), chunk)
         sum_in[...] = jnp.zeros_like(sum_in)
         sum_out[...] = jnp.zeros_like(sum_out)
 
         @pl.loop(0, tiles)
         def _(t):
-            rows = pl.ds(pl.multiple_of(t * TILE, TILE), TILE)
-            g_tile = g[rows, :]
-            inner = dot(x[rows, :], win[:, columns])
+            place = pl.ds(pl.multiple_of(t * TILE, TILE), TILE)
+            g_tile = g[place, :]
+            inner = dot(x[place, :], win[:, columns])
             grad_active = dot_nt(g_tile, wout[columns, :])
             active, slope = gelu_both(inner)
             active_low = active.astype(BF16)
             grad_inner = (grad_active * slope).astype(BF16)
-            branch[rows, :] += dot(active_low, wout[columns, :])
-            back[rows, :] += dot_nt(grad_inner, win[:, columns])
-            sum_in[...] += dot(x_turned[:, rows], grad_inner)
+            branch[place, :] += dot(active_low, wout[columns, :])
+            back[place, :] += dot_nt(grad_inner, win[:, columns])
+            sum_in[...] += dot(x_turned[:, place], grad_inner)
             sum_out[...] += dot_tn(active_low, g_tile)
 
         @pl.when(j > 0)
@@ -1283,86 +1387,122 @@
         for one in grad_copies(j):
             one.start()
 
+    def run_chunks(start, stop):
+        @pl.loop(start, stop)
+        def _(j):
+            chunk_step(j)
+
+    if mode == "plain":
+        run_chunks(0, chunks)
+    elif mode == "first":
+        run_chunks(0, chunks // 2)
+        wait_in(near)
+        far += [
+            remote.start(
+                landing[n].at[other_way[n] - 1],
+                landing[n].at[(one_way[n] ^ other_way[n]) - 1],
+                hops[one_way[n]],
+            )
+            for n in range(2)
+        ]
+        run_chunks(chunks // 2, chunks)
+    else:
+        run_chunks(0, chunks // 4)
+        last = second_hop(0)
+        first_hop(1)
+        run_chunks(chunks // 4, chunks // 2)
+        wait_in([hopped[n, 0, 0] for n in range(2)] + last)
+        half_sum(0, 0, up.at[2])
+        z_sent = [
+            remote.start(up.at[2, n, k], landed_z.at[n, k - 1], others[k - 1])
+            for k in range(1, moves.nz)
+            for n in range(2)
+        ]
+        own = pltpu.make_async_copy(up.at[2, :, 0], own_z, load_sems.at[0])
+        own.start()
+        own.wait()
+        run_chunks(chunks // 2, chunks - 1)
+        last = second_hop(1)
+        run_chunks(chunks - 1, chunks)
+
     @pl.loop(0, tiles)
     def _(t):
-        rows = pl.ds(pl.multiple_of(t * TILE, TILE), TILE)
-        x[rows, :] = branch[rows, :].astype(BF16)
-        g[rows, :] = back[rows, :].astype(BF16)
-
-    def each_result(act):
-        for n, skip, a, b in (
-            (own_n, 0, rows_out[0], rows_out[1]),
-            (other_n, own_n, rows_out[2], rows_out[3]),
-        ):
-
-            @pl.loop(0, n)
-            def _(i):
-                for outer, inner in ((a, x), (b, g)):
-                    act(
-                        pltpu.make_async_copy(
-                            inner.at[block_rows(skip + i)], outer.at[block_rows(i)], row_sem
-                        )
-                    )
-
-            @pl.loop(n, most)
-            def _(i):
-                for outer in (a, b):
-                    act(pltpu.make_async_copy(empty, outer.at[block_rows(i)], row_sem))
-
-    each_result(lambda one: one.start())
-    each_result(lambda one: one.wait())
-    for one in grad_copies(chunks - 1):
+        place = pl.ds(pl.multiple_of(t * TILE, TILE), TILE)
+        x[place, :] = branch[place, :].astype(BF16)
+        g[place, :] = back[place, :].astype(BF16)
+
+    stored = []
+    for n, (source, target) in enumerate(
+        ((x, rows_own.at[0]), (g, rows_own.at[1]), (x, rows_other.at[0]), (g, rows_other.at[1]))
+    ):
+        place = pl.ds((n // 2) * capacity, capacity)
+        stored.append(pltpu.make_async_copy(source.at[place], target, row_sems.at[n]))
+    for one in stored:
+        one.start()
+    for one in grad_copies(chunks - 1) + stored:
         one.wait()
-
-
-def expert_block(moves, expert, place, sorted_rows, weights, deep, half_hidden):
+    if mode == "first":
+        wait_in(far)
+    elif mode == "second":
+        wait_in([hopped[n, 0, 1] for n in range(2)] + last + z_sent + [crossed])
+    if mode != "plain":
+        for one in remote.made:
+            one.wait_send()
+
+
+def expert_block(moves, mode, expert, sorted_rows, extra, deep, half_hidden, grad_shapes, landing):
     capacity, width = sorted_rows[0].shape[1:]
-    most = 2 * capacity
-    if moves is not None:
-        chunks = moves.nz
-        copies = 4 * moves.nz * moves.nf
-    else:
-        chunks = 4
-        copies = 2
+    rows = 2 * capacity
+    chunks = 4 if mode == "plain" else moves.nz
     chunk = half_hidden // chunks
     anywhere = pl.BlockSpec(memory_space=pl.ANY)
     row_shape = jax.ShapeDtypeStruct((2, capacity, width), BF16)
-    if moves is not None:
-        block = (moves.nf // 2, moves.nz, 2 * deep, half_hidden)
-        grads = [jax.ShapeDtypeStruct(block, BF16)] * 4
-    else:
-        grads = [jax.ShapeDtypeStruct(w.shape, BF16) for w in weights]
+    outs = [row_shape] * 2 + grad_shapes + landing
+    scratch = [
+        pltpu.VMEM((width, half_hidden), BF16),
+        pltpu.VMEM((half_hidden, width), BF16),
+        pltpu.VMEM((rows, width), BF16),
+        pltpu.VMEM((width, rows), BF16),
+        pltpu.VMEM((rows, width), BF16),
+        pltpu.VMEM((rows, width), F32),
+        pltpu.VMEM((rows, width), F32),
+        pltpu.VMEM((width, chunk), F32),
+        pltpu.VMEM((chunk, width), F32),
+        pltpu.VMEM((width, chunk), BF16),
+        pltpu.VMEM((chunk, width), BF16),
+    ]
+    copies = 2 if mode == "plain" else 4 * moves.nz * moves.nf
+    scratch += [
+        pltpu.SemaphoreType.DMA((copies,)),
+        pltpu.SemaphoreType.DMA((4,)),
+        pltpu.SemaphoreType.DMA((copies,)),
+    ]
+    options = {}
+    if mode == "second":
+        block = (moves.nz, deep, half_hidden)
+        scratch += [
+            pltpu.VMEM((3, 2) + block, BF16),
+            pltpu.VMEM((2, 2) + block, BF16),
+            pltpu.SemaphoreType.DMA((6,)),
+        ]
+    if mode != "plain":
+        count = 13 + 2 * (moves.nz - 1) if mode == "second" else 6
+        scratch += [pltpu.SemaphoreType.DMA((count,))] * 2
+        options = {"collective_id": 2 + expert, "has_side_effects": True}
     return pl.pallas_call(
-        functools.partial(expert_kernel, (moves, deep, chunk, chunks, expert, len(weights))),
-        in_specs=[pl.BlockSpec(memory_space=pltpu.SMEM)] + [anywhere] * (4 + len(weights)),
-        out_specs=[anywhere] * (2 + len(grads)),
-        out_shape=[row_shape] * 2 + grads,
-        scratch_shapes=[
-            pltpu.VMEM((width, half_hidden), BF16),
-            pltpu.VMEM((half_hidden, width), BF16),
-            pltpu.VMEM((most, width), BF16),
-            pltpu.VMEM((width, most), BF16),
-            pltpu.VMEM((most, width), BF16),
-            pltpu.VMEM((most, width), F32),
-            pltpu.VMEM((most, width), F32),
-            pltpu.VMEM((width, chunk), F32),
-            pltpu.VMEM((chunk, width), F32),
-            pltpu.VMEM((width, chunk), BF16),
-            pltpu.VMEM((chunk, width), BF16),
-            pltpu.VMEM((BLOCK, width), BF16),
-            pltpu.SemaphoreType.DMA((copies,)),
-            pltpu.SemaphoreType.DMA,
-            pltpu.SemaphoreType.DMA((copies,)),
-            pltpu.SemaphoreType.DMA,
-        ],
-        compiler_params=pltpu.CompilerParams(vmem_limit_bytes=56 * MIB),
+        functools.partial(expert_kernel, moves, mode, expert, deep, chunk, chunks),
+        in_specs=[anywhere] * (4 + len(extra)),
+        out_specs=[anywhere] * len(outs),
+        out_shape=outs,
+        scratch_shapes=scratch,
+        compiler_params=pltpu.CompilerParams(vmem_limit_bytes=58 * MIB, **options),
         cost_estimate=pl.CostEstimate(
-            flops=12 * 1024 * width * half_hidden,
-            bytes_accessed=8 * width * half_hidden + 32 * 1024 * width,
-            transcendentals=1024 * half_hidden,
+            flops=12 * rows * width * half_hidden,
+            bytes_accessed=8 * width * half_hidden + 16 * rows * width,
+            transcendentals=rows * half_hidden,
         ),
-        name="expert_block",
-    )(place, *sorted_rows, *weights)
+        name="expert_" + mode,
+    )(*sorted_rows, *extra)
 
 
 def gather_experts_whole(w_expert_in, w_expert_out, core, nz):
@@ -1396,16 +1536,11 @@
 ):
     rows, width = tokens.shape
     deep = w_qkv.shape[0]
-    hidden = w_expert_in.shape[2]
-    half_hidden = hidden // 2
-    half = width // 2
     moves = Moves(nd, nf)
-    nz = moves.nz
-    staged = deep % 32 == 0
+    staged = deep % 32 == 0 and nf == 4 and moves.nz in (2, 4)
     core = lax.rem(lax.axis_index("dp"), 2)
     zed = lax.axis_index("dp") // 2
     flat = lax.axis_index("fsdp")
-    place = jnp.stack([zed, core, flat]).astype(jnp.int32)
 
     positions = jnp.arange(rows, dtype=jnp.int32)
     bounds = jnp.cumsum(seq_lengths[0])
@@ -1414,57 +1549,73 @@
     seg_col = jnp.broadcast_to(segment[:, None], (rows, BLOCK))
     routed = expert_ids[:, 0]
     rank_second = jnp.cumsum(routed) - routed
-    second_n = jnp.sum(routed)
     capacity = 3 * rows // 4
     slot = jnp.where(routed == 1, capacity + rank_second, positions - rank_second)
-    split = jnp.stack([rows - second_n, second_n]).astype(jnp.int32)
-    split = (split + BLOCK - 1) // BLOCK
 
     params = jnp.stack([ln1_gain, ln1_bias, ln2_gain, ln2_bias], axis=1)
     params = jnp.pad(params, ((0, 0), (0, BLOCK - 4)))
     mine = jnp.concatenate([w_qkv, w_attn_out, params], axis=1)
     arguments = (tokens, grad_out, mine, w_expert_in, w_expert_out)
     if staged:
-        return staged_block(moves, arguments, seg_row, seg_col, slot, split, (zed, core, flat))
-    return plain_block(moves, arguments, seg_row, seg_col, slot, split, (zed, core, flat))
-
-
-def staged_block(moves, arguments, seg_row, seg_col, slot, split, place):
+        return staged_block(moves, arguments, seg_row, seg_col, slot, (zed, core, flat))
+    return plain_block(moves, arguments, seg_row, seg_col, slot, (zed, core, flat))
+
+
+def staged_block(moves, arguments, seg_row, seg_col, slot, place):
     tokens, grad_out, mine, w_expert_in, w_expert_out = arguments
     rows, width = tokens.shape
     deep, hidden = w_expert_in.shape[1:]
     half_hidden = hidden // 2
     capacity = 3 * rows // 4
     zed, core, flat = place
-    note = jnp.broadcast_to(split[:, None].astype(BF16), (2, BLOCK))
-    note = jnp.pad(note, ((0, 14), (0, 0)))
     slot_row = jnp.broadcast_to(slot[None, :], (8, rows))
     slot_col = jnp.broadcast_to(slot[:, None], (rows, BLOCK))
     outs = forward_pass(
-        moves, tokens, mine, w_expert_in, w_expert_out, seg_row, seg_col, slot_row, grad_out, note
+        moves, tokens, mine, w_expert_in, w_expert_out, seg_row, seg_col, slot_row, grad_out
     )
     whole_qkv, whole_attn, params, first_in = [one.reshape(-1, one.shape[-1]) for one in outs[:4]]
     first_out = outs[4].reshape(half_hidden, width)
-    held = outs[5:7]
-    sorted_other, grad_other, noted = outs[7:10]
-    normed_one, projected, mixed, stats, hidden_one, sorted_rows, grad_sorted = outs[10:]
-    last = [moves.gather_last(held[0], 0), moves.gather_last(held[1], 1)]
-    weights = [[first_in, first_out], [held[0], last[0], held[1], last[1]]]
+    columns = list(outs[5:7])
+    sorted_other, grad_other = outs[7:9]
+    normed_one, projected, mixed, stats, hidden_one, sorted_rows, grad_sorted = outs[9:]
     by_expert = lambda value: value.reshape(EXPERTS, capacity, width)
     row_inputs = [by_expert(one) for one in (sorted_rows, sorted_other, grad_sorted, grad_other)]
-    split_other = noted[:2, 0].astype(jnp.int32)
-    made = []
-    for e in range(EXPERTS):
-        table = jnp.stack([zed, flat, split[e], split_other[e]]).astype(jnp.int32)
-        made.append(expert_block(moves, e, table, row_inputs, weights[e], deep, half_hidden))
-        if e == 0:
-            arrived = [moves.flat(made[0][3 + 2 * n], moves.orders[n][0]) for n in range(2)]
+    shape = lambda *dims: jax.ShapeDtypeStruct(dims, BF16)
+    nz, nf = moves.nz, moves.nf
+    block = (nz, 2 * deep, half_hidden)
+    grad_shapes = [shape(nf // 2, *block)] * 4
+    first = expert_block(
+        moves,
+        "first",
+        0,
+        row_inputs,
+        [first_in, first_out] + columns,
+        deep,
+        half_hidden,
+        grad_shapes,
+        [shape(nf - 1, *one.shape) for one in columns],
+    )
+    second = expert_block(
+        moves,
+        "second",
+        1,
+        row_inputs,
+        columns + list(first[6:8]) + list(first[2:6]) + [first[1]],
+        deep,
+        half_hidden,
+        grad_shapes,
+        [shape(2, *block)] * 2
+        + [shape(*block)] * 2
+        + [shape(2, capacity, width)]
+        + [shape(2, deep, half_hidden), shape(2, nz - 1, deep, half_hidden)],
+    )
+    landed = second[10]
     results = backward_pass(
         moves,
         deep,
         [projected, whole_qkv, whole_attn, hidden_one, normed_one, tokens, grad_out],
-        [made[0][0], made[1][0], made[0][1], made[1][1]],
-        [made[0][2], made[0][4]] + arrived + list(made[1][2:]),
+        [first[0], second[0], landed, second[1]],
+        [first[2], first[4]] + list(second[6:10]) + list(second[11:13]) + list(second[2:6]),
         stats.T,
         [seg_row, seg_col],
         slot_col,
@@ -1487,7 +1638,7 @@
     )
 
 
-def plain_block(moves, arguments, seg_row, seg_col, slot, split, place):
+def plain_block(moves, arguments, seg_row, seg_col, slot, place):
     tokens, grad_out, mine, w_expert_in, w_expert_out = arguments
     rows, width = tokens.shape
     hidden = w_expert_in.shape[2]
@@ -1517,11 +1668,13 @@
     for value in (normed_two, grad_out):
         ordered = dot(spread, value).astype(BF16)
         row_inputs += [by_expert(ordered), by_expert(moves.core(ordered))]
-    split_other = moves.core(jnp.broadcast_to(split[:, None], (2, BLOCK)))[:, 0]
     results, grad_pieces = [], []
     for e in range(EXPERTS):
-        table = jnp.stack([zed, flat, split[e], split_other[e]]).astype(jnp.int32)
-        outs = expert_block(None, e, table, row_inputs, expert_weights[e], deep, hidden // 2)
+        weights = expert_weights[e]
+        shapes = [jax.ShapeDtypeStruct(one.shape, BF16) for one in weights]
+        outs = expert_block(
+            moves, "plain", e, row_inputs, weights, deep, hidden // 2, shapes, []
+        )
         results.append(add_low(outs[0], moves.core(outs[1])))
         grad_pieces.append(outs[2:])
     both = jnp.concatenate(results, axis=1)

time: 517 us -> 464 us (0.90)
  Pallas kernels: 475 us -> 434 us
  other arithmetic: 11.6 us -> 5.08 us
    pallas_call x1, Pallas kernels: 222 us -> 138 us  [backward_pass(): pl.pallas_call(functools.partial(backward_kernel, moves, deep), in_specs=...]
    pallas_call x2, Pallas kernels: 86.7 us -> 156 us  [expert_block(): pl.pallas_call(functools.partial(expert_kernel, moves, mode, expert, deep...]
    pallas_call x1, Pallas kernels: 166 us -> 140 us  [forward_pass(): pl.pallas_call(functools.partial(forward_kernel, moves), in_specs=[inside...]
  transfers between devices with their start and end apart: 4 -> 0, of which waited for: 0 -> 0; matrix products, arithmetic and copies ran while one was open for 1% -> 0% of each run, Pallas kernels for 17% -> 0%
where the time goes in v3:
time: 464 us; the launch traced here: 455 us
  Pallas kernels  434 us (94%)
  local copies, waits for them, and re-layouts  14.6 us (3%)
  other arithmetic  5.08 us (1%)
    pallas_call x2, Pallas kernels, expert_block(): pl.pallas_call(functools.partial(expert_kernel, moves, mode, expert, deep...  156 us
    pallas_call x1, Pallas kernels, forward_pass(): pl.pallas_call(functools.partial(forward_kernel, moves), in_specs=[inside...  140 us
    pallas_call x1, Pallas kernels, backward_pass(): pl.pallas_call(functools.partial(backward_kernel, moves, deep), in_specs=...  138 us

profile of v3, /device:TPU:0, one launch (start us, length us, event | category | flops | bytes accessed | tf_op | source)
XLA Modules:
  0.0 455.0 jit_solution(17073663245293731732)
XLA Ops:
  0.6 0.7 pad_maximum_fusion
  1.4 0.1 copy.34
  1.5 1.7 fusion.1.mine
  3.2 0.8 reduce-window.19
  4.0 0.1 convert_reduce_fusion
  4.1 0.6 broadcast_in_dim.10.seg_row
  4.7 1.0 broadcast_in_dim.11.seg_col
  5.7 1.0 reduce-window.20
  6.6 0.1 slice.22
  6.7 0.1 slice_reduce_fusion.4
  6.9 0.8 subtract_select_fusion
  7.6 0.6 broadcast_in_dim.12.slot_row
  8.2 140.1 %forward_pass.1 = (bf16[4,2,4,32,3072]{4,3,2,1,0:T(8,128)(2,1)}, bf16[4,2,4,32,1024]{4,3,2,1,0:T(8,128)(2,1)}, bf16[4,2,4,32,128]{4,3,2,1,0:T(8,128)(2,1)}, bf16...) custom-call(bf16[1024,1024]{1,0:T(8,128)(2,1)} %tokens_in.1, ...), custom_call_target="tpu_custom_call" | custom-call | flops 10737418240 | bytes 83886080 | tf_op jit(solution)/shard_map/forward_pass/pallas_call | solution.py:567
  148.4 73.5 %expert_first.1 = (bf16[2,768,1024]{2,1,0:T(8,128)(2,1)}, bf16[2,768,1024]{2,1,0:T(8,128)(2,1)}, bf16[2,4,64,2048]{3,2,1,0:T(8,128)(2,1)}, bf16[2,4,64,2048]{3,2...) custom-call(bf16[2,768,1024]{2,1,0:T(8,128)(2,1)} %bitcast.44, ...), custom_call_target="tpu_custom_call" | custom-call | flops 38654705664 | bytes 41943040 | tf_op jit(solution)/shard_map/expert_first/pallas_call | solution.py:1492
  221.9 0.0 copy-start.3
  221.9 0.0 copy-start.6
  221.9 82.4 %expert_second.1 = (bf16[2,768,1024]{2,1,0:T(8,128)(2,1)}, bf16[2,768,1024]{2,1,0:T(8,128)(2,1)}, bf16[2,4,64,2048]{3,2,1,0:T(8,128)(2,1)}, bf16[2,4,64,2048]{3,...) custom-call(bf16[2,768,1024]{2,1,0:T(8,128)(2,1)} %bitcast.45, ...), custom_call_target="tpu_custom_call" | custom-call | flops 38654705664 | bytes 41943040 | tf_op jit(solution)/shard_map/expert_second/pallas_call | solution.py:1492
  304.3 0.0 copy-done.3
  304.3 1.0 copy.35
  305.3 0.0 copy-done.6
  305.3 1.0 broadcast_in_dim.14.slot_col
  306.3 138.1 %backward_pass.1 = (bf16[1024,1024]{1,0:T(8,128)(2,1)}, f32[1024,1024]{1,0:T(8,128)}, f32[2,32,4096]{2,1,0:T(8,128)}, f32[2,128,1024]{2,1,0:T(8,128)}, f32[32,30...) custom-call(bf16[1024,3072]{1,0:T(8,128)(2,1)} %get-tuple-element.54, ...), custom_call_target="tpu_custom_call" | custom-call | flops 32212254720 | bytes 83886080 | tf_op jit(solution)/shard_map/backward_pass/pallas_call | solution.py:1117
  444.5 0.7 slice_bitcast_fusion
  445.2 0.7 slice_reduce_fusion
  445.9 0.0 copy-start
  445.9 3.2 copy.42
  449.2 0.0 copy-done
  449.2 0.0 copy-start.4
  449.2 0.0 copy-start.5
  449.2 0.0 copy-start.2
  449.2 2.0 copy.43
  451.2 0.0 copy-done.4
  451.2 0.0 copy-start.1
  451.2 0.7 copy.44
  451.9 0.0 copy-done.5
  451.9 0.7 copy.45
  452.6 0.0 copy-done.2
  452.6 1.0 copy.46
  453.6 0.0 copy-done.1
  453.6 1.0 copy.47
  (2 shorter events, 0.0 us)
Async XLA Ops:
  221.9 82.4 %copy-start.3 = (f32[1024,128]{1,0:T(8,128)S(1)}, f32[1024,128]{1,0:T(8,128)}, u32[]{:S(2)}) copy-start(f32[1024,128]{1,0:T(8,128)} %get-tuple-element.88) | copy-start | bytes 1572868
  221.9 83.4 %copy-start.6 = (s32[1024,1]{0,1:T(1,128)S(1)}, s32[1024,1]{0,1:T(1,128)}, u32[]{:S(2)}) copy-start(s32[1024,1]{0,1:T(1,128)} %param.14) | copy-start | bytes 12292
  445.9 3.2 copy-start
  449.2 2.0 copy-start.4
  449.2 2.8 copy-start.5
  449.2 3.4 copy-start.2
  451.2 2.4 copy-start.1

commit v4 on v3

--- a/solution.py
+++ b/solution.py
@@ -334,15 +334,17 @@
     column_out,
     sorted_other,
     grad_other,
-    normed,
+    turned_normed,
     projected,
-    mixed,
+    turned_mixed,
     stats,
     hidden,
     sorted_rows,
     grad_sorted,
     weights,
     bias,
+    normed,
+    mixed,
     normed_two,
     send_sems,
     recv_sems,
@@ -353,7 +355,8 @@
     zed, core = dp // 2, lax.rem(dp, 2)
     rows, wide = tokens.shape
     sibling = (zed * 2 + 1 - core, flat)
-    others = [(lax.rem(zed + k, nz) * 2 + core, flat) for k in range(1, nz)]
+    next_z, across_z = [((zed ^ k) * 2 + core, flat) for k in (1, 2)]
+    others = [next_z, across_z]
     hops = {bit: (dp, flat ^ bit) for bit in moves.orders[0]}
 
     barrier = pltpu.get_barrier_semaphore()
@@ -373,16 +376,23 @@
     own = local_start(mine, weights.at[zed, core, flat])
     stream_columns = (slice(0, 2 * wide), slice(2 * wide, 4 * wide + BLOCK))
 
-    def send_column(stream):
-        columns = stream_columns[stream]
-        return [
-            remote.start(
-                mine.at[:, columns], weights.at[zed, core, flat, :, columns], device
-            )
-            for device in others
-        ]
-
-    column = [send_column(0)]
+    def column_start(source, place):
+        return [remote.start(source, place(zed), device) for device in (across_z, next_z)]
+
+    def column_next(column, place):
+        wait_in(column[:1])
+        column.append(remote.start(place(zed ^ 2), place(zed ^ 2), next_z))
+
+    def column_wait(column):
+        wait_in(column[1:])
+
+    def weight_place(stream):
+        return lambda z_of: weights.at[z_of, core, flat, :, stream_columns[stream]]
+
+    def weight_column(stream):
+        return column_start(mine.at[:, stream_columns[stream]], weight_place(stream))
+
+    columns_a = weight_column(0)
     targets = (first_in.at[zed, core, flat], column_in.at[zed, core])
     cut = own_in.shape[2] // (2 * nz)
     crossed, blocks = [], []
@@ -398,15 +408,17 @@
     blocks.append(local_start(own_out.at[0], first_out.at[zed, flat]))
     blocks.append(local_start(own_out.at[1], column_out.at[zed]))
 
-    def sort_rows(source, target):
+    capacity = sorted_rows.shape[0] // EXPERTS
+
+    def sort_rows(source, target, first):
         @pl.loop(0, target.shape[0] // TILE)
         def _(t):
             place = pl.ds(pl.multiple_of(t * TILE, TILE), TILE)
-            slot = lax.broadcasted_iota(jnp.int32, (TILE, rows), 0) + t * TILE
+            slot = lax.broadcasted_iota(jnp.int32, (TILE, rows), 0) + t * TILE + first
             chosen = (slot == slot_row[0:1, :]).astype(F32).astype(BF16)
             target[place, :] = dot(chosen, source[...]).astype(BF16)
 
-    sort_rows(grad_out, grad_sorted)
+    sort_rows(grad_out, grad_sorted, 0)
     for i in range(rows // TILE):
         span = (i + 1) * TILE
         place = slice(i * TILE, span)
@@ -424,21 +436,28 @@
     far = [moves.orders[n][0] for n in range(2)]
     hop_near, hop_far, across = [], [], []
     own.wait()
-    wait_in(column[0])
-    column.append(send_column(1))
+    column_next(columns_a, weight_place(0))
+    columns_b = weight_column(1)
+    column_wait(columns_a)
     hop_near.append(send_weights(0, flat, hops[near[0]]))
     hop_far.append(send_weights(0, flat, hops[far[0]]))
     across.append(send_weights(0, flat, sibling))
 
+    first_places = (
+        lambda z_of: first_in.at[z_of, :, flat],
+        lambda z_of: first_out.at[z_of, flat],
+    )
     wait_in(crossed)
     for one in blocks:
         one.wait()
-    wait_in(column[1])
-    place = first_in.at[zed, :, flat]
-    first_column = [[remote.start(place, place, device) for device in others]]
+    column_next(columns_b, weight_place(1))
+    first_a = column_start(first_in.at[zed, :, flat], first_places[0])
+    column_wait(columns_b)
     hop_near.append(send_weights(1, flat, hops[near[1]]))
     hop_far.append(send_weights(1, flat, hops[far[1]]))
     across.append(send_weights(1, flat, sibling))
+    column_next(first_a, first_places[0])
+    first_b = column_start(own_out.at[0], first_places[1])
     wait_in(hop_near)
     hop_last = [send_weights(n, flat ^ near[n], hops[far[n]]) for n in range(2)]
     across += [send_weights(n, flat ^ near[n], sibling) for n in range(2)]
@@ -448,20 +467,15 @@
         place = first_in.at[:, :, owner] if stream == 0 else first_out.at[:, owner]
         return remote.start(place, place, device)
 
-    first_near, first_far = [], []
-    wait_in(first_column[0])
-    first_column.append(
-        [
-            remote.start(own_out.at[0], first_out.at[zed, flat], device)
-            for device in others
-        ]
-    )
-    first_near.append(send_first(0, flat, hops[near[0]]))
-    first_far.append(send_first(0, flat, hops[far[0]]))
+    column_wait(first_a)
+    first_near = [send_first(0, flat, hops[near[0]])]
+    first_far = [send_first(0, flat, hops[far[0]])]
+    column_next(first_b, first_places[1])
     wait_in(hop_far)
     across += [send_weights(n, flat ^ far[n], sibling) for n in range(2)]
     wait_in(hop_last)
     across += [send_weights(n, flat ^ near[n] ^ far[n], sibling) for n in range(2)]
+
     wait_in(across)
     whole = 2 * nz * nf * mine.shape[0]
     writes = [
@@ -481,15 +495,6 @@
             columns = pl.ds(part * wide, wide)
             matrix = weights[:, :, :, :, columns].reshape(whole, wide)
             projected[place, columns] = dot(normed[place, :], matrix).astype(BF16)
-
-    wait_in(first_column[1])
-    first_near.append(send_first(1, flat, hops[near[1]]))
-    first_far.append(send_first(1, flat, hops[far[1]]))
-    second_column = []
-    for device in others:
-        place = column_in.at[zed]
-        second_column.append(remote.start(place, place, device))
-        second_column.append(remote.start(own_out.at[1], column_out.at[zed], device))
 
     lane = lax.broadcasted_iota(jnp.int32, (1, BLOCK), 1)
     pairs = wide // BLOCK
@@ -517,19 +522,29 @@
             stats[place, :] = held
             mixed[place, columns[0]] = result.astype(BF16)
 
+    def attend_pairs(start, stop):
+        @pl.loop(start, stop)
+        def _(pair):
+            attend_pair(pair)
+
+    attend_pairs(0, pairs // 4)
+    column_wait(first_b)
+    first_near.append(send_first(1, flat, hops[near[1]]))
+    first_far.append(send_first(1, flat, hops[far[1]]))
+
+    second_places = (lambda z_of: column_in.at[z_of], lambda z_of: column_out.at[z_of])
+    second_a = column_start(column_in.at[zed], second_places[0])
+
+    attend_pairs(pairs // 4, pairs // 2)
     wait_in([first_near[0]])
     first_last = [send_first(0, flat ^ near[0], hops[far[0]])]
-
-    @pl.loop(0, pairs // 2)
-    def _(pair):
-        attend_pair(pair)
-
+    column_next(second_a, second_places[0])
+    second_b = column_start(own_out.at[1], second_places[1])
+    attend_pairs(pairs // 2, 3 * pairs // 4)
     wait_in([first_near[1]])
     first_last.append(send_first(1, flat ^ near[1], hops[far[1]]))
-
-    @pl.loop(pairs // 2, pairs)
-    def _(pair):
-        attend_pair(pair)
+    column_next(second_b, second_places[1])
+    attend_pairs(3 * pairs // 4, pairs)
 
     gain_two, shift_two = turned[2:3, :], turned[3:4, :]
 
@@ -542,11 +557,18 @@
         scaled, _ = norm_parts(total)
         normed_two[place, :] = (scaled * gain_two + shift_two).astype(BF16)
 
-    sort_rows(normed_two, sorted_rows)
-    exchanged.append(remote.start(sorted_rows, sorted_other, sibling))
+    sort_rows(normed_two, sorted_rows.at[pl.ds(0, capacity)], 0)
+    place = pl.ds(0, capacity)
+    exchanged.append(remote.start(sorted_rows.at[place], sorted_other.at[place], sibling))
+    sort_rows(normed_two, sorted_rows.at[pl.ds(capacity, capacity)], capacity)
+    place = pl.ds(capacity, capacity)
+    exchanged.append(remote.start(sorted_rows.at[place], sorted_other.at[place], sibling))
+    turned_normed[...] = normed[...].T
+    turned_mixed[...] = mixed[...].T
     wait_in(first_far)
     wait_in(first_last)
-    wait_in(second_column)
+    column_wait(second_a)
+    column_wait(second_b)
     wait_in(exchanged)
     for one in remote.made:
         one.wait_send()
@@ -563,7 +585,7 @@
     anywhere = pl.BlockSpec(memory_space=pl.ANY)
     inside = pl.BlockSpec(memory_space=pltpu.VMEM)
     shape = jax.ShapeDtypeStruct
-    remote = 6 * (nz - 1) + 2 * nz + 24
+    remote = 6 * (nz - 1) + 2 * nz + 26
     return pl.pallas_call(
         functools.partial(forward_kernel, moves),
         in_specs=[inside] * 8,
@@ -578,9 +600,9 @@
             shape((nz, part, wide), BF16),
             shape((EXPERTS * capacity, wide), BF16),
             shape((EXPERTS * capacity, wide), BF16),
-            shape((rows, wide), BF16),
+            shape((wide, rows), BF16),
             shape((rows, 3 * wide), BF16),
-            shape((rows, wide), BF16),
+            shape((wide, rows), BF16),
             shape((rows, BLOCK), F32),
             shape((rows, wide), F32),
             shape((EXPERTS * capacity, wide), BF16),
@@ -589,6 +611,8 @@
         scratch_shapes=[
             pltpu.VMEM((nz, 2, nf, deep, 4 * wide + BLOCK), BF16),
             pltpu.VMEM((rows, rows), F32),
+            pltpu.VMEM((rows, wide), BF16),
+            pltpu.VMEM((rows, wide), BF16),
             pltpu.VMEM((rows, wide), BF16),
             pltpu.SemaphoreType.DMA((remote,)),
             pltpu.SemaphoreType.DMA((remote,)),
@@ -639,8 +663,7 @@
     sent_out,
     stats,
     seg_row,
-    seg_col,
-    slot_col,
+    marks,
     mixed,
     params,
     block_out,
@@ -679,7 +702,6 @@
     spare,
     up_first,
     z_first,
-    early,
     z_second,
     final,
     send_sems,
@@ -692,7 +714,8 @@
     rows, wide = tokens.shape
     share = wide // PARTS
     sibling = (zed * 2 + 1 - core, flat)
-    others = [((zed ^ k) * 2 + core, flat) for k in range(1, nz)]
+    next_z, across_z = [((zed ^ k) * 2 + core, flat) for k in (1, 2)]
+    others = [next_z, across_z]
     hops = {bit: (dp, flat ^ bit) for bit in moves.orders[0]}
 
     barrier = pltpu.get_barrier_semaphore()
@@ -760,12 +783,19 @@
                 arrived = [spare[n, m, k] for m in range(len(sources[n]) - 1)]
                 target[n, k] = sum_low(target[n, k], *arrived).astype(BF16)
 
-    def z_send(source, landing):
+    def z_first_step(source, landing):
         return [
-            remote.start(source.at[n, k], landing.at[n, k - 1], others[k - 1])
-            for k in range(1, nz)
+            remote.start(source.at[n, k], landing.at[n, k // 2], next_z)
+            for k in (3, 1)
             for n in range(2)
         ]
+
+    def z_second_step(source, landing, begun):
+        wait_in(begun[:2])
+        for n in range(2):
+            source[n, 2] = sum_low(source[n, 2], landing[n, 1]).astype(BF16)
+            begun.append(remote.start(source.at[n, 2], landing.at[n, 2], across_z))
+        return begun
 
     second_start(0)
     sum_blocks(
@@ -773,7 +803,7 @@
         [(keep_first[n].at[0], arrived[n].at[0], first_hop[n]) for n in range(2)],
         1,
     )
-    first_z = z_send(up_first, z_first)
+    first_z = z_first_step(up_first, z_first)
 
     for one in row_loads + phase_loads:
         one.wait()
@@ -794,7 +824,7 @@
         total = jnp.zeros((TILE, wide), F32)
         for e in range(EXPERTS):
             slot = lax.broadcasted_iota(jnp.int32, (TILE, capacity), 1) + e * capacity
-            chosen = (slot == slot_col[place, 0:1]).astype(F32).astype(BF16)
+            chosen = (slot == marks[place, 1:2]).astype(F32).astype(BF16)
             total = total + dot(chosen, grad_projected[pl.ds(0, capacity), pl.ds(e * wide, wide)])
         return total
 
@@ -835,10 +865,11 @@
         sum_blocks(
             up.at[h], [(keep[n].at[0], got[n].at[0], hop[n]) for n in range(2)], h
         )
-        return z_send(up.at[h], z_second.at[h])
+        return z_first_step(up.at[h], z_second.at[h])
 
     second_hop = second_next(0)
     second_start(1)
+    first_z = z_second_step(up_first, z_first, first_z)
     saved.wait()
 
     lane = lax.broadcasted_iota(jnp.int32, (1, BLOCK), 1)
@@ -848,7 +879,7 @@
         place = slice(i * TILE, span)
         query = lax.broadcasted_iota(jnp.int32, (span, TILE), 1) + i * TILE
         key = lax.broadcasted_iota(jnp.int32, (span, TILE), 0)
-        same = seg_col[:span, 0:1] == seg_row[0:1, place]
+        same = marks[:span, 0:1] == seg_row[0:1, place]
         wide_f32[:span, place] = jnp.where(same & (key <= query), 0.0, MASKED)
     loaded.wait()
     pairs = wide // BLOCK
@@ -895,8 +926,8 @@
         def _(z_of):
             span = 2 * nf * deep
             place = pl.ds(pl.multiple_of(z_of * span, span), span)
-            turned = normed[:, place].T
-            mixed_turned = mixed[:, place].T
+            turned = normed[place, :]
+            mixed_turned = mixed[place, :]
             for part in range(4):
                 if part < 3:
                     columns = pl.ds(part * wide + n * share, share)
@@ -940,16 +971,22 @@
             source[k, core, flat] = total.astype(source.dtype)
 
         return [
-            remote.start(source.at[zed ^ k, core, flat], z_landing.at[k - 1], others[k - 1])
-            for k in range(1, nz)
+            remote.start(source.at[zed ^ k, core, flat], z_landing.at[k // 2], next_z)
+            for k in (3, 1)
         ]
 
+    def z_next(source, z_landing, begun):
+        wait_in(begun[:1])
+        total = sum_low(source[zed ^ 2, core, flat], z_landing[1])
+        source[zed ^ 2, core, flat] = total.astype(source.dtype)
+        begun.append(remote.start(source.at[zed ^ 2, core, flat], z_landing.at[2], across_z))
+
     def z_total(source, z_landing):
-        return sum_low(source[zed, core, flat], *[z_landing[k] for k in range(nz - 1)])
+        return sum_low(source[zed, core, flat], z_landing[0], z_landing[2])
 
     def finish_half(e, h, own, landing):
         for n in range(2):
-            total = sum_low(own[n], *[landing[n, k] for k in range(nz - 1)])
+            total = sum_low(own[n], landing[n, 0], landing[n, 2])
             final[2 * e + n, half_rows[h]] = total
 
     def finish_expert(e, writes):
@@ -993,11 +1030,10 @@
     step = pairs // PARTS
     crossed, hopped, went, turned_z = {}, {}, {}, {}
 
+    def part_attend(n):
+        attend_pairs(n * step, (n + 1) * step)
+
     def part_begin(n):
-        attend_pairs(n * step, (n + 1) * step)
-        if n == 0:
-            for one in reloads:
-                one.wait()
         weight_grads(n)
         crossed[n] = cross_start(low.at[n], cross.at[n])
 
@@ -1014,35 +1050,46 @@
         wait_in([hopped[n][1], went[n]])
         turned_z[n] = z_start(low.at[n], got_q.at[n], hop_q.at[n], z_q.at[n])
 
+    def part_z_next(n):
+        z_next(low.at[n], z_q.at[n], turned_z[n])
+
     def part_end(n):
-        wait_in(turned_z[n])
+        wait_in(turned_z[n][1:])
         put_share(n, z_total(low.at[n], z_q.at[n]))
 
+    part_attend(0)
+    for one in reloads:
+        one.wait()
     part_begin(0)
-    second_zs = second_z(0, second_hop)
+    second_z_0 = second_z(0, second_hop)
+    part_attend(1)
+    part_hop(0)
     part_begin(1)
-    part_hop(0)
+    z_second_step(up.at[0], z_second.at[0], second_z_0)
     second_hop_late = second_next(1)
-    part_begin(2)
+    part_attend(2)
     part_hop(1)
     part_next(0)
-    attend_pairs(3 * step, 4 * step)
+    part_begin(2)
+    second_z_1 = second_z(1, second_hop_late)
+    part_attend(3)
     reload = local_start(whole_qkv, wide_low)
     restore = local_start(grad_tokens, wide_f32)
-    weight_grads(3)
-    crossed[3] = cross_start(low.at[3], cross.at[3])
     part_hop(2)
     part_next(1)
     part_z(0)
-    part_hop(3)
-    second_zs += second_z(1, second_hop_late)
+    part_begin(3)
+    z_second_step(up.at[1], z_second.at[1], second_z_1)
     reload.wait()
     restore.wait()
-    sums = lax.fori_loop(0, rows // TILE // 2, norm_tile, (empty, empty))
+    sums = lax.fori_loop(0, 1, norm_tile, (empty, empty))
+    part_hop(3)
     part_next(2)
+    sums = lax.fori_loop(1, 3, norm_tile, sums)
     part_z(1)
+    part_z_next(0)
     part_next(3)
-    sums = lax.fori_loop(rows // TILE // 2, rows // TILE, norm_tile, sums)
+    sums = lax.fori_loop(3, rows // TILE, norm_tile, sums)
     result = local_start(wide_f32, grad_tokens)
     index = lax.broadcasted_iota(jnp.int32, (BLOCK, 1), 0)
     stacked = jnp.zeros((BLOCK, wide), F32)
@@ -1050,48 +1097,60 @@
         stacked = jnp.where(index == n, one, stacked)
     vec[...] = stacked.T.reshape(nz, 2, nf, deep, BLOCK)
     crossed_v = [cross_start(vec, cross_vec)]
-    part_z(2)
-    part_z(3)
+    wait_in(first_z[2:])
+    load(
+        (first_own, spare.at[0, 0, pl.ds(0, 2)]),
+        *[(first_landed.at[n], spare.at[n, 1, pl.ds(0, nz - 1)]) for n in range(2)],
+    )
+    finish_half(0, 0, [spare[0, 0, n] for n in range(2)], spare.at[:, 1])
+    finish_half(0, 1, [up_first[n, 0] for n in range(2)], z_first)
+    finish_expert(0, writes)
     wait_in(crossed_v)
     cross_add(vec, cross_vec)
     hops_v = hop_start(vec, got_vec, 0)
-    wait_in(first_z)
-    load((first_own, spare.at[0, 0, pl.ds(0, 2)]), (first_landed, early))
-    finish_half(0, 0, [spare[0, 0, n] for n in range(2)], early)
-    finish_half(0, 1, [up_first[n, 0] for n in range(2)], z_first)
-    finish_expert(0, writes)
+    part_z(2)
+    part_z_next(1)
+
+    result.wait()
+    wait_in(crossed_late)
+    late = [
+        local_start(source, target)
+        for source, target in [(hidden, wide_f32), (landed, grad_mixed.at[pl.ds(0, capacity)])]
+        + [
+            (source.at[0], grad_projected.at[pl.ds(0, capacity), pl.ds(e * wide, wide)])
+            for e, source in enumerate((rows_first, rows_second, landed_first))
+        ]
+    ]
+    part_z(3)
+    part_z_next(2)
     wait_in(hops_v)
     next_v = hop_next(vec, got_vec, hop_vec.at[1], hop_vec.at[0], 0)
-
-    result.wait()
-    wait_in(crossed_late)
-    load(
-        (hidden, wide_f32),
-        *[
-            (source.at[0], grad_projected.at[pl.ds(0, capacity), pl.ds(e * wide, wide)])
-            for e, source in enumerate((rows_first, rows_second, landed_first))
-        ],
-        (landed, grad_mixed.at[pl.ds(0, capacity)]),
-    )
+    for one in late:
+        one.wait()
     add_rows(first_columns, grad_projected, pl.ds(2 * wide, wide))
     add_rows(second_columns, grad_mixed, first_columns)
-
-    @pl.loop(0, rows // TILE)
-    def _(t):
-        place = pl.ds(pl.multiple_of(t * TILE, TILE), TILE)
-        branch[place, :] = (wide_f32[place, :] + tokens_order(place)).astype(BF16)
-
-    stored.append(local_start(branch, block_out))
     wait_in([next_v])
     z_v = z_start(vec, got_vec, hop_vec.at[0], z_vec)
+    part_z_next(3)
+
+    def output_tiles(start, stop):
+        @pl.loop(start, stop)
+        def _(t):
+            place = pl.ds(pl.multiple_of(t * TILE, TILE), TILE)
+            branch[place, :] = (wide_f32[place, :] + tokens_order(place)).astype(BF16)
+
+    output_tiles(0, rows // TILE // 2)
+    z_next(vec, z_vec, z_v)
     for n in range(PARTS - 1):
         part_end(n)
-    wait_in(second_zs)
+    output_tiles(rows // TILE // 2, rows // TILE)
+    stored.append(local_start(branch, block_out))
+    wait_in(second_z_0[2:] + second_z_1[2:])
     for h in range(2):
         finish_half(1, h, [up[h, n, 0] for n in range(2)], z_second.at[h])
     finish_expert(1, writes)
     part_end(PARTS - 1)
-    wait_in(z_v)
+    wait_in(z_v[1:])
     share_vectors[...] = z_total(vec, z_vec)
     wait_in(writes)
     for one in remote.made:
@@ -1101,7 +1160,7 @@
         one.wait()
 
 
-def backward_pass(moves, deep, big, row_parts, sums, stats, seg, slot_col, mixed, params):
+def backward_pass(moves, deep, big, row_parts, sums, stats, seg_row, marks, mixed, params):
     nz, nf = moves.nz, moves.nf
     rows, wide = mixed.shape
     share = wide // PARTS
@@ -1116,7 +1175,7 @@
     inputs = list(big) + list(row_parts) + list(sums)
     return pl.pallas_call(
         functools.partial(backward_kernel, moves, deep),
-        in_specs=[anywhere] * len(inputs) + [inside] * 6,
+        in_specs=[anywhere] * len(inputs) + [inside] * 5,
         out_specs=[anywhere] * 4 + [inside] * 3 + [anywhere] * 5,
         out_shape=[
             shape((rows, wide), BF16),
@@ -1157,7 +1216,6 @@
             pltpu.VMEM((2, 2, nz) + half_block, BF16),
             pltpu.VMEM((2, nz) + half_block, BF16),
             pltpu.VMEM((2, nz - 1) + half_block, BF16),
-            pltpu.VMEM((2, nz - 1) + half_block, BF16),
             pltpu.VMEM((2, 2, nz - 1) + half_block, BF16),
             pltpu.VMEM((4,) + block, F32),
             pltpu.SemaphoreType.DMA((remote,)),
@@ -1165,13 +1223,13 @@
             pltpu.SemaphoreType.DMA((60 + 2 * nz,)),
         ],
         compiler_params=pltpu.CompilerParams(
-            collective_id=1, has_side_effects=True, vmem_limit_bytes=62 * MIB
+            collective_id=1, has_side_effects=True, vmem_limit_bytes=63 * MIB
         ),
         cost_estimate=pl.CostEstimate(
             flops=30 * rows * wide * wide, bytes_accessed=80 * wide * wide, transcendentals=0
         ),
         name="backward_pass",
-    )(*inputs, stats, *seg, slot_col, mixed, params)
+    )(*inputs, stats, seg_row, marks, mixed, params)
 
 
 def gelu_both(value):
@@ -1218,7 +1276,7 @@
         sibling = (zed * 2 + 1 - core, flat)
         devices = list(hops.values())
         if mode == "second":
-            others = [((zed ^ k) * 2 + core, flat) for k in range(1, moves.nz)]
+            others = [((zed ^ k) * 2 + core, flat) for k in (1, 2)]
             devices += [sibling] + others
             up, spare, load_sems = take(3)
             half_rows = [pl.ds(h * deep, deep) for h in range(2)]
@@ -1414,8 +1472,8 @@
         wait_in([hopped[n, 0, 0] for n in range(2)] + last)
         half_sum(0, 0, up.at[2])
         z_sent = [
-            remote.start(up.at[2, n, k], landed_z.at[n, k - 1], others[k - 1])
-            for k in range(1, moves.nz)
+            remote.start(up.at[2, n, k], landed_z.at[n, k // 2], others[0])
+            for k in (3, 1)
             for n in range(2)
         ]
         own = pltpu.make_async_copy(up.at[2, :, 0], own_z, load_sems.at[0])
@@ -1423,6 +1481,18 @@
         own.wait()
         run_chunks(chunks // 2, chunks - 1)
         last = second_hop(1)
+        wait_in(z_sent[:2])
+        begun = [
+            pltpu.make_async_copy(landed_z.at[n, 1], spare.at[n, 0, 0], load_sems.at[n])
+            for n in range(2)
+        ]
+        for one in begun:
+            one.start()
+        for one in begun:
+            one.wait()
+        for n in range(2):
+            up[2, n, 2] = sum_low(up[2, n, 2], spare[n, 0, 0]).astype(BF16)
+            z_sent.append(remote.start(up.at[2, n, 2], landed_z.at[n, 2], others[1]))
         run_chunks(chunks - 1, chunks)
 
     @pl.loop(0, tiles)
@@ -1444,7 +1514,7 @@
     if mode == "first":
         wait_in(far)
     elif mode == "second":
-        wait_in([hopped[n, 0, 1] for n in range(2)] + last + z_sent + [crossed])
+        wait_in([hopped[n, 0, 1] for n in range(2)] + last + z_sent[2:] + [crossed])
     if mode != "plain":
         for one in remote.made:
             one.wait_send()
@@ -1537,7 +1607,7 @@
     rows, width = tokens.shape
     deep = w_qkv.shape[0]
     moves = Moves(nd, nf)
-    staged = deep % 32 == 0 and nf == 4 and moves.nz in (2, 4)
+    staged = deep % 32 == 0 and nf == 4 and moves.nz == 4
     core = lax.rem(lax.axis_index("dp"), 2)
     zed = lax.axis_index("dp") // 2
     flat = lax.axis_index("fsdp")
@@ -1569,7 +1639,8 @@
     capacity = 3 * rows // 4
     zed, core, flat = place
     slot_row = jnp.broadcast_to(slot[None, :], (8, rows))
-    slot_col = jnp.broadcast_to(slot[:, None], (rows, BLOCK))
+    lane = jnp.arange(BLOCK, dtype=jnp.int32)[None, :]
+    marks = jnp.where(lane == 0, seg_col, slot[:, None])
     outs = forward_pass(
         moves, tokens, mine, w_expert_in, w_expert_out, seg_row, seg_col, slot_row, grad_out
     )
@@ -1617,8 +1688,8 @@
         [first[0], second[0], landed, second[1]],
         [first[2], first[4]] + list(second[6:10]) + list(second[11:13]) + list(second[2:6]),
         stats.T,
-        [seg_row, seg_col],
-        slot_col,
+        seg_row,
+        marks,
         mixed,
         params,
     )

time: 464 us -> 451 us (0.972)
  Pallas kernels: 434 us -> 422 us
    pallas_call x2, Pallas kernels: 156 us -> 146 us  [expert_block(): pl.pallas_call(functools.partial(expert_kernel, moves, mode, expert, deep...]
where the time goes in v4:
time: 451 us; the launch traced here: 443 us
  Pallas kernels  422 us (94%)
  local copies, waits for them, and re-layouts  13.6 us (3%)
  other arithmetic  6.22 us (1%)
    pallas_call x2, Pallas kernels, expert_block(): pl.pallas_call(functools.partial(expert_kernel, moves, mode, expert, deep...  146 us
    pallas_call x1, Pallas kernels, backward_pass(): pl.pallas_call(functools.partial(backward_kernel, moves, deep), in_specs=...  140 us
    pallas_call x1, Pallas kernels, forward_pass(): pl.pallas_call(functools.partial(forward_kernel, moves), in_specs=[inside...  136 us

profile of v4, /device:TPU:0, one launch (start us, length us, event | category | flops | bytes accessed | tf_op | source)
XLA Modules:
  0.0 442.9 jit_solution(15737852696942069193)
XLA Ops:
  0.6 0.7 pad_maximum_fusion
  1.4 0.1 copy.34
  1.5 1.7 fusion.1.mine
  3.2 0.8 reduce-window.19
  4.0 0.1 convert_reduce_fusion
  4.1 0.6 broadcast_in_dim.18.seg_row
  4.7 1.0 broadcast_in_dim.19.seg_col
  5.7 1.0 reduce-window.20
  6.6 0.1 slice.22
  6.7 0.1 slice_reduce_fusion.4
  6.9 0.8 subtract_select_fusion
  7.6 0.6 broadcast_in_dim.20.slot_row
  8.2 136.0 %forward_pass.1 = (bf16[4,2,4,32,3072]{4,3,2,1,0:T(8,128)(2,1)}, bf16[4,2,4,32,1024]{4,3,2,1,0:T(8,128)(2,1)}, bf16[4,2,4,32,128]{4,3,2,1,0:T(8,128)(2,1)}, bf16...) custom-call(bf16[1024,1024]{1,0:T(8,128)(2,1)} %tokens_in.1, ...), custom_call_target="tpu_custom_call" | custom-call | flops 10737418240 | bytes 83886080 | tf_op jit(solution)/shard_map/forward_pass/pallas_call | solution.py:589
  144.2 72.3 %expert_first.1 = (bf16[2,768,1024]{2,1,0:T(8,128)(2,1)}, bf16[2,768,1024]{2,1,0:T(8,128)(2,1)}, bf16[2,4,64,2048]{3,2,1,0:T(8,128)(2,1)}, bf16[2,4,64,2048]{3,2...) custom-call(bf16[2,768,1024]{2,1,0:T(8,128)(2,1)} %bitcast.44, ...), custom_call_target="tpu_custom_call" | custom-call | flops 38654705664 | bytes 41943040 | tf_op jit(solution)/shard_map/expert_first/pallas_call | solution.py:1562
  216.5 0.0 copy-start.3
  216.6 0.0 copy-start.6
  216.6 73.6 %expert_second.1 = (bf16[2,768,1024]{2,1,0:T(8,128)(2,1)}, bf16[2,768,1024]{2,1,0:T(8,128)(2,1)}, bf16[2,4,64,2048]{3,2,1,0:T(8,128)(2,1)}, bf16[2,4,64,2048]{3,...) custom-call(bf16[2,768,1024]{2,1,0:T(8,128)(2,1)} %bitcast.45, ...), custom_call_target="tpu_custom_call" | custom-call | flops 38654705664 | bytes 41943040 | tf_op jit(solution)/shard_map/expert_second/pallas_call | solution.py:1562
  290.1 0.0 copy-done.3
  290.1 1.0 copy.35
  291.1 0.0 copy-done.6
  291.2 1.1 broadcast_select_fusion.marks
  292.3 140.1 %backward_pass.1 = (bf16[1024,1024]{1,0:T(8,128)(2,1)}, f32[1024,1024]{1,0:T(8,128)}, f32[2,32,4096]{2,1,0:T(8,128)}, f32[2,128,1024]{2,1,0:T(8,128)}, f32[32,30...) custom-call(bf16[1024,3072]{1,0:T(8,128)(2,1)} %get-tuple-element.54, ...), custom_call_target="tpu_custom_call" | custom-call | flops 32212254720 | bytes 83886080 | tf_op jit(solution)/shard_map/backward_pass/pallas_call | solution.py:1176
  432.4 0.7 slice_bitcast_fusion
  433.1 0.7 slice_reduce_fusion
  433.9 0.0 copy-start
  433.9 3.2 copy.42
  437.1 0.0 copy-done
  437.1 0.0 copy-start.4
  437.1 0.0 copy-start.5
  437.1 0.0 copy-start.2
  437.1 2.0 copy.43
  439.1 0.0 copy-done.4
  439.1 0.0 copy-start.1
  439.1 0.7 copy.44
  439.9 0.0 copy-done.5
  439.9 0.7 copy.45
  440.5 0.0 copy-done.2
  440.5 1.0 copy.46
  441.5 0.0 copy-done.1
  441.5 1.0 copy.47
  (3 shorter events, 0.0 us)
Async XLA Ops:
  216.5 73.6 %copy-start.3 = (f32[1024,128]{1,0:T(8,128)S(1)}, f32[1024,128]{1,0:T(8,128)}, u32[]{:S(2)}) copy-start(f32[1024,128]{1,0:T(8,128)} %get-tuple-element.88) | copy-start | bytes 1572868
  216.6 74.6 %copy-start.6 = (s32[1024,1]{0,1:T(1,128)S(1)}, s32[1024,1]{0,1:T(1,128)}, u32[]{:S(2)}) copy-start(s32[1024,1]{0,1:T(1,128)} %param.14) | copy-start | bytes 12292
  433.9 3.2 copy-start
  437.1 2.0 copy-start.4
  437.1 2.8 copy-start.5
  437.1 3.4 copy-start.2
  439.1 2.4 copy-start.1

commit v5 on v4

--- a/solution.py
+++ b/solution.py
@@ -337,7 +337,7 @@
     turned_normed,
     projected,
     turned_mixed,
-    stats,
+    turned_stats,
     hidden,
     sorted_rows,
     grad_sorted,
@@ -345,6 +345,7 @@
     bias,
     normed,
     mixed,
+    stats,
     normed_two,
     send_sems,
     recv_sems,
@@ -418,16 +419,6 @@
             chosen = (slot == slot_row[0:1, :]).astype(F32).astype(BF16)
             target[place, :] = dot(chosen, source[...]).astype(BF16)
 
-    sort_rows(grad_out, grad_sorted, 0)
-    for i in range(rows // TILE):
-        span = (i + 1) * TILE
-        place = slice(i * TILE, span)
-        query = lax.broadcasted_iota(jnp.int32, (TILE, span), 0) + i * TILE
-        key = lax.broadcasted_iota(jnp.int32, (TILE, span), 1)
-        same = seg_col[place, 0:1] == seg_row[0:1, :span]
-        bias[place, :span] = jnp.where(same & (key <= query), 0.0, MASKED)
-    stats[...] = jnp.zeros_like(stats)
-
     def send_weights(stream, owner, device):
         place = weights.at[:, core, owner, :, stream_columns[stream]]
         return remote.start(place, place, device)
@@ -458,6 +449,17 @@
     across.append(send_weights(1, flat, sibling))
     column_next(first_a, first_places[0])
     first_b = column_start(own_out.at[0], first_places[1])
+
+    sort_rows(grad_out, grad_sorted, 0)
+    for i in range(rows // TILE):
+        span = (i + 1) * TILE
+        place = slice(i * TILE, span)
+        query = lax.broadcasted_iota(jnp.int32, (TILE, span), 0) + i * TILE
+        key = lax.broadcasted_iota(jnp.int32, (TILE, span), 1)
+        same = seg_col[place, 0:1] == seg_row[0:1, :span]
+        bias[place, :span] = jnp.where(same & (key <= query), 0.0, MASKED)
+    stats[...] = jnp.zeros_like(stats)
+
     wait_in(hop_near)
     hop_last = [send_weights(n, flat ^ near[n], hops[far[n]]) for n in range(2)]
     across += [send_weights(n, flat ^ near[n], sibling) for n in range(2)]
@@ -565,6 +567,7 @@
     exchanged.append(remote.start(sorted_rows.at[place], sorted_other.at[place], sibling))
     turned_normed[...] = normed[...].T
     turned_mixed[...] = mixed[...].T
+    turned_stats[...] = stats[...].T
     wait_in(first_far)
     wait_in(first_last)
     column_wait(second_a)
@@ -603,7 +606,7 @@
             shape((wide, rows), BF16),
             shape((rows, 3 * wide), BF16),
             shape((wide, rows), BF16),
-            shape((rows, BLOCK), F32),
+            shape((BLOCK, rows), F32),
             shape((rows, wide), F32),
             shape((EXPERTS * capacity, wide), BF16),
             shape((EXPERTS * capacity, wide), BF16),
@@ -613,6 +616,7 @@
             pltpu.VMEM((rows, rows), F32),
             pltpu.VMEM((rows, wide), BF16),
             pltpu.VMEM((rows, wide), BF16),
+            pltpu.VMEM((rows, BLOCK), F32),
             pltpu.VMEM((rows, wide), BF16),
             pltpu.SemaphoreType.DMA((remote,)),
             pltpu.SemaphoreType.DMA((remote,)),
@@ -1642,7 +1646,7 @@
     lane = jnp.arange(BLOCK, dtype=jnp.int32)[None, :]
     marks = jnp.where(lane == 0, seg_col, slot[:, None])
     outs = forward_pass(
-        moves, tokens, mine, w_expert_in, w_expert_out, seg_row, seg_col, slot_row, grad_out
+        moves, tokens, mine, w_expert_in, w_expert_out, seg_row, marks, slot_row, grad_out
     )
     whole_qkv, whole_attn, params, first_in = [one.reshape(-1, one.shape[-1]) for one in outs[:4]]
     first_out = outs[4].reshape(half_hidden, width)
@@ -1687,7 +1691,7 @@
         [projected, whole_qkv, whole_attn, hidden_one, normed_one, tokens, grad_out],
         [first[0], second[0], landed, second[1]],
         [first[2], first[4]] + list(second[6:10]) + list(second[11:13]) + list(second[2:6]),
-        stats.T,
+        stats,
         seg_row,
         marks,
         mixed,

time: 451 us -> 449 us (level)
  no operation moved by 1% of the time
where the time goes in v5:
time: 449 us; the launch traced here: 441 us
  Pallas kernels  421 us (94%)
  local copies, waits for them, and re-layouts  11.6 us (3%)
  other arithmetic  6.9 us (2%)
    pallas_call x2, Pallas kernels, expert_block(): pl.pallas_call(functools.partial(expert_kernel, moves, mode, expert, deep...  146 us
    pallas_call x1, Pallas kernels, backward_pass(): pl.pallas_call(functools.partial(backward_kernel, moves, deep), in_specs=...  140 us
    pallas_call x1, Pallas kernels, forward_pass(): pl.pallas_call(functools.partial(forward_kernel, moves), in_specs=[inside...  136 us

profile of v5, /device:TPU:0, one launch (start us, length us, event | category | flops | bytes accessed | tf_op | source)
XLA Modules:
  0.0 441.1 jit_solution(13495374159714471075)
XLA Ops:
  0.6 0.8 reduce-window.19
  1.5 0.7 pad_maximum_fusion
  2.2 0.1 convert_reduce_fusion
  2.3 1.0 reduce-window.20
  3.2 0.1 slice.22
  3.3 0.1 slice_reduce_fusion.4
  3.5 0.8 subtract_select_fusion
  4.2 0.7 compare_select_fusion
  4.9 0.1 copy.31
  5.0 0.6 broadcast_in_dim.45.slot_row
  5.6 0.6 broadcast_in_dim.18.seg_row
  6.3 1.7 fusion.1.mine
  8.0 1.1 broadcast_select_fusion.seg_col.marks
  9.1 136.0 %forward_pass.1 = (bf16[4,2,4,32,3072]{4,3,2,1,0:T(8,128)(2,1)}, bf16[4,2,4,32,1024]{4,3,2,1,0:T(8,128)(2,1)}, bf16[4,2,4,32,128]{4,3,2,1,0:T(8,128)(2,1)}, bf16...) custom-call(bf16[1024,1024]{1,0:T(8,128)(2,1)} %tokens_in.1, ...), custom_call_target="tpu_custom_call" | custom-call | flops 10737418240 | bytes 83886080 | tf_op jit(solution)/shard_map/forward_pass/pallas_call | solution.py:592
  145.1 72.3 %expert_first.1 = (bf16[2,768,1024]{2,1,0:T(8,128)(2,1)}, bf16[2,768,1024]{2,1,0:T(8,128)(2,1)}, bf16[2,4,64,2048]{3,2,1,0:T(8,128)(2,1)}, bf16[2,4,64,2048]{3,2...) custom-call(bf16[2,768,1024]{2,1,0:T(8,128)(2,1)} %bitcast.42, ...), custom_call_target="tpu_custom_call" | custom-call | flops 38654705664 | bytes 41943040 | tf_op jit(solution)/shard_map/expert_first/pallas_call | solution.py:1566
  217.4 73.6 %expert_second.1 = (bf16[2,768,1024]{2,1,0:T(8,128)(2,1)}, bf16[2,768,1024]{2,1,0:T(8,128)(2,1)}, bf16[2,4,64,2048]{3,2,1,0:T(8,128)(2,1)}, bf16[2,4,64,2048]{3,...) custom-call(bf16[2,768,1024]{2,1,0:T(8,128)(2,1)} %bitcast.43, ...), custom_call_target="tpu_custom_call" | custom-call | flops 38654705664 | bytes 41943040 | tf_op jit(solution)/shard_map/expert_second/pallas_call | solution.py:1566
  291.0 139.6 %backward_pass.1 = (bf16[1024,1024]{1,0:T(8,128)(2,1)}, f32[1024,1024]{1,0:T(8,128)}, f32[2,32,4096]{2,1,0:T(8,128)}, f32[2,128,1024]{2,1,0:T(8,128)}, f32[32,30...) custom-call(bf16[1024,3072]{1,0:T(8,128)(2,1)} %get-tuple-element.54, ...), custom_call_target="tpu_custom_call" | custom-call | flops 32212254720 | bytes 83886080 | tf_op jit(solution)/shard_map/backward_pass/pallas_call | solution.py:1180
  430.6 0.7 slice_bitcast_fusion
  431.3 0.7 slice_reduce_fusion
  432.1 0.0 copy-start
  432.1 3.2 copy.38
  435.3 0.0 copy-done
  435.3 0.0 copy-start.3
  435.3 0.0 copy-start.4
  435.3 0.0 copy-start.2
  435.3 2.0 copy.39
  437.3 0.0 copy-done.3
  437.3 0.0 copy-start.1
  437.3 0.7 copy.40
  438.1 0.0 copy-done.4
  438.1 0.7 copy.41
  438.7 0.0 copy-done.2
  438.7 1.0 copy.42
  439.7 0.0 copy-done.1
  439.7 1.0 copy.43
  (2 shorter events, 0.0 us)
Async XLA Ops:
  432.1 3.2 copy-start
  435.3 2.0 copy-start.3
  435.3 2.8 copy-start.4
  435.3 3.4 copy-start.2
  437.3 2.4 copy-start.1
